TPU v7x, 128 devices: a whole 4x4x4 slice. The times are simulated.
128 devices in a mesh: grp: 8 (over z_hi, x), ctx: 16 (over z_lo, y, core).
Axes of the slice: x: 4, y: 4, z: 4 (z_hi: 2, z_lo: 2; z = z_hi * 2 + z_lo), core: 2. Of those that a mesh axis runs over, the one named last changes fastest.
Arguments:
- acts: bfloat16 [8, 16, 128, 2048], P('grp', 'ctx'), may hold values from -6 to 6
- doc_lengths: int32 [8, 2], P('grp'), may hold values from 256 to 1792, as said below
- w_query: bfloat16 [2048, 2048], P(None, 'ctx'), may hold values from -0.125 to 0.125
- w_key: bfloat16 [2048, 2048], P(None, 'ctx'), may hold values from -0.125 to 0.125
- w_value: bfloat16 [2048, 2048], P(None, 'ctx'), may hold values from -0.125 to 0.125
- w_out: bfloat16 [2048, 2048], P('ctx'), may hold values from -6 to 6
- w_gate: bfloat16 [2048, 5504], P(None, 'ctx'), may hold values from -0.125 to 0.125
- w_up: bfloat16 [2048, 5504], P(None, 'ctx'), may hold values from -0.125 to 0.125
- w_down: bfloat16 [5504, 2048], P('ctx'), may hold values from -0.078125 to 0.078125
- gain_attn: bfloat16 [2048], P('ctx'), may hold values from 0.5 to 1.5
- gain_mlp: bfloat16 [2048], P('ctx'), may hold values from 0.5 to 1.5
- cotangent: bfloat16 [8, 16, 128, 2048], P('grp', 'ctx'), may hold values from -6 to 6
Outputs:
- mixed: bfloat16 [8, 16, 128, 2048], P('grp', 'ctx')
- acts_grad: float32 [8, 16, 128, 2048], P('grp', 'ctx')
- grad_query: float32 [2048, 2048], P(None, 'ctx')
- grad_key: float32 [2048, 2048], P(None, 'ctx')
- grad_value: float32 [2048, 2048], P(None, 'ctx')
- grad_out: float32 [2048, 2048], P('ctx')
- grad_gate: float32 [2048, 5504], P(None, 'ctx')
- grad_up: float32 [2048, 5504], P(None, 'ctx')
- grad_down: float32 [5504, 2048], P('ctx')
- grad_gain_attn: float32 [2048], P('ctx')
- grad_gain_mlp: float32 [2048], P('ctx')
Inputs may be any that keep to these rules, and one draw needn't show every extreme that they name: `doc_lengths`: in each group the two lengths sum to 2048 and one of them is at least 1536; either may come first.
All inputs are finite; a program needn't handle non-finite values.
Results may differ from a plain program's by a relative error of at most 0.028.
Values may be sent and summed in bfloat16 or wider, within the bound.
A program may use at most 384 MiB of HBM per device.

v0:
```python
import math

import jax
import jax.numpy as jnp
from jax import lax
from jax.sharding import PartitionSpec as P

HEADS = 16


EPSILON = 1e-05


def rotary(offsets, head_size):
    frequency = 10000.0 ** (-(jnp.arange(head_size // 2).astype(jnp.float32) * 2.0 / head_size))
    angles = offsets.astype(jnp.float32)[:, None] * frequency[None, :]
    return (jnp.cos(angles)[:, None, :], jnp.sin(angles)[:, None, :])


def rotate(tensor, cosine, sine_table):
    middle = tensor.shape[-1] // 2
    first_half = tensor[..., :middle]
    second = tensor[..., middle:]
    return jnp.concatenate(
        [first_half * cosine - second * sine_table, second * cosine + first_half * sine_table], -1
    )


def norm_back(source, factor, gain, incoming):
    scaled = incoming * gain
    grad_source = factor * scaled - source * factor**3 * jnp.mean(
        scaled * source, -1, keepdims=True
    )
    grad_gain = jnp.sum(incoming * source * factor, 0)
    return (grad_source, grad_gain)


def sequence_pos(device, slot_index, middle, ctx_count):
    return jnp.where(
        slot_index < middle,
        device * middle + slot_index,
        (2 * ctx_count - 1 - device) * middle + slot_index - middle,
    )


def local(
    acts,
    doc_lengths,
    w_query,
    w_key,
    w_value,
    w_out,
    w_gate,
    w_up,
    w_down,
    gain_attn,
    gain_mlp,
    cotangent,
):
    tok_dev = acts.shape[2]
    model_width = acts.shape[3]
    head_size = model_width // HEADS
    scale_factor = 1.0 / math.sqrt(head_size)
    ctx_count = lax.axis_size("ctx")
    ctx_index = lax.axis_index("ctx")
    middle = tok_dev // 2
    row_keys = ctx_count * tok_dev
    acts_rows = acts.reshape(tok_dev, model_width)
    tokens = acts_rows.astype(jnp.float32)
    cot_low = cotangent.reshape(tok_dev, model_width)
    lengths = doc_lengths.reshape(2)
    key_index = jnp.arange(row_keys, dtype=jnp.int32)
    key_pos = sequence_pos(key_index // tok_dev, key_index % tok_dev, middle, ctx_count)
    key_doc = (key_pos >= lengths[0]).astype(jnp.int32)
    factor_one = lax.rsqrt(jnp.mean(tokens * tokens, -1, keepdims=True) + EPSILON)
    query_pos = sequence_pos(ctx_index, jnp.arange(tok_dev, dtype=jnp.int32), middle, ctx_count)
    query_doc = (query_pos >= lengths[0]).astype(jnp.int32)
    offsets = query_pos - query_doc * lengths[0]
    own_length = jnp.where(query_doc == 0, lengths[0], lengths[1])
    bias_term = -jnp.log(own_length.astype(jnp.float32))
    cosine, sine_table = rotary(offsets, head_size)
    visible = (
        (key_doc[None, :] == query_doc[:, None]) & (key_pos[None, :] <= query_pos[:, None])
    ).astype(jnp.float32)
    full_query, full_key, full_value, full_out, gain_one, gain_two = (
        lax.all_gather(w_query, "ctx", axis=1, tiled=True),
        lax.all_gather(w_key, "ctx", axis=1, tiled=True),
        lax.all_gather(w_value, "ctx", axis=1, tiled=True),
        lax.all_gather(w_out, "ctx", axis=0, tiled=True),
        lax.all_gather(gain_attn, "ctx", axis=0, tiled=True),
        lax.all_gather(gain_mlp, "ctx", axis=0, tiled=True),
    )
    gain_first = gain_one.astype(jnp.float32)
    gain_second = gain_two.astype(jnp.float32)
    normed = (tokens * factor_one * gain_first).astype(jnp.bfloat16)
    proj_query = jnp.dot(normed, full_query, preferred_element_type=jnp.float32)
    proj_key = jnp.dot(normed, full_key, preferred_element_type=jnp.float32)
    proj_value = jnp.dot(normed, full_value, preferred_element_type=jnp.float32)
    q_rot = rotate(proj_query.reshape(tok_dev, HEADS, head_size), cosine, sine_table).astype(
        jnp.bfloat16
    )
    k_rot = (
        rotate(proj_key.reshape(tok_dev, HEADS, head_size), cosine, sine_table)
        .reshape(tok_dev, model_width)
        .astype(jnp.bfloat16)
    )
    v_low = proj_value.astype(jnp.bfloat16)
    keys_all, values_all = (
        lax.all_gather(k_rot, "ctx", axis=0, tiled=True),
        lax.all_gather(v_low, "ctx", axis=0, tiled=True),
    )
    keys_heads = keys_all.reshape(row_keys, HEADS, head_size)
    values_heads = values_all.reshape(row_keys, HEADS, head_size)
    score = (
        jnp.einsum("qhd,khd->hqk", q_rot, keys_heads, preferred_element_type=jnp.float32)
        * scale_factor
        + bias_term[None, :, None]
    )
    sig_score = jax.nn.sigmoid(score)
    attn_probs = (sig_score * visible[None]).astype(jnp.bfloat16)
    attended = (
        jnp.einsum("hqk,khd->qhd", attn_probs, values_heads, preferred_element_type=jnp.float32)
        .reshape(tok_dev, model_width)
        .astype(jnp.bfloat16)
    )
    residual = tokens + jnp.dot(attended, full_out, preferred_element_type=jnp.float32)
    factor_two = lax.rsqrt(jnp.mean(residual * residual, -1, keepdims=True) + EPSILON)
    normed_two = (residual * factor_two * gain_second).astype(jnp.bfloat16)
    full_gate, full_up, full_down = (
        lax.all_gather(w_gate, "ctx", axis=1, tiled=True),
        lax.all_gather(w_up, "ctx", axis=1, tiled=True),
        lax.all_gather(w_down, "ctx", axis=0, tiled=True),
    )
    gate_proj = jnp.dot(normed_two, full_gate, preferred_element_type=jnp.float32)
    up_proj = jnp.dot(normed_two, full_up, preferred_element_type=jnp.float32)
    sig_gate = jax.nn.sigmoid(gate_proj)
    silu_gate = gate_proj * sig_gate
    hidden = (silu_gate * up_proj).astype(jnp.bfloat16)
    mixed = (residual + jnp.dot(hidden, full_down, preferred_element_type=jnp.float32)).astype(
        jnp.bfloat16
    )
    d_hidden = jnp.dot(cot_low, full_down.T, preferred_element_type=jnp.float32)
    d_gate = (d_hidden * up_proj * sig_gate * (1.0 + gate_proj * (1.0 - sig_gate))).astype(
        jnp.bfloat16
    )
    d_up = (d_hidden * silu_gate).astype(jnp.bfloat16)
    grad_down = jnp.dot(hidden.T, cot_low, preferred_element_type=jnp.float32)
    grad_gate = jnp.dot(normed_two.T, d_gate, preferred_element_type=jnp.float32)
    grad_up = jnp.dot(normed_two.T, d_up, preferred_element_type=jnp.float32)
    shard_gate, shard_up, shard_down = (
        lax.psum_scatter(
            grad_gate.astype(jnp.bfloat16), "ctx", scatter_dimension=1, tiled=True
        ).astype(jnp.float32),
        lax.psum_scatter(
            grad_up.astype(jnp.bfloat16), "ctx", scatter_dimension=1, tiled=True
        ).astype(jnp.float32),
        lax.psum_scatter(
            grad_down.astype(jnp.bfloat16), "ctx", scatter_dimension=0, tiled=True
        ).astype(jnp.float32),
    )
    d_normed_two = jnp.dot(d_gate, full_gate.T, preferred_element_type=jnp.float32) + jnp.dot(
        d_up, full_up.T, preferred_element_type=jnp.float32
    )
    d_from_two, gain_two_grad = norm_back(residual, factor_two, gain_second, d_normed_two)
    d_residual = cot_low.astype(jnp.float32) + d_from_two
    d_branch = d_residual.astype(jnp.bfloat16)
    again_query, again_key, again_value, again_out = (
        lax.all_gather(w_query, "ctx", axis=1, tiled=True),
        lax.all_gather(w_key, "ctx", axis=1, tiled=True),
        lax.all_gather(w_value, "ctx", axis=1, tiled=True),
        lax.all_gather(w_out, "ctx", axis=0, tiled=True),
    )
    grad_out = jnp.dot(attended.T, d_branch, preferred_element_type=jnp.float32)
    d_attended = (
        jnp.dot(d_branch, again_out.T, preferred_element_type=jnp.float32)
        .astype(jnp.bfloat16)
        .reshape(tok_dev, HEADS, head_size)
    )
    d_prob = jnp.einsum(
        "qhd,khd->hqk", d_attended, values_heads, preferred_element_type=jnp.float32
    )
    d_score = (d_prob * sig_score * (1.0 - sig_score) * visible[None]).astype(jnp.bfloat16)
    d_qrot = (
        jnp.einsum("hqk,khd->qhd", d_score, keys_heads, preferred_element_type=jnp.float32)
        * scale_factor
    )
    key_part = (
        jnp.einsum("hqk,qhd->khd", d_score, q_rot, preferred_element_type=jnp.float32)
        * scale_factor
    ).reshape(row_keys, model_width)
    value_part = jnp.einsum(
        "hqk,qhd->khd", attn_probs, d_attended, preferred_element_type=jnp.float32
    ).reshape(row_keys, model_width)
    d_krot, d_vsum = (
        lax.psum_scatter(
            key_part.astype(jnp.bfloat16), "ctx", scatter_dimension=0, tiled=True
        ).astype(jnp.float32),
        lax.psum_scatter(
            value_part.astype(jnp.bfloat16), "ctx", scatter_dimension=0, tiled=True
        ).astype(jnp.float32),
    )
    d_query = rotate(d_qrot, cosine, -sine_table).reshape(tok_dev, model_width).astype(jnp.bfloat16)
    d_key = (
        rotate(d_krot.reshape(tok_dev, HEADS, head_size), cosine, -sine_table)
        .reshape(tok_dev, model_width)
        .astype(jnp.bfloat16)
    )
    d_value = d_vsum.astype(jnp.bfloat16)
    grad_query = jnp.dot(normed.T, d_query, preferred_element_type=jnp.float32)
    grad_key = jnp.dot(normed.T, d_key, preferred_element_type=jnp.float32)
    grad_value = jnp.dot(normed.T, d_value, preferred_element_type=jnp.float32)
    d_normed = (
        jnp.dot(d_query, again_query.T, preferred_element_type=jnp.float32)
        + jnp.dot(d_key, again_key.T, preferred_element_type=jnp.float32)
        + jnp.dot(d_value, again_value.T, preferred_element_type=jnp.float32)
    )
    d_from_one, gain_one_grad = norm_back(tokens, factor_one, gain_first, d_normed)
    acts_grad = (d_residual + d_from_one).reshape(1, 1, tok_dev, model_width)
    shard_query, shard_key, shard_value, shard_out, shard_gain_one, shard_gain_two = (
        lax.psum_scatter(
            grad_query.astype(jnp.bfloat16), "ctx", scatter_dimension=1, tiled=True
        ).astype(jnp.float32),
        lax.psum_scatter(
            grad_key.astype(jnp.bfloat16), "ctx", scatter_dimension=1, tiled=True
        ).astype(jnp.float32),
        lax.psum_scatter(
            grad_value.astype(jnp.bfloat16), "ctx", scatter_dimension=1, tiled=True
        ).astype(jnp.float32),
        lax.psum_scatter(
            grad_out.astype(jnp.bfloat16), "ctx", scatter_dimension=0, tiled=True
        ).astype(jnp.float32),
        lax.psum_scatter(
            gain_one_grad.astype(jnp.bfloat16), "ctx", scatter_dimension=0, tiled=True
        ).astype(jnp.float32),
        lax.psum_scatter(
            gain_two_grad.astype(jnp.bfloat16), "ctx", scatter_dimension=0, tiled=True
        ).astype(jnp.float32),
    )
    totals = (
        lax.psum(shard_query.astype(jnp.bfloat16), "grp").astype(jnp.float32),
        lax.psum(shard_key.astype(jnp.bfloat16), "grp").astype(jnp.float32),
        lax.psum(shard_value.astype(jnp.bfloat16), "grp").astype(jnp.float32),
        lax.psum(shard_out.astype(jnp.bfloat16), "grp").astype(jnp.float32),
        lax.psum(shard_gate.astype(jnp.bfloat16), "grp").astype(jnp.float32),
        lax.psum(shard_up.astype(jnp.bfloat16), "grp").astype(jnp.float32),
        lax.psum(shard_down.astype(jnp.bfloat16), "grp").astype(jnp.float32),
        lax.psum(shard_gain_one.astype(jnp.bfloat16), "grp").astype(jnp.float32),
        lax.psum(shard_gain_two.astype(jnp.bfloat16), "grp").astype(jnp.float32),
    )
    return (
        mixed.reshape(1, 1, tok_dev, model_width),
        acts_grad,
        totals[0],
        totals[1],
        totals[2],
        totals[3],
        totals[4],
        totals[5],
        totals[6],
        totals[7],
        totals[8],
    )


def solution(mesh):
    in_specs = (
        P("grp", "ctx", None, None),
        P("grp", None),
        P(None, "ctx"),
        P(None, "ctx"),
        P(None, "ctx"),
        P("ctx", None),
        P(None, "ctx"),
        P(None, "ctx"),
        P("ctx", None),
        P("ctx"),
        P("ctx"),
        P("grp", "ctx", None, None),
    )
    out_specs = (
        P("grp", "ctx", None, None),
        P("grp", "ctx", None, None),
        P(None, "ctx"),
        P(None, "ctx"),
        P(None, "ctx"),
        P("ctx", None),
        P(None, "ctx"),
        P(None, "ctx"),
        P("ctx", None),
        P("ctx"),
        P("ctx"),
    )
    return jax.shard_map(local, mesh=mesh, in_specs=in_specs, out_specs=out_specs, check_vma=False)
```

profile of v0, /device:TPU:0, one launch (start us, length us, event | category | flops | bytes accessed | tf_op | source)
XLA Modules:
  0.0 1809.3 jit_solution(3787558131211717108)
XLA Ops:
  9.4 20.4 %all-gather = bf16[16,1,128]{2,1,0:T(2,128)(2,1)S(1)} all-gather(bf16[1,1,128]{2,1,0:T(2,128)(2,1)} %bitcast.189), channel_id=1, replica_groups=mesh['grp'=8,'ctx'=16] {'ctx'}, dimensions={0}, use_global_device_ids=true | all-gather | bytes 4352 | tf_op jit(solution)/shard_map/all_gather | solution.py:90
  35.1 37.5 %all-gather.18.cloned.1.call-done = bf16[2048,2048]{1,0:T(8,128)(2,1)} async-done(((bf16[2048,128]{1,0:T(8,128)(2,1)}), bf16[2048,2048]{1,0:T(8,128)(2,1)}) %all-gather.18.cloned.1.call-update) | async-done | bytes 8388624 | tf_op jit(solution)/shard_map/all_gather | solution.py:87
  72.6 12.4 copy.40
  85.0 50.0 %all-gather.16.cloned.1.call-done = bf16[2048,2048]{1,0:T(8,128)(2,1)} async-done(((bf16[2048,128]{1,0:T(8,128)(2,1)}), bf16[2048,2048]{1,0:T(8,128)(2,1)}) %all-gather.16.cloned.1.call-update) | async-done | bytes 8388624 | tf_op jit(solution)/shard_map/all_gather | solution.py:86
  135.0 12.4 copy.39
  147.4 6.0 fusion.35
  153.5 2.5 fusion.37
  157.3 40.0 %all-gather.12.cloned.1.call-done = bf16[2048,2048]{1,0:T(8,128)(2,1)} async-done(((bf16[2048,128]{1,0:T(8,128)(2,1)}), bf16[2048,2048]{1,0:T(8,128)(2,1)}) %all-gather.12.cloned.1.call-update) | async-done | bytes 8388624 | tf_op jit(solution)/shard_map/all_gather | solution.py:88
  197.3 5.5 convolution_convert_fusion.9
  205.7 18.2 %all-gather.1 = bf16[16,1,128]{2,1,0:T(2,128)(2,1)S(1)} all-gather(bf16[1,1,128]{2,1,0:T(2,128)(2,1)S(1)} %bitcast.190), channel_id=1, replica_groups=mesh['grp'=8,'ctx'=16] {'ctx'}, dimensions={0}, use_global_device_ids=true | all-gather | bytes 4352 | tf_op jit(solution)/shard_map/all_gather | solution.py:91
  226.1 34.0 %all-gather.20.cloned.1.call-done = bf16[2048,2048]{0,1:T(8,128)(2,1)} async-done(((bf16[128,2048]{0,1:T(8,128)(2,1)}), bf16[2048,2048]{0,1:T(8,128)(2,1)}) %all-gather.20.cloned.1.call-update) | async-done | bytes 8388624 | tf_op jit(solution)/shard_map/all_gather | solution.py:109
  260.2 11.5 add_divide_fusion
  271.7 42.8 %all-gather.14.cloned.1.call-done = bf16[2048,2048]{1,0:T(8,128)(2,1)} async-done(((bf16[128,2048]{1,0:T(8,128)(2,1)}), bf16[2048,2048]{1,0:T(8,128)(2,1)}) %all-gather.14.cloned.1.call-update) | async-done | bytes 8388624 | tf_op jit(solution)/shard_map/all_gather | solution.py:110
  314.5 10.2 fusion.17
  324.7 44.4 %all-gather.22.cloned.1.call-done = bf16[2048,2048]{1,0:T(8,128)(2,1)} async-done(((bf16[128,2048]{1,0:T(8,128)(2,1)}), bf16[2048,2048]{1,0:T(8,128)(2,1)}) %all-gather.22.cloned.1.call-update) | async-done | bytes 8388624 | tf_op jit(solution)/shard_map/all_gather | solution.py:89
  369.0 4.7 multiply_reduce_fusion.2
  374.0 116.5 %all-gather.24.cloned.1.call-done = bf16[2048,5504]{0,1:T(8,128)(2,1)} async-done(((bf16[2048,344]{0,1:T(8,128)(2,1)}), bf16[2048,5504]{0,1:T(8,128)(2,1)}) %all-gather.24.cloned.1.call-update) | async-done | bytes 22544400 | tf_op jit(solution)/shard_map/all_gather | solution.py:130
  490.4 13.3 fusion.73
  503.7 108.0 %all-gather.26.cloned.1.call-done = bf16[2048,5504]{0,1:T(8,128)(2,1)} async-done(((bf16[2048,344]{0,1:T(8,128)(2,1)}), bf16[2048,5504]{0,1:T(8,128)(2,1)}) %all-gather.26.cloned.1.call-update) | async-done | bytes 22544400 | tf_op jit(solution)/shard_map/all_gather | solution.py:131
  611.7 13.3 fusion.74
  625.0 108.0 %all-gather.28.cloned.1.call-done = bf16[5504,2048]{1,0:T(8,128)(2,1)} async-done(((bf16[344,2048]{1,0:T(8,128)(2,1)}), bf16[5504,2048]{1,0:T(8,128)(2,1)}) %all-gather.28.cloned.1.call-update) | async-done | bytes 22544400 | tf_op jit(solution)/shard_map/all_gather | solution.py:132
  733.0 14.8 multiply_convert_fusion.3
  747.8 9.6 fusion.75
  757.5 10.2 multiply_reduce_fusion
  768.0 3.7 convolution_convert_fusion.8
  771.7 2.0 copy.59
  773.8 11.8 convolution_convert_fusion.7
  785.6 12.3 copy.51
  798.0 14.6 multiply_convert_fusion.1
  812.6 9.3 multiply_convert_fusion
  821.9 12.4 copy.49
  834.3 39.4 %reduce-scatter.30.cloned.1.call-done = bf16[128,2048]{1,0:T(8,128)(2,1)} async-done(((bf16[2048,2048]{1,0:T(8,128)(2,1)}), bf16[128,2048]{1,0:T(8,128)(2,1)}) %reduce-scatter.30.cloned.1.call-update) | async-done | bytes 524304
  873.7 6.8 convolution_convert_fusion.4
  880.5 11.8 copy.57
  892.6 9.2 fusion.11
  901.8 47.6 %reduce-scatter.28.cloned.1.call-done = bf16[128,2048]{1,0:T(8,128)(2,1)} async-done(((bf16[2048,2048]{1,0:T(8,128)(2,1)}), bf16[128,2048]{1,0:T(8,128)(2,1)}) %reduce-scatter.28.cloned.1.call-update) | async-done | bytes 524304
  949.4 2.0 copy.50
  955.8 5.8 convolution_convert_fusion.6
  961.5 12.4 copy.53
  974.0 6.8 convolution_convert_fusion.5
  980.8 12.4 copy.55
  993.3 6.7 convolution_convert_fusion.3
  1000.3 12.4 convolution_convert_fusion.2
  1012.7 12.2 convolution_convert_fusion.1
  1026.0 12.3 convolution_convert_fusion
  1038.7 2.0 copy.58
  1040.7 60.0 %reduce-scatter.32.cloned.1.call-done = bf16[128,2048]{1,0:T(8,128)(2,1)} async-done(((bf16[2048,2048]{1,0:T(8,128)(2,1)}), bf16[128,2048]{1,0:T(8,128)(2,1)}) %reduce-scatter.32.cloned.1.call-update) | async-done | bytes 524304
  1100.7 2.0 copy.54
  1102.8 73.6 %reduce-scatter.34.cloned.1.call-done = bf16[128,2048]{1,0:T(8,128)(2,1)} async-done(((bf16[2048,2048]{1,0:T(8,128)(2,1)}), bf16[128,2048]{1,0:T(8,128)(2,1)}) %reduce-scatter.34.cloned.1.call-update) | async-done | bytes 524304
  1176.4 2.0 copy.56
  1178.4 73.5 %reduce-scatter.20.cloned.1.call-done = bf16[128,2048]{1,0:T(8,128)(2,1)} async-done(((bf16[2048,2048]{1,0:T(8,128)(2,1)}), bf16[128,2048]{1,0:T(8,128)(2,1)}) %reduce-scatter.20.cloned.1.call-update) | async-done | bytes 524304 | tf_op jit(solution)/shard_map/reduce_scatter | solution.py:229
  1251.9 128.2 %reduce-scatter.22.cloned.1.call-done = bf16[2048,344]{0,1:T(8,128)(2,1)} async-done(((bf16[2048,5504]{0,1:T(8,128)(2,1)}), bf16[2048,344]{0,1:T(8,128)(2,1)}) %reduce-scatter.22.cloned.1.call-update) | async-done | bytes 1409040 | tf_op jit(solution)/shard_map/reduce_scatter | solution.py:151
  1380.2 128.4 %reduce-scatter.24.cloned.1.call-done = bf16[2048,344]{0,1:T(8,128)(2,1)} async-done(((bf16[2048,5504]{0,1:T(8,128)(2,1)}), bf16[2048,344]{0,1:T(8,128)(2,1)}) %reduce-scatter.24.cloned.1.call-update) | async-done | bytes 1409040 | tf_op jit(solution)/shard_map/reduce_scatter | solution.py:154
  1508.6 128.4 %reduce-scatter.26.cloned.1.call-done = bf16[344,2048]{1,0:T(8,128)(2,1)} async-done(((bf16[5504,2048]{1,0:T(8,128)(2,1)}), bf16[344,2048]{1,0:T(8,128)(2,1)}) %reduce-scatter.26.cloned.1.call-update) | async-done | bytes 1409040 | tf_op jit(solution)/shard_map/reduce_scatter | solution.py:157
  1638.3 11.8 fusion.10
  1650.2 6.4 fusion.76
  1656.7 6.5 convolution_add_fusion.3
  1663.3 3.1 fusion.29
  1666.3 30.8 %all-reduce.2 = (bf16[2048]{0:T(1024)(128)(2,1)S(1)}, bf16[2048]{0:T(1024)(128)(2,1)S(1)}) all-reduce(bf16[2048]{0:T(1024)(128)(2,1)S(1)} %get-tuple-element.13, bf16[2048]{0:T(1024)(128)(2,1)S(1)} %copy-done.23), channel_id=11, replica_groups=mesh['grp'=8,'ctx'=16] {'ctx'}, use_global_device_ids=true, to_apply=%region_21.22.clone | all-reduce | flops 4096 | bytes 16384
  1697.3 24.5 %all-reduce.3 = (bf16[128]{0:T(256)(128)(2,1)S(1)}, bf16[128]{0:T(256)(128)(2,1)S(1)}) all-reduce(bf16[128]{0:T(256)(128)(2,1)S(1)} %dynamic-slice.1, bf16[128]{0:T(256)(128)(2,1)S(1)} %dynamic-slice.3), channel_id=1, replica_groups=mesh['grp'=8,'ctx'=16] {'grp'}, use_global_device_ids=true, to_apply=%region_22.23 | all-reduce | flops 256 | bytes 1024 | tf_op jit(solution)/shard_map/psum | solution.py:247
  1724.3 65.4 %all-reduce.7.cloned.1.call-done = (bf16[2048,128]{1,0:T(8,128)(2,1)}, bf16[2048,128]{1,0:T(8,128)(2,1)}, bf16[2048,128]{1,0:T(8,128)(2,1)}, bf16[128,2048]{1,0:...) async-done(((bf16[2048,128]{1,0:T(8,128)(2,1)}, bf16[2048,128]{1,0:T(8,128)(2,1)}, bf16[2048,128]{1,0:T(8,128)(2,1)}, ...) | async-done | bytes 6324240 | tf_op jit(solution)/shard_map/psum | solution.py:240
  1789.6 3.4 convert_element_type.289
  1793.0 3.2 convert_element_type.291
  1796.3 1.9 convert_element_type.293
  (136 shorter events, 28.2 us)
Async XLA Ops:
  7.2 65.5 %all-gather.18.cloned.1.call-start = ((), (), s32[]{:S(2)}) async-start(), calls=%async_computation.12 | async-start | bytes 8912896 | tf_op jit(solution)/shard_map/all_gather | solution.py:87
  7.9 127.1 %all-gather.16.cloned.1.call-start = ((), (), s32[]{:S(2)}) async-start(), calls=%async_computation.11 | async-start | bytes 8912896 | tf_op jit(solution)/shard_map/all_gather | solution.py:86
  8.7 188.6 %all-gather.12.cloned.1.call-start = ((), (), s32[]{:S(2)}) async-start(), calls=%async_computation.9 | async-start | bytes 8912896 | tf_op jit(solution)/shard_map/all_gather | solution.py:88
  9.4 250.8 %all-gather.20.cloned.1.call-start = ((), (), s32[]{:S(2)}) async-start(), calls=%async_computation.13 | async-start | bytes 8912896 | tf_op jit(solution)/shard_map/all_gather | solution.py:109
  35.1 120.8 %copy-start.20 = (f32[128,64]{0,1:T(8,128)}, f32[128,64]{0,1:T(8,128)S(1)}, u32[]{:S(2)}) copy-start(f32[128,64]{0,1:T(8,128)S(1)} %get-tuple-element.45) | copy-start | bytes 98308
  135.0 12.4 copy-start
  147.4 6.0 copy-start.1
  156.3 103.9 %copy-start.13 = (bf16[128,16,64]{0,2,1:T(8,128)(2,1)}, bf16[128,16,64]{0,2,1:T(8,128)(2,1)S(1)}, u32[]{:S(2)}) copy-start(bf16[128,16,64]{0,2,1:T(8,128)(2,1)S(1)} %get-tuple-element.35) | copy-start | bytes 786436
  156.3 103.9 %copy-start.15 = (bf16[128,16,64]{0,2,1:T(8,128)(2,1)}, bf16[128,16,64]{0,2,1:T(8,128)(2,1)S(1)}, u32[]{:S(2)}) copy-start(bf16[128,16,64]{0,2,1:T(8,128)(2,1)S(1)} %get-tuple-element.36) | copy-start | bytes 786436
  157.3 48.4 %copy-start.25 = (bf16[128]{0:T(256)(128)(2,1)S(1)}, bf16[128]{0:T(256)(128)(2,1)}, u32[]{:S(2)}) copy-start(bf16[128]{0:T(256)(128)(2,1)} %param.22) | copy-start | bytes 772
  157.3 157.2 %all-gather.14.cloned.1.call-start = ((), (), s32[]{:S(2)}) async-start(), calls=%async_computation.10 | async-start | bytes 8912896 | tf_op jit(solution)/shard_map/all_gather | solution.py:110
  202.8 166.3 %all-gather.22.cloned.1.call-start = ((), (), s32[]{:S(2)}) async-start(), calls=%async_computation.14 | async-start | bytes 8912896 | tf_op jit(solution)/shard_map/all_gather | solution.py:89
  203.4 287.1 %all-gather.24.cloned.1.call-start = ((), (), s32[]{:S(2)}) async-start(), calls=%async_computation.15 | async-start | bytes 23953408 | tf_op jit(solution)/shard_map/all_gather | solution.py:130
  204.1 407.6 %all-gather.26.cloned.1.call-start = ((), (), s32[]{:S(2)}) async-start(), calls=%async_computation.16 | async-start | bytes 23953408 | tf_op jit(solution)/shard_map/all_gather | solution.py:131
  204.9 528.1 %all-gather.28.cloned.1.call-start = ((), (), s32[]{:S(2)}) async-start(), calls=%async_computation.17 | async-start | bytes 23953408 | tf_op jit(solution)/shard_map/all_gather | solution.py:132
  205.6 668.1 %reduce-scatter.30.cloned.1.call-start = ((), (), s32[]{:S(2)}) async-start(), calls=%async_computation.23 | async-start | bytes 8912896
  226.1 88.3 %copy-start.2 = (f32[128,2048]{1,0:T(8,128)}, f32[128,2048]{1,0:T(8,128)S(1)}, u32[]{:S(2)}) copy-start(f32[128,2048]{1,0:T(8,128)S(1)} %and_convert_fusion) | copy-start | bytes 3145732
  324.7 49.1 %copy-start.3 = (bf16[16,128,128]{2,1,0:T(8,128)(2,1)}, bf16[16,128,128]{2,1,0:T(8,128)(2,1)S(1)}, u32[]{:S(2)}) copy-start(bf16[16,128,128]{2,1,0:T(8,128)(2,1)S(1)} %fusion.17) | copy-start | bytes 1572868
  747.8 9.7 copy-start.4
  747.8 9.7 copy-start.5
  747.8 20.2 %slice-start = ((s8[8388608]{0:T(1024)(128)(4,1)}), s8[4194304]{0:T(1024)(128)(4,1)S(1)}, s32[]{:S(2)}) async-start(s8[8388608]{0:T(1024)(128)(4,1)} %bitcast.151), calls=%async_computation.28 | async-start | bytes 8388608
  757.4 10.2 copy-start.9
  757.5 10.6 slice-start.1
  797.9 14.7 copy-start.14
  797.9 151.5 %reduce-scatter.28.cloned.1.call-start = ((), (), s32[]{:S(2)}) async-start(), calls=%async_computation.22 | async-start | bytes 8912896
  834.2 204.4 %reduce-scatter.36.cloned.1.call-start = ((), (), s32[]{:S(2)}) async-start(), calls=%async_computation.26 | async-start | bytes 8912896
  892.3 60.3 %copy-start.21 = (f32[128,64]{0,1:T(8,128)S(1)}, f32[128,64]{0,1:T(8,128)}, u32[]{:S(2)}) copy-start(f32[128,64]{0,1:T(8,128)} %copy-done.20) | copy-start | bytes 98308
  892.3 60.3 %copy-start.22 = (f32[128,64]{0,1:T(8,128)S(1)}, f32[128,64]{0,1:T(8,128)}, u32[]{:S(2)}) copy-start(f32[128,64]{0,1:T(8,128)} %get-tuple-element.43) | copy-start | bytes 98308
  892.3 208.4 %reduce-scatter.32.cloned.1.call-start = ((), (), s32[]{:S(2)}) async-start(), calls=%async_computation.24 | async-start | bytes 8912896
  955.0 0.8 copy-start.6
  973.9 202.4 %reduce-scatter.34.cloned.1.call-start = ((), (), s32[]{:S(2)}) async-start(), calls=%async_computation.25 | async-start | bytes 8912896
  993.2 258.7 %reduce-scatter.20.cloned.1.call-start = ((), (), s32[]{:S(2)}) async-start(), calls=%async_computation.18 | async-start | bytes 8912896 | tf_op jit(solution)/shard_map/reduce_scatter | solution.py:229
  1000.0 380.2 %reduce-scatter.22.cloned.1.call-start = ((), (), s32[]{:S(2)}) async-start(), calls=%async_computation.19 | async-start | bytes 23953408 | tf_op jit(solution)/shard_map/reduce_scatter | solution.py:151
  1012.7 495.9 %reduce-scatter.24.cloned.1.call-start = ((), (), s32[]{:S(2)}) async-start(), calls=%async_computation.20 | async-start | bytes 23953408 | tf_op jit(solution)/shard_map/reduce_scatter | solution.py:154
  1024.9 1.0 copy-start.10
  1025.0 612.1 %reduce-scatter.26.cloned.1.call-start = ((), (), s32[]{:S(2)}) async-start(), calls=%async_computation.21 | async-start | bytes 23953408 | tf_op jit(solution)/shard_map/reduce_scatter | solution.py:157
  1038.3 598.7 %copy-start.26 = (u32[128]{0:T(128)S(1)}, u32[128]{0:T(128)}, u32[]{:S(2)}) copy-start(u32[128]{0:T(128)} %constant.81) | copy-start | bytes 1540
  1038.3 751.3 %all-reduce.7.cloned.1.call-start = ((), (), s32[]{:S(2)}) async-start(), calls=%async_computation.27 | async-start | bytes 12648448 | tf_op jit(solution)/shard_map/psum | solution.py:240
  1638.3 11.9 copy-start.7
  1650.2 6.5 copy-start.8
  1650.2 13.0 slice-start.2
  1650.2 13.0 copy-start.11
  1656.6 6.6 slice-start.3
  1663.2 3.1 copy-start.23
  1663.2 59.6 %copy-start.24 = (f32[128]{0:T(128)S(1)}, f32[128]{0:T(128)}, u32[]{:S(2)}) copy-start(f32[128]{0:T(128)} %get-tuple-element.46) | copy-start | bytes 1540
  1789.6 6.7 copy-start.12
  1789.6 8.5 copy-start.19
  1789.6 9.6 copy-start.18
  1789.6 10.6 copy-start.17
  1789.6 11.7 copy-start.16
Sparse Core Ops, SparseCore 0:
  9.6 62.9 all-gather.17
  74.2 60.7 all-gather.15
  136.6 60.6 all-gather.11
  199.3 60.7 all-gather.19
  262.3 52.1 all-gather.13
  316.0 52.9 all-gather.21
  370.7 119.6 all-gather.23
  492.1 119.5 all-gather.25
  613.4 119.5 all-gather.27
  798.0 75.5 reduce-scatter.29
  876.1 73.2 reduce-scatter.27
  951.7 73.2 reduce-scatter.35
  1027.4 73.2 reduce-scatter.31
  1103.0 73.3 reduce-scatter.33
  1178.6 73.2 reduce-scatter.19
  1254.2 125.9 reduce-scatter.21
  1382.4 126.1 reduce-scatter.23
  1510.9 126.1 reduce-scatter.25
  1641.3 148.3 all-reduce.6
where the time goes:
time: 1820 us; the launch traced here: 1810 us
  waiting for transfers between devices  1330 us (73%)
  matrix products  241 us (13%)
  local copies, waits for them, and re-layouts  100 us (5%)
  blocking collectives  94 us (5%)
  other arithmetic  26.5 us (1%)
    unnamed x24, waiting for transfers between devices  225 us
    reduce_scatter x1, waiting for transfers between devices, local(): lax.psum_scatter(grad_down.astype(jnp.bfloat16), 'ctx', scatter_dimension...  128 us
    reduce_scatter x1, waiting for transfers between devices, local(): lax.psum_scatter(grad_up.astype(jnp.bfloat16), 'ctx', scatter_dimension=1...  128 us
    reduce_scatter x1, waiting for transfers between devices, local(): lax.psum_scatter(grad_gate.astype(jnp.bfloat16), 'ctx', scatter_dimension...  128 us
    all_gather x1, waiting for transfers between devices, local(): lax.all_gather(w_gate, 'ctx', axis=1, tiled=True)  116 us
    all_gather x1, waiting for transfers between devices, local(): lax.all_gather(w_down, 'ctx', axis=0, tiled=True)  108 us
    all_gather x1, waiting for transfers between devices, local(): lax.all_gather(w_up, 'ctx', axis=1, tiled=True)  108 us
    reduce_scatter x1, waiting for transfers between devices, local(): lax.psum_scatter(grad_out.astype(jnp.bfloat16), 'ctx', scatter_dimension=...  73.5 us
  transfers between devices with their start and end apart: 19, of which 18 were waited for; matrix products, arithmetic and copies ran while one was open for 16% of the time, Pallas kernels for 0%

commit v1 on v0

v1 whole, which is shorter than its diff:
```python
import math

import jax
import jax.numpy as jnp
from jax import lax
from jax.sharding import PartitionSpec as P

EPSILON = 1e-05
BF = jnp.bfloat16
F32 = jnp.float32


def dot(a, b):
    return jnp.dot(a, b, preferred_element_type=F32)


def dot_t(a, b):
    return lax.dot_general(a, b, (((1,), (1,)), ((), ())), preferred_element_type=F32)


def t_dot(a, b):
    return lax.dot_general(a, b, (((0,), (0,)), ((), ())), preferred_element_type=F32)


def rotary(offsets, head_size):
    frequency = 10000.0 ** (-(jnp.arange(head_size // 2).astype(F32) * 2.0 / head_size))
    angles = offsets.astype(F32)[:, None] * frequency[None, :]
    return jnp.cos(angles), jnp.sin(angles)


def rotate(tensor, cosine, sine):
    middle = tensor.shape[-1] // 2
    a, b = tensor[..., :middle], tensor[..., middle:]
    return jnp.concatenate([a * cosine - b * sine, b * cosine + a * sine], -1)


def norm_back(source, factor, gain, incoming):
    scaled = incoming * gain
    grad_source = factor * scaled - source * factor**3 * jnp.mean(
        scaled * source, -1, keepdims=True
    )
    return grad_source, jnp.sum(incoming * source * factor, 0)


def to_rows(packed, n_ctx):
    rest = packed.shape[1:]
    v = packed.reshape((n_ctx, 2, -1) + rest)
    return jnp.concatenate([v[:, 0], v[::-1, 1]], 0).reshape((-1,) + rest)


def to_packed(rows, n_ctx):
    rest = rows.shape[1:]
    v = rows.reshape((2 * n_ctx, -1) + rest)
    return jnp.stack([v[:n_ctx], v[n_ctx:][::-1]], 1).reshape((-1,) + rest)


def local(
    acts,
    doc_lengths,
    w_query,
    w_key,
    w_value,
    w_out,
    w_gate,
    w_up,
    w_down,
    gain_attn,
    gain_mlp,
    cotangent,
):
    tok = acts.shape[2]
    width = acts.shape[3]
    n_ctx = lax.axis_size("ctx")
    me = lax.axis_index("ctx")
    row = n_ctx * tok
    head = w_query.shape[1]
    scale = 1.0 / math.sqrt(head)

    acts_rows = acts.reshape(tok, width)
    cot_low = cotangent.reshape(tok, width)
    gains = jnp.zeros((16, width), BF)
    gains = gains.at[0, :head].set(gain_attn).at[1, :head].set(gain_mlp)
    gathered = lax.all_gather(
        jnp.concatenate([acts_rows, gains], 0), "ctx", axis=0, tiled=False
    )
    cot_all = lax.all_gather(cot_low, "ctx", axis=0, tiled=True)
    tokens_all = gathered[:, :tok].reshape(row, width).astype(F32)
    gain_first = gathered[:, tok, :head].reshape(width).astype(F32)
    gain_second = gathered[:, tok + 1, :head].reshape(width).astype(F32)

    factor_all = lax.rsqrt(jnp.mean(tokens_all * tokens_all, -1, keepdims=True) + EPSILON)
    normed = (tokens_all * factor_all * gain_first).astype(BF)
    w_qkv = jnp.concatenate([w_query, w_key, w_value], 1)
    qkv = to_rows(dot(normed, w_qkv), n_ctx)

    lengths = doc_lengths.reshape(2)
    pos = jnp.arange(row, dtype=jnp.int32)
    doc = (pos >= lengths[0]).astype(jnp.int32)
    own = jnp.where(doc == 0, lengths[0], lengths[1])
    bias = -jnp.log(own.astype(F32))
    cosine, sine = rotary(pos - doc * lengths[0], head)
    visible = ((doc[None, :] == doc[:, None]) & (pos[None, :] <= pos[:, None])).astype(F32)

    q_rot = rotate(qkv[:, :head], cosine, sine).astype(BF)
    k_rot = rotate(qkv[:, head : 2 * head], cosine, sine).astype(BF)
    v_low = qkv[:, 2 * head :].astype(BF)
    score = dot_t(q_rot, k_rot) * scale + bias[:, None]
    sig = jax.nn.sigmoid(score)
    prob = (sig * visible).astype(BF)
    attended = to_packed(dot(prob, v_low).astype(BF), n_ctx)
    branch = lax.psum_scatter(
        dot(attended, w_out).astype(BF), "ctx", scatter_dimension=0, tiled=True
    ).astype(F32)

    tokens = acts_rows.astype(F32)
    factor_one = lax.rsqrt(jnp.mean(tokens * tokens, -1, keepdims=True) + EPSILON)
    residual = tokens + branch
    factor_two = lax.rsqrt(jnp.mean(residual * residual, -1, keepdims=True) + EPSILON)
    normed_two = (residual * factor_two * gain_second).astype(BF)
    normed_two_all = lax.all_gather(normed_two, "ctx", axis=0, tiled=True)

    gate = dot(normed_two_all, w_gate)
    up = dot(normed_two_all, w_up)
    d_hidden = dot_t(cot_all, w_down)
    sig_gate = jax.nn.sigmoid(gate)
    silu = gate * sig_gate
    hidden = (silu * up).astype(BF)
    d_gate = (d_hidden * up * sig_gate * (1.0 + gate * (1.0 - sig_gate))).astype(BF)
    d_up = (d_hidden * silu).astype(BF)
    d_normed_two = lax.psum_scatter(
        (dot_t(d_gate, w_gate) + dot_t(d_up, w_up)).astype(BF),
        "ctx",
        scatter_dimension=0,
        tiled=True,
    ).astype(F32)
    mlp_out = lax.psum_scatter(
        dot(hidden, w_down).astype(BF), "ctx", scatter_dimension=0, tiled=True
    ).astype(F32)
    mixed = (residual + mlp_out).astype(BF)
    grad_down = t_dot(hidden, cot_all)
    grad_gate = t_dot(normed_two_all, d_gate)
    grad_up = t_dot(normed_two_all, d_up)
    ff_totals = lax.psum(
        (grad_gate.astype(BF), grad_up.astype(BF), grad_down.astype(BF)), "grp"
    )

    d_from_two, gain_two_part = norm_back(residual, factor_two, gain_second, d_normed_two)
    d_residual = cot_low.astype(F32) + d_from_two
    d_branch = lax.all_gather(d_residual.astype(BF), "ctx", axis=0, tiled=True)
    grad_out = t_dot(attended, d_branch)
    d_attended = to_rows(dot_t(d_branch, w_out).astype(BF), n_ctx)

    d_prob = dot_t(d_attended, v_low)
    d_score = (d_prob * sig * (1.0 - sig) * visible).astype(BF)
    d_qrot = dot(d_score, k_rot) * scale
    d_krot = t_dot(d_score, q_rot) * scale
    d_vsum = t_dot(prob, d_attended)
    d_qkv = to_packed(
        jnp.concatenate(
            [rotate(d_qrot, cosine, -sine), rotate(d_krot, cosine, -sine), d_vsum], 1
        ).astype(BF),
        n_ctx,
    )
    grad_qkv = t_dot(normed, d_qkv)
    d_normed = lax.psum_scatter(
        dot_t(d_qkv, w_qkv).astype(BF), "ctx", scatter_dimension=0, tiled=True
    ).astype(F32)
    d_from_one, gain_one_part = norm_back(tokens, factor_one, gain_first, d_normed)
    acts_grad = d_residual + d_from_one

    attn_totals = lax.psum((grad_qkv.astype(BF), grad_out.astype(BF)), "grp")
    gain_parts = lax.psum(jnp.stack([gain_one_part, gain_two_part]), ("grp", "ctx"))
    gain_mine = lax.dynamic_slice_in_dim(gain_parts, me * head, head, 1)
    total_qkv = attn_totals[0].astype(F32)
    return (
        mixed.reshape(1, 1, tok, width),
        acts_grad.reshape(1, 1, tok, width),
        total_qkv[:, :head],
        total_qkv[:, head : 2 * head],
        total_qkv[:, 2 * head :],
        attn_totals[1].astype(F32),
        ff_totals[0].astype(F32),
        ff_totals[1].astype(F32),
        ff_totals[2].astype(F32),
        gain_mine[0],
        gain_mine[1],
    )


def solution(mesh):
    row = P("grp", "ctx", None, None)
    col = P(None, "ctx")
    dep = P("ctx", None)
    vec = P("ctx")
    in_specs = (row, P("grp", None), col, col, col, dep, col, col, dep, vec, vec, row)
    out_specs = (row, row, col, col, col, dep, col, col, dep, vec, vec)
    return jax.shard_map(local, mesh=mesh, in_specs=in_specs, out_specs=out_specs, check_vma=False)
```

time: 1820 us -> 844 us (0.46)
  waiting for transfers between devices: 1330 us -> 520 us
  matrix products: 241 us -> 139 us
  local copies, waits for them, and re-layouts: 100 us -> 28.5 us
  other arithmetic: 26.5 us -> 68.7 us
  blocking collectives: 94 us -> 66.8 us
    all_gather x9 -> x4, waiting for transfers between devices: 581 us -> 168 us  [the longest x1 51.6 us: local(): lax.all_gather(jnp.concatenate([acts_rows, gains], 0), 'ctx', axis=0, til...]
    reduce_scatter x4, waiting for transfers between devices: 459 us -> 221 us  [the longest x1 75.8 us: local(): lax.psum_scatter(dot(attended, w_out).astype(BF), 'ctx', scatter_dimensio...]
    unnamed x24 -> x9, waiting for transfers between devices: 225 us -> 0.65 us
    dot_general x27 -> x21, matrix products: 241 us -> 139 us  [the longest x7 65.5 us: dot_t(): lax.dot_general(a, b, (((1,), (1,)), ((), ())), preferred_element_type=F32)]
    psum x1, waiting for transfers between devices: 65.4 us -> 130 us  [local(): attn_totals = lax.psum((grad_qkv.astype(BF), grad_out.astype(BF)), 'grp')]
    unnamed x74 -> x102, local copies, waits for them, and re-layouts: 72 us -> 11.2 us
    psum x1, blocking collectives: 24.5 us -> 66.8 us  [local(): lax.psum(jnp.stack([gain_one_part, gain_two_part]), ('grp', 'ctx'))]
    all_gather x2 -> x0, blocking collectives: 38.7 us -> none  [the longest x1 20.4 us: local(): lax.all_gather(gain_attn, 'ctx', axis=0, tiled=True)]
  transfers between devices with their start and end apart: 19 -> 9, of which waited for: 18 -> 9; matrix products, arithmetic and copies ran while one was open for 16% -> 9% of each run, Pallas kernels for 0% -> 0%
where the time goes in v1:
time: 844 us; the launch traced here: 839 us
  waiting for transfers between devices  520 us (62%)
  matrix products  139 us (16%)
  other arithmetic  68.7 us (8%)
  blocking collectives  66.8 us (8%)
  local copies, waits for them, and re-layouts  28.5 us (3%)
  between operations  15 us (2%)
    psum x1, waiting for transfers between devices, local(): attn_totals = lax.psum((grad_qkv.astype(BF), grad_out.astype(BF)), 'grp')  130 us
    reduce_scatter x1, waiting for transfers between devices, local(): lax.psum_scatter(dot(attended, w_out).astype(BF), 'ctx', scatter_dimensio...  75.8 us
    reduce_scatter x1, waiting for transfers between devices, local(): lax.psum_scatter((dot_t(d_gate, w_gate) + dot_t(d_up, w_up)).astype(BF),...  75.8 us
    psum x1, blocking collectives, local(): lax.psum(jnp.stack([gain_one_part, gain_two_part]), ('grp', 'ctx'))  66.8 us
    dot_general x7, matrix products, dot_t(): lax.dot_general(a, b, (((1,), (1,)), ((), ())), preferred_element_type=F32)  65.5 us
    reduce_scatter x1, waiting for transfers between devices, local(): lax.psum_scatter(dot_t(d_qkv, w_qkv).astype(BF), 'ctx', scatter_dimension...  63.4 us
    all_gather x1, waiting for transfers between devices, local(): lax.all_gather(jnp.concatenate([acts_rows, gains], 0), 'ctx', axis=0, til...  51.6 us
    all_gather x1, waiting for transfers between devices, local(): normed_two_all = lax.all_gather(normed_two, 'ctx', axis=0, tiled=True)  49.5 us
  transfers between devices with their start and end apart: 9, of which 9 were waited for; matrix products, arithmetic and copies ran while one was open for 9% of the time, Pallas kernels for 0%

profile of v1, /device:TPU:0, one launch (start us, length us, event | category | flops | bytes accessed | tf_op | source)
XLA Modules:
  0.0 839.2 jit_solution(5324974461255950302)
XLA Ops:
  8.9 1.9 pad_maximum_fusion.2
  10.9 1.3 fusion.77
  12.8 1.2 fusion.68
  14.1 1.3 log_negate_fusion
  15.4 1.9 constant_dynamic-update-slice_fusion.2
  18.9 51.6 %all-gather.11.cloned.1.call-done = bf16[2304,2048]{1,0:T(8,128)(2,1)} async-done(((bf16[144,2048]{1,0:T(8,128)(2,1)}), bf16[2304,2048]{1,0:T(8,128)(2,1)}) %all-gather.11.cloned.1.call-update) | async-done | bytes 9437200 | tf_op jit(solution)/shard_map/all_gather | solution.py:83
  70.5 5.1 multiply_reduce_fusion
  76.4 11.3 %slice_convert_fusion = f32[16,128,2048]{2,1,0:T(8,128)} fusion(bf16[16,144,2048]{2,1,0:T(8,128)(2,1)} %bitcast.116), kind=kLoop, calls=%fused_computation.10 | loop fusion | flops 4194304 | bytes 25165824 | tf_op jit(solution)/shard_map/convert_element_type | solution.py:87
  87.9 8.8 %fusion.1 = f32[16,2,64,384]{3,2,1,0:T(8,128)S(1)} fusion(f32[16,2,64,2048]{3,2,1,0:T(8,128)} %bitcast.124, f32[2048]{0:T(1024)S(1)} %bitcast.141, f32[16,2,64]{2,1,0:T(2,128)S(1)} %rsqrt.35, bf16[2048,384]{1,0:T(8,128)(2,1)} %constant_dynamic-update-slice_fusion), kind=kOutput, calls=%fused_computation.9 | convolution fusion | flops 3233808384 | bytes 21512192 | tf_op jit(solution)/shard_map/dot_general | solution.py:14
  97.4 2.8 fusion.73
  100.3 1.5 copy.42
  101.9 1.5 copy.43
  103.4 2.3 copy.41
  106.9 3.8 fusion.56
  110.7 10.0 %select_convert_fusion.1 = (bf16[2048,2048]{1,0:T(8,128)(2,1)S(1)}, f32[2048,2048]{1,0:T(8,128)}) fusion(s32[2048]{0:T(1024)S(1)} %copy-done.32, f32[2048]{0:T(1024)S(1)} %log_negate_fusion, bf16[2048,64]{0,1:T(8,128)(2,1)S(1)} %get-tuple-element.71, bf16[2048,64]{0,1:T(8,128)(2,1)S(1)} %get-tuple-element.72, bf16[2048,64]{0,1:T(8,128)(2,1)S(1)} %get-tuple-element.62, ...), kind=kOutput, calls=%fused_computation.3 | convolution fusion | flops 1113587712 | bytes 26230784 | tf_op jit(solution)/shard_map/dot_general | solution.py:18
  120.8 4.4 convolution_convert_fusion.9
  126.3 5.6 convolution_convert_fusion.2
  132.0 75.8 %reduce-scatter.5.cloned.1.call-done = bf16[128,2048]{1,0:T(8,128)(2,1)} async-done(((bf16[2048,2048]{1,0:T(8,128)(2,1)}), bf16[128,2048]{1,0:T(8,128)(2,1)}) %reduce-scatter.5.cloned.1.call-update) | async-done | bytes 524304 | tf_op jit(solution)/shard_map/reduce_scatter | solution.py:111
  207.9 1.3 multiply_reduce_fusion.1
  209.2 2.0 multiply_convert_fusion.6
  212.3 49.5 %all-gather.7.cloned.1.call-done = bf16[2048,2048]{1,0:T(8,128)(2,1)} async-done(((bf16[128,2048]{1,0:T(8,128)(2,1)}), bf16[2048,2048]{1,0:T(8,128)(2,1)}) %all-gather.7.cloned.1.call-update) | async-done | bytes 8388624 | tf_op jit(solution)/shard_map/all_gather | solution.py:120
  261.9 8.5 %fusion.79 = f32[2048,344]{0,1:T(8,128)} fusion(bf16[2048,2048]{1,0:T(8,128)(2,1)} %all-gather.7.cloned.1.call-done, bf16[2048,344]{0,1:T(8,128)(2,1)} %param.23), kind=kOutput, calls=%fused_computation.149 | convolution fusion | flops 2885681152 | bytes 12615680 | tf_op jit(solution)/shard_map/dot_general | solution.py:14
  270.4 4.7 fusion.78
  275.2 41.3 %all-gather.13.cloned.1.call-done = bf16[1,1,2048,2048]{3,2,1,0:T(8,128)(2,1)} async-done(((bf16[1,1,128,2048]{3,2,1,0:T(8,128)(2,1)}), bf16[1,1,2048,2048]{3,2,1,0:T(8,128)(2,1)}) %all-gather.13.cloned.1.call-update) | async-done | bytes 8388624 | tf_op jit(solution)/shard_map/all_gather | solution.py:86
  316.4 11.8 %multiply_convert_fusion.3 = (bf16[2048,344]{0,1:T(8,128)(2,1)S(1)}, bf16[2048,344]{0,1:T(8,128)(2,1)S(1)}, bf16[2048,344]{0,1:T(8,128)(2,1)}) fusion(f32[2048,344]{0,1:T(8,128)} %fusion.78, f32[2048,344]{0,1:T(8,128)} %fusion.79, bf16[344,2048]{1,0:T(8,128)(2,1)S(1)} %copy-done, bf16[1,1,2048,2048]{3,2,1,0:T(8,128)(2,1)} %all-gather.13.cloned.1.call-done), kind=kOutput, calls=%fused_computation.21 | convolution fusion | flops 2896248832 | bytes 19660800 | tf_op jit(solution)/shard_map/dot_general | solution.py:18
  328.2 8.2 fusion.80
  336.4 10.2 %add_convert_fusion = bf16[2048,2048]{1,0:T(8,128)(2,1)} fusion(f32[2048,2048]{1,0:T(8,128)} %fusion.80, bf16[2048,344]{0,1:T(8,128)(2,1)S(1)} %get-tuple-element.47, bf16[2048,344]{0,1:T(8,128)(2,1)S(1)} %copy-done.16), kind=kOutput, calls=%fused_computation.2 | convolution fusion | flops 2894069760 | bytes 27983872 | tf_op jit(solution)/shard_map/dot_general | solution.py:18
  346.8 75.8 %reduce-scatter.9.cloned.1.call-done = bf16[128,2048]{1,0:T(8,128)(2,1)} async-done(((bf16[2048,2048]{1,0:T(8,128)(2,1)}), bf16[128,2048]{1,0:T(8,128)(2,1)}) %reduce-scatter.9.cloned.1.call-update) | async-done | bytes 524304 | tf_op jit(solution)/shard_map/reduce_scatter | solution.py:130
  422.6 2.0 fusion.24
  424.6 2.3 fusion.72
  427.0 8.6 %multiply_convert_fusion = bf16[16,128,2048]{2,1,0:T(8,128)(2,1)} fusion(f32[2048]{0:T(1024)S(1)} %bitcast.142, f32[16,128]{1,0:T(8,128)S(1)} %add_rsqrt_fusion, bf16[16,144,2048]{2,1,0:T(8,128)(2,1)} %bitcast.117), kind=kLoop, calls=%fused_computation | loop fusion | flops 16777216 | bytes 16793600 | tf_op jit(solution)/shard_map/convert_element_type | solution.py:92
  435.6 7.7 convolution_convert_fusion.4
  443.3 4.2 convolution_convert_fusion.5
  447.5 4.2 fusion.9
  451.7 25.9 %all-gather.9.cloned.1.call-done = bf16[2048,2048]{1,0:T(8,128)(2,1)} async-done(((bf16[128,2048]{1,0:T(8,128)(2,1)}), bf16[2048,2048]{1,0:T(8,128)(2,1)}) %all-gather.9.cloned.1.call-update) | async-done | bytes 8388624 | tf_op jit(solution)/shard_map/all_gather | solution.py:149
  477.6 5.8 convolution_convert_fusion.8
  483.6 9.7 %select_convert_fusion = bf16[2048,2048]{1,0:T(8,128)(2,1)S(1)} fusion(f32[2048,2048]{1,0:T(8,128)} %get-tuple-element.82, bf16[2048,128]{1,0:T(8,128)(2,1)S(1)} %bitcast.134, s32[2048]{0:T(1024)S(1)} %copy-done.33, f32[2048,384]{1,0:T(8,128)} %bitcast.123), kind=kOutput, calls=%fused_computation.1 | convolution fusion | flops 1107296256 | bytes 26230784 | tf_op jit(solution)/shard_map/dot_general | solution.py:18
  493.3 1.3 convolution_multiply_fusion
  494.7 2.9 convolution_multiply_fusion.1
  497.6 2.3 fusion.67
  499.9 2.3 fusion.66
  502.1 2.3 fusion.65
  504.4 2.3 fusion.64
  506.7 1.3 fusion.12
  508.0 1.3 fusion.75
  509.3 2.3 copy.36
  511.6 2.3 copy.37
  513.9 1.2 reverse_bitcast_fusion.1
  515.1 1.3 pad_maximum_fusion.1
  516.6 9.8 %convolution_convert_fusion.3 = bf16[2048,384]{1,0:T(8,128)(2,1)} fusion(bf16[2048,2048]{1,0:T(8,128)(2,1)} %bitcast.127, bf16[2048,384]{1,0:T(8,128)(2,1)S(1)} %bitcast.130), kind=kOutput, calls=%fused_computation.26 | convolution fusion | flops 3222011904 | bytes 11534336 | tf_op jit(solution)/shard_map/dot_general | solution.py:22
  526.4 2.1 convolution_convert_fusion.6
  528.8 9.8 %convolution_convert_fusion = bf16[2048,2048]{1,0:T(8,128)(2,1)} fusion(bf16[2048,384]{1,0:T(8,128)(2,1)} %bitcast.131, bf16[2048,384]{1,0:T(8,128)(2,1)} %constant_dynamic-update-slice_fusion), kind=kOutput, calls=%fused_computation.17 | convolution fusion | flops 3225419776 | bytes 11534336 | tf_op jit(solution)/shard_map/dot_general | solution.py:18
  538.7 8.2 convolution_convert_fusion.1
  548.1 130.1 %all-reduce.4.cloned.1.call-done = (bf16[2048,384]{1,0:T(8,128)(2,1)}, bf16[128,2048]{1,0:T(8,128)(2,1)}, bf16[2048,344]{0,1:T(8,128)(2,1)}, bf16[2048,344]{0,1:T(8,128)(2,1)}, bf16[344,2048]{1,0:T(8,128)(2,1)}) async-done(((bf16[2048,384]{1,0:T(8,128)(2,1)}, bf16[128,2048]{1,0:T(8,128)(2,1)}, bf16[2048,344]{0,1:T(8,128)(2,1)}, bf16[2048,344]{0,1:T(8,128)(2,1)}, bf16[344,2048]{1,0:T(8,128)(2,1)}), ...) | async-done | bytes 6324240 | tf_op jit(solution)/shard_map/psum | solution.py:171
  678.2 2.2 convert_element_type.207
  680.4 3.2 convert_element_type.209
  683.7 1.9 convert_element_type.211
  685.6 1.9 convert_element_type.213
  687.7 1.8 fusion.74
  689.4 63.4 %reduce-scatter.11.cloned.1.call-done = bf16[128,2048]{1,0:T(8,128)(2,1)} async-done(((bf16[2048,2048]{1,0:T(8,128)(2,1)}), bf16[128,2048]{1,0:T(8,128)(2,1)}) %reduce-scatter.11.cloned.1.call-update) | async-done | bytes 524304 | tf_op jit(solution)/shard_map/reduce_scatter | solution.py:165
  752.9 1.9 fusion.29
  754.8 66.8 %psum.47 = f32[2,2048]{1,0:T(2,128)} all-reduce(f32[2,2048]{1,0:T(2,128)S(1)} %pad_maximum_fusion.11), channel_id=1, replica_groups=mesh['grp'=8,'ctx'=16] {'grp','ctx'}, use_global_device_ids=true, to_apply=%region_16.17 | all-reduce | flops 4096 | bytes 32768 | tf_op jit(solution)/shard_map/psum | solution.py:172
  823.4 5.6 reduce-scatter.7.cloned.1.call-done
  829.0 3.2 fusion.19
  (145 shorter events, 13.2 us)
Async XLA Ops:
  7.2 309.3 %copy-start = (bf16[344,2048]{1,0:T(8,128)(2,1)S(1)}, bf16[344,2048]{1,0:T(8,128)(2,1)}, u32[]{:S(2)}) copy-start(bf16[344,2048]{1,0:T(8,128)(2,1)} %param.24) | copy-start | bytes 4227076
  7.2 10.1 %copy-start.21 = (bf16[2048,128]{1,0:T(8,128)(2,1)S(1)}, bf16[2048,128]{1,0:T(8,128)(2,1)}, u32[]{:S(2)}) copy-start(bf16[2048,128]{1,0:T(8,128)(2,1)} %param.19) | copy-start | bytes 1572868
  7.2 10.9 %copy-start.22 = (bf16[2048,128]{1,0:T(8,128)(2,1)S(1)}, bf16[2048,128]{1,0:T(8,128)(2,1)}, u32[]{:S(2)}) copy-start(bf16[2048,128]{1,0:T(8,128)(2,1)} %param.20) | copy-start | bytes 1572868
  7.2 63.3 %all-gather.11.cloned.1.call-start = ((), (), s32[]{:S(2)}) async-start(), calls=%async_computation.10 | async-start | bytes 10027008 | tf_op jit(solution)/shard_map/all_gather | solution.py:83
  10.8 197.1 %reduce-scatter.5.cloned.1.call-start = ((), (), s32[]{:S(2)}) async-start(), calls=%async_computation.4 | async-start | bytes 8912896 | tf_op jit(solution)/shard_map/reduce_scatter | solution.py:111
  10.8 96.0 %copy-start.30 = (f32[64]{0:T(128)}, f32[64]{0:T(128)S(1)}, u32[]{:S(2)}) copy-start(f32[64]{0:T(128)S(1)} %negate_power_fusion) | copy-start | bytes 772
  12.8 94.1 %copy-start.24 = (f32[2048]{0:T(1024)}, f32[2048]{0:T(1024)S(1)}, u32[]{:S(2)}) copy-start(f32[2048]{0:T(1024)S(1)} %subtract_convert_fusion) | copy-start | bytes 24580
  97.4 2.9 copy-start.2
  106.9 3.8 copy-start.32
  110.7 10.1 %copy-start.17 = (bf16[2048,64]{0,1:T(8,128)(2,1)}, bf16[2048,64]{0,1:T(8,128)(2,1)S(1)}, u32[]{:S(2)}) copy-start(bf16[2048,64]{0,1:T(8,128)(2,1)S(1)} %get-tuple-element.61) | copy-start | bytes 786436
  110.7 10.1 %copy-start.19 = (bf16[2048,64]{0,1:T(8,128)(2,1)}, bf16[2048,64]{0,1:T(8,128)(2,1)S(1)}, u32[]{:S(2)}) copy-start(bf16[2048,64]{0,1:T(8,128)(2,1)S(1)} %get-tuple-element.62) | copy-start | bytes 786436
  110.7 10.1 %copy-start.26 = (bf16[2048,64]{0,1:T(8,128)(2,1)}, bf16[2048,64]{0,1:T(8,128)(2,1)S(1)}, u32[]{:S(2)}) copy-start(bf16[2048,64]{0,1:T(8,128)(2,1)S(1)} %get-tuple-element.71) | copy-start | bytes 786436
  110.7 10.1 %copy-start.28 = (bf16[2048,64]{0,1:T(8,128)(2,1)}, bf16[2048,64]{0,1:T(8,128)(2,1)S(1)}, u32[]{:S(2)}) copy-start(bf16[2048,64]{0,1:T(8,128)(2,1)S(1)} %get-tuple-element.72) | copy-start | bytes 786436
  120.8 4.5 copy-start.38
  125.2 1.0 copy-start.23
  131.9 75.9 %copy-start.1 = (bf16[1,1,128,2048]{3,2,1,0:T(8,128)(2,1)S(1)}, bf16[1,1,128,2048]{3,2,1,0:T(8,128)(2,1)}, u32[]{:S(2)}) copy-start(bf16[1,1,128,2048]{3,2,1,0:T(8,128)(2,1)} %param.16) | copy-start | bytes 1572868
  132.0 129.9 %all-gather.7.cloned.1.call-start = ((), (), s32[]{:S(2)}) async-start(), calls=%async_computation.5 | async-start | bytes 8912896 | tf_op jit(solution)/shard_map/all_gather | solution.py:120
  209.2 215.4 %copy-start.34 = (f32[128]{0:T(128)}, f32[128]{0:T(128)S(1)}, u32[]{:S(2)}) copy-start(f32[128]{0:T(128)S(1)} %get-tuple-element.77) | copy-start | bytes 1540
  211.2 105.2 %all-gather.13.cloned.1.call-start = ((), (), s32[]{:S(2)}) async-start(), calls=%async_computation.11 | async-start | bytes 8912896 | tf_op jit(solution)/shard_map/all_gather | solution.py:86
  211.8 210.7 %reduce-scatter.9.cloned.1.call-start = ((), (), s32[]{:S(2)}) async-start(), calls=%async_computation.7 | async-start | bytes 8912896 | tf_op jit(solution)/shard_map/reduce_scatter | solution.py:130
  261.9 8.6 %copy-start.14 = (bf16[2048,344]{0,1:T(8,128)(2,1)S(1)}, bf16[2048,344]{0,1:T(8,128)(2,1)}, u32[]{:S(2)}) copy-start(bf16[2048,344]{0,1:T(8,128)(2,1)} %param.22) | copy-start | bytes 4227076
  261.9 8.6 %copy-start.37 = (bf16[2048,2048]{1,0:T(8,128)(2,1)S(1)}, bf16[2048,2048]{1,0:T(8,128)(2,1)}, u32[]{:S(2)}) copy-start(bf16[2048,2048]{1,0:T(8,128)(2,1)} %all-gather.7.cloned.1.call-done) | copy-start | bytes 25165828
  316.4 11.8 %copy-start.15 = (bf16[2048,344]{0,1:T(8,128)(2,1)S(1)}, bf16[2048,344]{0,1:T(8,128)(2,1)}, u32[]{:S(2)}) copy-start(bf16[2048,344]{0,1:T(8,128)(2,1)} %param.22) | copy-start | bytes 4227076
  328.2 8.2 copy-start.9
  328.2 8.2 copy-start.5
  328.2 8.2 copy-start.16
  346.7 75.9 %copy-start.3 = (bf16[128,2048]{1,0:T(8,128)(2,1)S(1)}, bf16[128,2048]{1,0:T(8,128)(2,1)}, u32[]{:S(2)}) copy-start(bf16[128,2048]{1,0:T(8,128)(2,1)} %reduce-scatter.5.cloned.1.call-done) | copy-start | bytes 1572868
  346.7 77.9 %copy-start.8 = (bf16[1,1,128,2048]{3,2,1,0:T(8,128)(2,1)S(1)}, bf16[1,1,128,2048]{3,2,1,0:T(8,128)(2,1)}, u32[]{:S(2)}) copy-start(bf16[1,1,128,2048]{3,2,1,0:T(8,128)(2,1)} %param.27) | copy-start | bytes 1572868
  346.7 130.9 %all-gather.9.cloned.1.call-start = ((), (), s32[]{:S(2)}) async-start(), calls=%async_computation.8 | async-start | bytes 8912896 | tf_op jit(solution)/shard_map/all_gather | solution.py:149
  424.6 11.0 %copy-start.35 = (f32[128]{0:T(128)}, f32[128]{0:T(128)S(1)}, u32[]{:S(2)}) copy-start(f32[128]{0:T(128)S(1)} %broadcast_multiply_fusion.1) | copy-start | bytes 1540
  426.9 251.3 %all-reduce.4.cloned.1.call-start = ((), (), s32[]{:S(2)}) async-start(), calls=%async_computation.12 | async-start | bytes 12648448 | tf_op jit(solution)/shard_map/psum | solution.py:171
  426.9 8.6 %copy-start.6 = (bf16[2048,344]{0,1:T(8,128)(2,1)S(1)}, bf16[2048,344]{0,1:T(8,128)(2,1)}, u32[]{:S(2)}) copy-start(bf16[2048,344]{0,1:T(8,128)(2,1)} %copy-done.5) | copy-start | bytes 4227076
  426.9 16.4 %slice-start.2 = ((s8[8388608]{0:T(1024)(128)(4,1)}), s8[4194304]{0:T(1024)(128)(4,1)S(1)}, s32[]{:S(2)}) async-start(s8[8388608]{0:T(1024)(128)(4,1)} %bitcast.149), calls=%async_computation.15 | async-start | bytes 8388608
  435.5 7.8 copy-start.10
  435.5 7.8 slice-start.3
  435.5 12.0 %slice-start.4 = ((s8[8388608]{0:T(1024)(128)(4,1)}), s8[4194304]{0:T(1024)(128)(4,1)S(1)}, s32[]{:S(2)}) async-start(s8[8388608]{0:T(1024)(128)(4,1)} %bitcast.151), calls=%async_computation.17 | async-start | bytes 8388608
  443.3 4.2 slice-start.5
  443.3 4.2 copy-start.39
  451.7 31.8 %copy-start.33 = (s32[2048]{0:T(1024)S(1)}, s32[2048]{0:T(1024)}, u32[]{:S(2)}) copy-start(s32[2048]{0:T(1024)} %fusion.68) | copy-start | bytes 24580
  483.5 9.7 %copy-start.18 = (bf16[2048,64]{0,1:T(8,128)(2,1)S(1)}, bf16[2048,64]{0,1:T(8,128)(2,1)}, u32[]{:S(2)}) copy-start(bf16[2048,64]{0,1:T(8,128)(2,1)} %copy-done.17) | copy-start | bytes 786436
  483.6 9.7 %copy-start.20 = (bf16[2048,64]{0,1:T(8,128)(2,1)S(1)}, bf16[2048,64]{0,1:T(8,128)(2,1)}, u32[]{:S(2)}) copy-start(bf16[2048,64]{0,1:T(8,128)(2,1)} %copy-done.19) | copy-start | bytes 786436
  493.3 1.4 copy-start.27
  493.3 1.4 copy-start.29
  493.3 13.3 %slice-start.6 = ((s8[8388608]{0:T(1024)(128)(4,1)}), s8[4194304]{0:T(1024)(128)(4,1)S(1)}, s32[]{:S(2)}) async-start(s8[8388608]{0:T(1024)(128)(4,1)} %bitcast.153), calls=%async_computation.19 | async-start | bytes 8388608
  494.7 2.9 copy-start.25
  494.7 2.9 copy-start.31
  494.7 12.0 %slice-start.7 = ((s8[8388608]{0:T(1024)(128)(4,1)}), s8[4194304]{0:T(1024)(128)(4,1)S(1)}, s32[]{:S(2)}) async-start(s8[8388608]{0:T(1024)(128)(4,1)} %bitcast.153), calls=%async_computation.20 | async-start | bytes 8388608
  516.4 10.0 %slice-start = ((s8[8388608]{0:T(1024)(128)(4,1)}), s8[4194304]{0:T(1024)(128)(4,1)S(1)}, s32[]{:S(2)}) async-start(s8[8388608]{0:T(1024)(128)(4,1)} %bitcast.118), calls=%async_computation.13 | async-start | bytes 8388608
  516.6 9.8 %copy-start.11 = (bf16[16,2,64,384]{3,2,1,0:T(8,128)(2,1)}, bf16[16,2,64,384]{3,2,1,0:T(8,128)(2,1)S(1)}, u32[]{:S(2)}) copy-start(bf16[16,2,64,384]{3,2,1,0:T(8,128)(2,1)S(1)} %copy.38) | copy-start | bytes 4718596
  516.6 9.8 %slice-start.1 = ((s8[8388608]{0:T(1024)(128)(4,1)}), s8[4194304]{0:T(1024)(128)(4,1)S(1)}, s32[]{:S(2)}) async-start(s8[8388608]{0:T(1024)(128)(4,1)} %bitcast.118), calls=%async_computation.14 | async-start | bytes 8388608
  528.5 224.4 %reduce-scatter.11.cloned.1.call-start = ((), (), s32[]{:S(2)}) async-start(), calls=%async_computation.9 | async-start | bytes 8912896 | tf_op jit(solution)/shard_map/reduce_scatter | solution.py:165
  538.6 290.4 %reduce-scatter.7.cloned.1.call-start = ((), (), s32[]{:S(2)}) async-start(), calls=%async_computation.6 | async-start | bytes 8912896 | tf_op jit(solution)/shard_map/reduce_scatter | solution.py:136
  546.9 0.7 copy-start.36
  678.2 5.5 copy-start.13
  683.7 1.9 copy-start.12
  685.6 2.1 copy-start.4
  687.7 141.4 %copy-start.7 = (bf16[128,2048]{1,0:T(8,128)(2,1)S(1)}, bf16[128,2048]{1,0:T(8,128)(2,1)}, u32[]{:S(2)}) copy-start(bf16[128,2048]{1,0:T(8,128)(2,1)} %reduce-scatter.9.cloned.1.call-done) | copy-start | bytes 1572868
Sparse Core Ops, SparseCore 0:
  10.9 59.5 all-gather.10
  132.1 75.7 reduce-scatter.4
  211.4 50.4 all-gather.6
  263.4 52.9 all-gather.12
  346.8 75.6 reduce-scatter.8
  427.0 50.5 all-gather.8
  528.6 149.5 all-reduce.3
  680.6 72.2 reduce-scatter.10
  755.3 73.7 reduce-scatter.6

commit v2 on v1

v2 whole, which is shorter than its diff:
```python
import math

import jax
import jax.numpy as jnp
from jax import lax
from jax.experimental import pallas as pl
from jax.experimental.pallas import tpu as pltpu
from jax.sharding import PartitionSpec as P

EPSILON = 1e-05
BF = jnp.bfloat16
F32 = jnp.float32
MESH = pl.DeviceIdType.MESH
VM = pl.BlockSpec(memory_space=pltpu.VMEM)
FF_ROWS = 352
FF_PAD = 384


def dot(a, b):
    return jnp.dot(a, b, preferred_element_type=F32)


def dot_t(a, b):
    return lax.dot_general(a, b, (((1,), (1,)), ((), ())), preferred_element_type=F32)


def t_dot(a, b):
    return lax.dot_general(a, b, (((0,), (0,)), ((), ())), preferred_element_type=F32)


def place():
    c, g = lax.axis_index("ctx"), lax.axis_index("grp")
    return c // 8, (c // 2) % 4, c % 2, g // 4, g % 4


def slot_at(pos, dz, dy, dk=0):
    z, y, k = pos[:3]
    return ((z + dz) % 2) * 8 + ((y + dy) % 4) * 2 + (k + dk) % 2


HOPS = {"p": (0, 1, 0), "m": (0, 3, 0), "z": (1, 0, 0), "c": (0, 0, 1)}
GROUP_HOPS = {"e": (0, 1), "w": (0, 3), "h": (1, 0)}


def neighbour(pos, link):
    if link in HOPS:
        return (lax.axis_index("grp"), slot_at(pos, *HOPS[link]))
    dh, dx = GROUP_HOPS[link]
    return (((pos[3] + dh) % 2) * 4 + (pos[4] + dx) % 4, lax.axis_index("ctx"))


def ctx_peer(d):
    return (lax.axis_index("grp"), (lax.axis_index("ctx") + d) % 16)


def grp_peer(d):
    return ((lax.axis_index("grp") + d) % 8, lax.axis_index("ctx"))


def greet(targets):
    barrier = pltpu.get_barrier_semaphore()
    for t in targets:
        pl.semaphore_signal(barrier, inc=1, device_id=t, device_id_type=MESH)
    pl.semaphore_wait(barrier, len(targets))


class Copies:
    def __init__(self, pos, send, recv):
        self.pos, self.send, self.recv, self.all = pos, send, recv, {}
        self.unsent, self.count = {}, 0

    def start(self, name, target, src, dst):
        n, self.count = self.count, self.count + 1
        if isinstance(target, str):
            target = neighbour(self.pos, target)
        copy = pltpu.make_async_remote_copy(
            src_ref=src,
            dst_ref=dst,
            send_sem=self.send.at[n],
            recv_sem=self.recv.at[n],
            device_id=target,
            device_id_type=MESH,
        )
        copy.start()
        self.all[name] = self.unsent[name] = copy

    def got(self, *names):
        for name in names:
            self.all[name].wait_recv()

    def sent(self, name):
        self.unsent.pop(name).wait_send()

    def finish(self):
        for name in list(self.unsent):
            self.sent(name)


def columns(width, body, step=512):
    def tile(j, _):
        body(pl.ds(pl.multiple_of(j * step, step), step))
        return 0

    lax.fori_loop(0, width // step, tile, 0)


def add_to(dst, *srcs):
    def tile(cols):
        total = dst[:, cols].astype(F32)
        for s in srcs:
            total = total + s[:, cols].astype(F32)
        dst[:, cols] = total.astype(dst.dtype)

    columns(dst.shape[1], tile)


N_GATHER = 35


def gather_steps(net, pos, buf, tag):
    def send(name, link, dz, dy, lo, n):
        ref = buf.at[slot_at(pos, dz, dy), pl.ds(lo, n)]
        net.start(tag + name, link, ref, ref)

    def got(*names):
        net.got(*[tag + name for name in names])

    send("p1", "p", 0, 0, 0, 128)
    send("m1", "m", 0, 0, 0, 128)
    send("z0", "z", 0, 0, 32, 64)
    send("c0", "c", 0, 0, 0, 128)
    send("zb00", "z", 0, 0, 0, 32)
    send("zb01", "z", 0, 0, 96, 32)
    got("c0")
    yield 0, 0
    got("p1")
    send("p2", "p", 0, 3, 0, 64)
    send("zb30", "z", 0, 3, 0, 32)
    send("zb31", "z", 0, 3, 96, 32)
    send("c1", "c", 0, 3, 0, 128)
    got("m1")
    send("m2", "m", 0, 1, 64, 64)
    send("zb10", "z", 0, 1, 0, 32)
    send("zb11", "z", 0, 1, 96, 32)
    send("c2", "c", 0, 1, 0, 128)
    got("z0")
    send("p3", "p", 1, 0, 32, 64)
    send("m3", "m", 1, 0, 32, 64)
    send("c3", "c", 1, 0, 32, 64)
    got("c1")
    yield 0, 3
    got("zb00", "zb01")
    send("c4", "c", 1, 0, 0, 32)
    send("c5", "c", 1, 0, 96, 32)
    got("c2")
    yield 0, 1
    got("p2")
    send("zb20", "z", 0, 2, 0, 32)
    send("c6", "c", 0, 2, 0, 64)
    got("m2")
    send("zb21", "z", 0, 2, 96, 32)
    send("c7", "c", 0, 2, 64, 64)
    got("c3", "c4", "c5")
    yield 1, 0
    got("p3")
    send("p4", "p", 1, 3, 32, 32)
    send("c8", "c", 1, 3, 32, 64)
    got("m3")
    send("m4", "m", 1, 1, 64, 32)
    send("c9", "c", 1, 1, 32, 64)
    got("c6", "c7")
    yield 0, 2
    got("zb30", "zb31")
    send("c10", "c", 1, 3, 0, 32)
    send("c11", "c", 1, 3, 96, 32)
    got("zb10", "zb11")
    send("c12", "c", 1, 1, 0, 32)
    send("c13", "c", 1, 1, 96, 32)
    got("c8", "c10", "c11")
    yield 1, 3
    got("p4")
    send("c14", "c", 1, 2, 32, 32)
    got("m4")
    send("c15", "c", 1, 2, 64, 32)
    got("zb20")
    send("c16", "c", 1, 2, 0, 32)
    got("zb21")
    send("c17", "c", 1, 2, 96, 32)
    got("c9", "c12", "c13")
    yield 1, 1
    got("c14", "c15", "c16", "c17")
    yield 1, 2


N_SCATTER = 25
INBOX_ROWS = 896


def scatter_scratch(w):
    return [
        pltpu.VMEM((16, 128, w), BF),
        pltpu.VMEM((8, 128, w), BF),
        pltpu.VMEM((INBOX_ROWS, w), BF),
    ]


class Scatter:
    def __init__(self, net, pos, part, sib, inbox, tag):
        self.net, self.pos, self.part, self.sib, self.tag = net, pos, part, sib, tag
        self.box, at = {}, 0
        for key, n in (
            [("zb%d%d" % (dy, h), 32) for dy in range(4) for h in range(2)]
            + [("p4", 32), ("m4", 32), ("p3", 64), ("m3", 64), ("p2", 64), ("m2", 64)]
            + [("p1", 128), ("m1", 128), ("z0", 64)]
        ):
            self.box[key] = inbox.at[pl.ds(at, n)]
            at += n

    def mine(self, dz, dy, lo=0, n=128):
        return self.part.at[slot_at(self.pos, dz, dy), pl.ds(lo, n)]

    def swap(self, dz, dy):
        src = self.part.at[slot_at(self.pos, dz, dy, 1)]
        self.net.start(self.tag + "c%d%d" % (dz, dy), "c", src, self.sib.at[dz * 4 + dy])

    def joined(self, dz, dy):
        self.got("c%d%d" % (dz, dy))
        add_to(self.mine(dz, dy), self.sib.at[dz * 4 + dy])

    def got(self, *names):
        self.net.got(*[self.tag + name for name in names])

    def put(self, name, link, src):
        self.net.start(self.tag + name, link, src, self.box[name])

    def put_zb(self, dy):
        for h, lo in ((0, 0), (1, 96)):
            self.put("zb%d%d" % (dy, h), "z", self.mine(1, dy, lo, 32))

    def take(self, name, dz, dy, lo, n):
        self.got(name)
        add_to(self.mine(dz, dy, lo, n), self.box[name])

    def take_zb(self, dy):
        self.take("zb%d0" % dy, 0, dy, 0, 32)
        self.take("zb%d1" % dy, 0, dy, 96, 32)

    def steps(self):
        self.joined(1, 2)
        self.put_zb(2)
        self.put("p4", "p", self.mine(1, 2, 64, 32))
        self.put("m4", "m", self.mine(1, 2, 32, 32))
        self.joined(1, 1)
        self.put_zb(1)
        self.joined(1, 3)
        self.put_zb(3)
        self.joined(1, 0)
        self.put_zb(0)
        self.joined(0, 2)
        yield
        self.take("p4", 1, 1, 64, 32)
        self.put("p3", "p", self.mine(1, 1, 32, 64))
        self.take("m4", 1, 3, 32, 32)
        self.put("m3", "m", self.mine(1, 3, 32, 64))
        self.joined(0, 1)
        self.joined(0, 3)
        yield
        self.take_zb(2)
        self.put("p2", "p", self.mine(0, 2, 64, 64))
        self.put("m2", "m", self.mine(0, 2, 0, 64))
        self.joined(0, 0)
        yield
        self.take("p3", 1, 0, 32, 64)
        self.take("m3", 1, 0, 32, 64)
        self.put("z0", "z", self.mine(1, 0, 32, 64))
        yield
        self.take_zb(1)
        self.take("p2", 0, 1, 64, 64)
        self.put("p1", "p", self.mine(0, 1))
        self.take_zb(3)
        self.take("m2", 0, 3, 0, 64)
        self.put("m1", "m", self.mine(0, 3))
        yield
        self.take_zb(0)
        self.take("z0", 0, 0, 32, 64)
        yield
        self.got("p1", "m1")

    def total(self, cols):
        sums = self.mine(0, 0)[:, cols].astype(F32)
        return sums + self.box["p1"][:, cols].astype(F32) + self.box["m1"][:, cols].astype(F32)


SCATTER_ORDER = [(1, 2), (1, 1), (1, 3), (1, 0), (0, 2), (0, 1), (0, 3), (0, 0)]


def pair_rows(pos, dz, dy):
    first = slot_at(pos, dz, dy) // 2
    return first * 2, pl.ds(pl.multiple_of(first * 256, 256), 256)


def product(pos, part, dz, dy, *factors):
    slot, rows = pair_rows(pos, dz, dy)

    def tile(cols):
        total = None
        for a, b in factors:
            term = dot(a[rows, :], b[:, cols])
            total = term if total is None else total + term
        part[slot, :, cols] = total[:128].astype(BF)
        part[slot + 1, :, cols] = total[128:].astype(BF)

    columns(part.shape[2], tile)


def quarter(pos, d, half=None):
    start = ((pos[4] + d) % 4) * 512
    if half is None:
        return pl.ds(pl.multiple_of(start, 512), 512)
    return pl.ds(pl.multiple_of(start + half * 256, 256), 256)


def ring_sum_scratch(rows):
    return [
        pltpu.VMEM((2, rows, 256), BF),
        pltpu.VMEM((3, rows, 512), BF),
    ]


N_RING_SUM = 5


def ring_sum_steps(net, pos, terms, chunk, far, near, tag):
    rows = terms.shape[0]
    net.start(tag + "e2", "e", terms.at[:, quarter(pos, 2, 0)], far.at[0])
    net.start(tag + "w2", "w", terms.at[:, quarter(pos, 2, 1)], far.at[1])
    yield
    for name, d, half in (("e", 1, 0), ("w", 3, 1)):
        net.got(tag + name + "2")

        def fold(i, _, d=d, half=half):
            r = pl.ds(pl.multiple_of(i * 32, 32), 32)
            cols = quarter(pos, d, half)
            terms[r, cols] = (terms[r, cols].astype(F32) + far[half, r, :].astype(F32)).astype(BF)
            return 0

        lax.fori_loop(0, rows // 32, fold, 0)
        net.start(tag + name + "1", name, terms.at[:, quarter(pos, d)], near.at[half])
    yield
    net.got(tag + "e1", tag + "w1")

    def join(i, _):
        r = pl.ds(pl.multiple_of(i * 32, 32), 32)
        total = terms[r, quarter(pos, 0)].astype(F32) + near[0, r, :].astype(F32)
        chunk[r, :] = (total + near[1, r, :].astype(F32)).astype(BF)
        return 0

    lax.fori_loop(0, rows // 32, join, 0)
    net.start(tag + "h", "h", chunk, near.at[2])
    yield
    net.got(tag + "h")
    net.sent(tag + "h")

    def across(i, _):
        r = pl.ds(pl.multiple_of(i * 32, 32), 32)
        chunk[r, :] = (chunk[r, :].astype(F32) + near[2, r, :].astype(F32)).astype(BF)
        return 0

    lax.fori_loop(0, rows // 32, across, 0)


N_RING_SHARE = 4


def ring_share_steps(net, pos, chunk, whole, tag):
    mine = quarter(pos, 0)
    net.start(tag + "e1", "e", chunk, whole.at[:, mine])
    net.start(tag + "w1", "w", chunk, whole.at[:, mine])
    whole[:, mine] = chunk[...]
    yield
    net.got(tag + "e1")
    ref = whole.at[:, quarter(pos, 3, 0)]
    net.start(tag + "e2", "e", ref, ref)
    net.got(tag + "w1")
    ref = whole.at[:, quarter(pos, 1, 1)]
    net.start(tag + "w2", "w", ref, ref)
    yield
    net.got(tag + "e2", tag + "w2")


def run(*steps):
    steps = list(steps)
    while steps:
        for s in list(steps):
            try:
                next(s)
            except StopIteration:
                steps.remove(s)


def sems(n):
    return [pltpu.SemaphoreType.DMA((n,)), pltpu.SemaphoreType.DMA((n,))]


def call(kernel, name, cid, outs, scratch, args, mib=60):
    return pl.pallas_call(
        kernel,
        out_shape=[jax.ShapeDtypeStruct(s, d) for s, d in outs],
        in_specs=[VM] * len(args),
        out_specs=[VM] * len(outs),
        scratch_shapes=scratch,
        compiler_params=pltpu.CompilerParams(
            collective_id=cid, has_side_effects=True, vmem_limit_bytes=mib * 2**20
        ),
        name=name,
    )(*args)


def norm_factor(u):
    return lax.rsqrt(jnp.mean(u * u, -1, keepdims=True) + EPSILON)


def acts_kernel(x, gains, out, gains_out, send, recv):
    pos = place()
    net = Copies(pos, send, recv)
    me = lax.axis_index("ctx")
    out[me] = x[...]
    gains_out[me] = gains[...]
    greet([ctx_peer(d) for d in range(1, 16)])
    for d in range(1, 16):
        ref = gains_out.at[me]
        net.start("g%d" % d, ctx_peer(d), ref, ref)
    for _ in gather_steps(net, pos, out, "x"):
        pass
    net.got(*["g%d" % d for d in range(1, 16)])
    net.finish()


def gather_acts(x, gains, cid):
    return call(
        acts_kernel,
        "gather_acts",
        cid,
        [((16, 128, 2048), BF), ((16, 16, 128), BF)],
        sems(N_GATHER + 15),
        [x, gains],
    )


def branch_kernel(a, w_out, cot, branch, cot_all, part, sib, inbox, send, recv):
    pos = place()
    net = Copies(pos, send, recv)
    cot_all[lax.axis_index("ctx")] = cot[...]
    greet([neighbour(pos, l) for l in "pmzc"])
    sums = Scatter(net, pos, part, sib, inbox, "s")
    for dz, dy in SCATTER_ORDER:
        product(pos, part, dz, dy, (a, w_out))
        sums.swap(dz, dy)
    run(sums.steps(), gather_steps(net, pos, cot_all, "x"))

    def last(cols):
        branch[:, cols] = sums.total(cols)

    columns(2048, last)
    net.finish()


def attention_branch(attended, w_out, cot, cid):
    return call(
        branch_kernel,
        "attention_branch",
        cid,
        [((128, 2048), F32), ((16, 128, 2048), BF)],
        scatter_scratch(2048) + sems(N_SCATTER + N_GATHER),
        [attended, w_out, cot],
    )


def mlp_kernel(
    acts,
    branch,
    gain,
    cot,
    w,
    residual,
    d_res,
    gain_part,
    hidden,
    grads,
    buf,
    low_t,
    part,
    sib,
    inbox,
    send,
    recv,
):
    pos = place()
    net = Copies(pos, send, recv)
    me = lax.axis_index("ctx")

    def normalise(i, _):
        r = pl.ds(pl.multiple_of(i * 32, 32), 32)
        u = acts[r, :].astype(F32) + branch[r, :]
        residual[r, :] = u
        buf[me, r, :] = (u * norm_factor(u) * gain[...]).astype(BF)
        return 0

    lax.fori_loop(0, 4, normalise, 0)
    greet([neighbour(pos, l) for l in "pmzc"])
    sums = Scatter(net, pos, part, sib, inbox, "s")
    for dz, dy in gather_steps(net, pos, buf, "x"):
        slot, rows = pair_rows(pos, dz, dy)
        n2 = buf[pl.ds(slot, 2)].reshape(256, 2048)
        ct = cot[pl.ds(slot, 2)].reshape(256, 2048)
        gate = dot_t(n2, w[0])
        up = dot_t(n2, w[1])
        d_hidden = dot_t(ct, w[2])
        sig = jax.nn.sigmoid(gate)
        silu = gate * sig
        h = (silu * up).astype(BF)
        dg = (d_hidden * up * sig * (1.0 + gate * (1.0 - sig))).astype(BF)
        du = (d_hidden * silu).astype(BF)
        hidden[rows, :] = h
        low_t[0, :, rows] = dg.T
        low_t[1, :, rows] = du.T
        low_t[2, :, rows] = h.T

        def tile(cols):
            t = dot(dg, w[0, :, cols]) + dot(du, w[1, :, cols])
            part[slot, :, cols] = t[:128].astype(BF)
            part[slot + 1, :, cols] = t[128:].astype(BF)

        columns(2048, tile)
        sums.swap(dz, dy)

    def weight_grads():
        for i, other in ((0, buf), (1, buf), (2, cot)):

            def tile(cols, i=i, other=other):
                rhs = other[:, :, cols].reshape(2048, 256)
                g = dot(low_t[i], rhs)
                grads[i * FF_ROWS : (i + 1) * FF_ROWS, cols] = g[:FF_ROWS].astype(BF)

            for half in range(2):

                def part_tile(j, _, half=half, tile=tile):
                    tile(pl.ds(pl.multiple_of(half * 1024 + j * 256, 256), 256))
                    return 0

                lax.fori_loop(0, 4, part_tile, 0)
                yield

    run(sums.steps(), weight_grads())

    gain_part[...] = jnp.zeros_like(gain_part)

    def back(i, _):
        r = pl.ds(pl.multiple_of(i * 32, 32), 32)
        slot = me
        e = (
            part[slot, r, :].astype(F32)
            + sums.box["p1"][r, :].astype(F32)
            + sums.box["m1"][r, :].astype(F32)
        )
        u = residual[r, :]
        f = norm_factor(u)
        scaled = e * gain[...]
        grad = f * scaled - u * f * f * f * jnp.mean(scaled * u, -1, keepdims=True)
        d_res[r, :] = cot[slot, r, :].astype(F32) + grad
        gain_part[...] += jnp.sum(e * u * f, 0, keepdims=True)
        return 0

    lax.fori_loop(0, 4, back, 0)
    net.finish()


def mlp(acts, branch, gain, cot_all, w, cid):
    return call(
        mlp_kernel,
        "mlp",
        cid,
        [
            ((128, 2048), F32),
            ((128, 2048), F32),
            ((1, 2048), F32),
            ((2048, FF_PAD), BF),
            ((3 * FF_ROWS, 2048), BF),
        ],
        [pltpu.VMEM((16, 128, 2048), BF), pltpu.VMEM((3, FF_PAD, 2048), BF)]
        + scatter_scratch(2048)
        + sems(N_SCATTER + N_GATHER),
        [acts, branch, gain, cot_all, w],
    )


def d_branch_kernel(
    d_res, attended, w_out, ff, d_att, grad_out, chunk, buf, total, far, near, send, recv
):
    pos = place()
    net = Copies(pos, send, recv)
    buf[lax.axis_index("ctx")] = d_res[...].astype(BF)
    total[...] = jnp.zeros_like(total)
    greet([neighbour(pos, l) for l in "pmzcewh"])

    def rows_in():
        for dz, dy in gather_steps(net, pos, buf, "x"):
            slot, rows = pair_rows(pos, dz, dy)
            d = buf[pl.ds(slot, 2)].reshape(256, 2048)
            d_att[rows, :] = dot_t(d, w_out[...]).astype(BF)
            total[...] += t_dot(attended[rows, :], d)
            yield

    run(ring_sum_steps(net, pos, ff, chunk, far, near, "r"), rows_in())
    grad_out[...] = total[...].astype(BF)
    net.finish()


def d_branch(d_res, attended, w_out, ff, cid):
    return call(
        d_branch_kernel,
        "d_branch",
        cid,
        [((2048, 128), BF), ((128, 2048), BF), ((3 * FF_ROWS, 512), BF)],
        [pltpu.VMEM((16, 128, 2048), BF), pltpu.VMEM((128, 2048), F32)]
        + ring_sum_scratch(3 * FF_ROWS)
        + sems(N_GATHER + N_RING_SUM),
        [d_res, attended, w_out, ff],
    )


def mixed_kernel(hidden, w, residual, chunk, mixed, whole, part, sib, inbox, send, recv):
    pos = place()
    net = Copies(pos, send, recv)
    greet([neighbour(pos, l) for l in "pmzcew"])
    sums = Scatter(net, pos, part, sib, inbox, "s")
    share = ring_share_steps(net, pos, chunk, whole, "r")
    next(share)
    for dz, dy in SCATTER_ORDER:
        product(pos, part, dz, dy, (hidden, w))
        sums.swap(dz, dy)
    run(sums.steps(), share)

    def last(cols):
        mixed[:, cols] = (residual[:, cols] + sums.total(cols)).astype(BF)

    columns(2048, last)
    net.finish()


def mlp_out(hidden, w_down, residual, chunk, cid):
    return call(
        mixed_kernel,
        "mlp_out",
        cid,
        [((128, 2048), BF), ((3 * FF_ROWS, 2048), BF)],
        scatter_scratch(2048) + sems(N_SCATTER + N_RING_SHARE),
        [hidden, w_down, residual, chunk],
    )


def d_normed_kernel(
    d_qkv,
    w,
    normed,
    acts,
    d_res,
    gain,
    grad_out,
    gain_two_part,
    acts_grad,
    whole,
    gains,
    part,
    sib,
    inbox,
    terms,
    chunk,
    far,
    near,
    low_t,
    gain_terms,
    gain_box,
    gain_sum,
    gain_wide,
    send,
    recv,
):
    pos = place()
    net = Copies(pos, send, recv)
    me = lax.axis_index("ctx")
    greet([ctx_peer(d) for d in range(1, 16)] + [grp_peer(d) for d in range(1, 8)])
    sums = Scatter(net, pos, part, sib, inbox, "s")
    low_t[...] = d_qkv[...].T
    terms[pl.ds(384, 128), :] = grad_out[...]
    gain_terms[...] = jnp.zeros_like(gain_terms)
    for j in range(16):
        cols = slice(j * 128, (j + 1) * 128)
        gain_terms[j, 0:1, :] = gain_two_part[:, cols]

    def weight_grads(d):
        for half in range(2):
            cols = quarter(pos, d, half)
            g = dot(low_t[...], normed[:, :, cols].reshape(2048, 256))
            terms[pl.ds(0, 384), cols] = g.astype(BF)
            by_column = jnp.sum(g * w[:, cols].astype(F32), 0, keepdims=True) / gain[:, cols]
            first = ((pos[4] + d) % 4) * 4 + half * 2
            gain_terms[first, 1:2, :] = by_column[:, :128]
            gain_terms[first + 1, 1:2, :] = by_column[:, 128:]

    def products(pairs):
        for dz, dy in pairs:
            product(pos, part, dz, dy, (d_qkv, w))
            sums.swap(dz, dy)

    weight_grads(2)
    ring = ring_sum_steps(net, pos, terms, chunk, far, near, "r")
    next(ring)
    products(SCATTER_ORDER[:4])
    back = sums.steps()
    weight_grads(1)
    products(SCATTER_ORDER[4:])
    next(back)
    weight_grads(3)
    weight_grads(0)
    next(back)
    next(ring)

    for d in range(1, 16):
        net.start("g%d" % d, ctx_peer(d), gain_terms.at[(me + d) % 16], gain_box.at[d])
    gain_box[0] = gain_terms[me]
    next(back)
    next(ring)
    net.got(*["g%d" % d for d in range(1, 16)])
    gain_sum[...] = jnp.sum(gain_box[...], 0)
    for d in range(1, 8):
        net.start("h%d" % d, grp_peer(d), gain_sum, gain_wide.at[d])
    gain_wide[0] = gain_sum[...]
    run(back, chain(ring, ring_share_steps(net, pos, chunk, whole, "q")))
    net.got(*["h%d" % d for d in range(1, 8)])
    gains[...] = jnp.sum(gain_wide[...], 0)

    def finish(i, _):
        r = pl.ds(pl.multiple_of(i * 32, 32), 32)
        e = (
            part[me, r, :].astype(F32)
            + sums.box["p1"][r, :].astype(F32)
            + sums.box["m1"][r, :].astype(F32)
        )
        u = acts[r, :].astype(F32)
        f = norm_factor(u)
        scaled = e * gain[...]
        grad = f * scaled - u * f * f * f * jnp.mean(scaled * u, -1, keepdims=True)
        acts_grad[r, :] = d_res[r, :] + grad
        return 0

    lax.fori_loop(0, 4, finish, 0)
    net.finish()


def chain(*steps):
    for s in steps:
        yield from s


def d_normed(d_qkv, w, normed, acts, d_res, gain, grad_out, gain_two_part, cid):
    return call(
        d_normed_kernel,
        "d_normed",
        cid,
        [((128, 2048), F32), ((512, 2048), BF), ((8, 128), F32)],
        scatter_scratch(2048)
        + [pltpu.VMEM((512, 2048), BF), pltpu.VMEM((512, 512), BF)]
        + ring_sum_scratch(512)
        + [
            pltpu.VMEM((384, 2048), BF),
            pltpu.VMEM((16, 8, 128), F32),
            pltpu.VMEM((16, 8, 128), F32),
            pltpu.VMEM((8, 128), F32),
            pltpu.VMEM((8, 8, 128), F32),
        ]
        + sems(N_SCATTER + N_RING_SUM + N_RING_SHARE + 22),
        [d_qkv, w, normed, acts, d_res, gain, grad_out, gain_two_part],
    )


def rotary(offsets, head_size):
    frequency = 10000.0 ** (-(jnp.arange(head_size // 2).astype(F32) * 2.0 / head_size))
    angles = offsets.astype(F32)[:, None] * frequency[None, :]
    return jnp.cos(angles), jnp.sin(angles)


def rotate(tensor, cosine, sine):
    middle = tensor.shape[-1] // 2
    a, b = tensor[..., :middle], tensor[..., middle:]
    return jnp.concatenate([a * cosine - b * sine, b * cosine + a * sine], -1)


def to_rows(packed, n_ctx):
    rest = packed.shape[1:]
    v = packed.reshape((n_ctx, 2, -1) + rest)
    return jnp.concatenate([v[:, 0], v[::-1, 1]], 0).reshape((-1,) + rest)


def to_packed(rows, n_ctx):
    rest = rows.shape[1:]
    v = rows.reshape((2 * n_ctx, -1) + rest)
    return jnp.stack([v[:n_ctx], v[n_ctx:][::-1]], 1).reshape((-1,) + rest)


def local(
    acts,
    doc_lengths,
    w_query,
    w_key,
    w_value,
    w_out,
    w_gate,
    w_up,
    w_down,
    gain_attn,
    gain_mlp,
    cotangent,
):
    tok = acts.shape[2]
    width = acts.shape[3]
    n_ctx = lax.axis_size("ctx")
    row = n_ctx * tok
    head = w_query.shape[1]
    ff = w_gate.shape[1]
    scale = 1.0 / math.sqrt(head)

    acts_rows = acts.reshape(tok, width)
    cot_low = cotangent.reshape(tok, width)
    gains = jnp.zeros((16, head), BF).at[0].set(gain_attn).at[1].set(gain_mlp)
    acts_all, gains_all = gather_acts(acts_rows, gains, 0)
    gain_first = gains_all[:, 0].reshape(1, width).astype(F32)
    gain_second = gains_all[:, 1].reshape(1, width).astype(F32)

    tokens_all = acts_all.reshape(row, width).astype(F32)
    normed = (tokens_all * norm_factor(tokens_all) * gain_first).astype(BF)
    w_qkv = jnp.concatenate([w_query, w_key, w_value], 1)
    qkv = to_rows(dot(normed, w_qkv), n_ctx)

    lengths = doc_lengths.reshape(2)
    pos = jnp.arange(row, dtype=jnp.int32)
    doc = (pos >= lengths[0]).astype(jnp.int32)
    own = jnp.where(doc == 0, lengths[0], lengths[1])
    bias = -jnp.log(own.astype(F32))
    cosine, sine = rotary(pos - doc * lengths[0], head)
    visible = ((doc[None, :] == doc[:, None]) & (pos[None, :] <= pos[:, None])).astype(F32)

    q_rot = rotate(qkv[:, :head], cosine, sine).astype(BF)
    k_rot = rotate(qkv[:, head : 2 * head], cosine, sine).astype(BF)
    v_low = qkv[:, 2 * head :].astype(BF)
    score = dot_t(q_rot, k_rot) * scale + bias[:, None]
    sig = jax.nn.sigmoid(score)
    prob = (sig * visible).astype(BF)
    attended = to_packed(dot(prob, v_low).astype(BF), n_ctx)
    branch, cot_all = attention_branch(attended, w_out, cot_low, 1)

    def padded(w):
        return jnp.pad(w, ((0, FF_PAD - ff), (0, 0)))

    ff_w = jnp.stack([padded(w_gate.T), padded(w_up.T), padded(w_down)])
    residual, d_res, gain_two_part, hidden, ff_grads = mlp(
        acts_rows, branch, gain_second, cot_all, ff_w, 2
    )
    d_att, grad_out, chunk = d_branch(d_res, attended, w_out, ff_grads, 3)
    mixed, ff_sums = mlp_out(hidden, ff_w[2], residual, chunk, 4)

    d_attended = to_rows(d_att, n_ctx)
    d_prob = dot_t(d_attended, v_low)
    d_score = (d_prob * sig * (1.0 - sig) * visible).astype(BF)
    d_qrot = dot(d_score, k_rot) * scale
    d_krot = t_dot(d_score, q_rot) * scale
    d_vsum = t_dot(prob, d_attended)
    d_qkv = to_packed(
        jnp.concatenate(
            [rotate(d_qrot, cosine, -sine), rotate(d_krot, cosine, -sine), d_vsum], 1
        ).astype(BF),
        n_ctx,
    )
    acts_grad, attn_sums, gain_grads = d_normed(
        d_qkv,
        w_qkv.T,
        normed.reshape(n_ctx, tok, width),
        acts_rows,
        d_res,
        gain_first,
        grad_out,
        gain_two_part,
        5,
    )

    def ff_grad(i):
        return ff_sums[i * FF_ROWS : i * FF_ROWS + ff].astype(F32)

    def attn_grad(i):
        return attn_sums[i * head : (i + 1) * head].astype(F32)

    return (
        mixed.reshape(1, 1, tok, width),
        acts_grad.reshape(1, 1, tok, width),
        attn_grad(0).T,
        attn_grad(1).T,
        attn_grad(2).T,
        attn_grad(3),
        ff_grad(0).T,
        ff_grad(1).T,
        ff_grad(2),
        gain_grads[1],
        gain_grads[0],
    )


def solution(mesh):
    row = P("grp", "ctx", None, None)
    col = P(None, "ctx")
    dep = P("ctx", None)
    vec = P("ctx")
    in_specs = (row, P("grp", None), col, col, col, dep, col, col, dep, vec, vec, row)
    out_specs = (row, row, col, col, col, dep, col, col, dep, vec, vec)
    return jax.shard_map(local, mesh=mesh, in_specs=in_specs, out_specs=out_specs, check_vma=False)
```

time: 844 us -> 564 us (0.67)
  waiting for transfers between devices: 520 us -> 0 us
  Pallas kernels: 0 us -> 439 us
  matrix products: 139 us -> 34.7 us
  blocking collectives: 66.8 us -> 0 us
  other arithmetic: 68.7 us -> 45 us
  between operations: 15 us -> 1.55 us
    pallas_call x0 -> x6, Pallas kernels: none -> 439 us  [call(): pl.pallas_call(kernel, out_shape=[jax.ShapeDtypeStruct(s, d) for s, d in...]
    reduce_scatter x4 -> x0, waiting for transfers between devices: 221 us -> none  [the longest x1 75.8 us: local(): lax.psum_scatter(dot(attended, w_out).astype(BF), 'ctx', scatter_dimensio...]
    all_gather x4 -> x0, waiting for transfers between devices: 168 us -> none  [the longest x1 51.6 us: local(): lax.all_gather(jnp.concatenate([acts_rows, gains], 0), 'ctx', axis=0, til...]
    psum x1 -> x0, waiting for transfers between devices: 130 us -> none  [local(): attn_totals = lax.psum((grad_qkv.astype(BF), grad_out.astype(BF)), 'grp')]
    psum x1 -> x0, blocking collectives: 66.8 us -> none  [local(): lax.psum(jnp.stack([gain_one_part, gain_two_part]), ('grp', 'ctx'))]
    dot_general x7 -> x2, matrix products: 65.5 us -> 19.8 us  [dot_t(): lax.dot_general(a, b, (((1,), (1,)), ((), ())), preferred_element_type=F32)]
    dot_general x7 -> x3, matrix products: 43.3 us -> 12.2 us  [dot(): return jnp.dot(a, b, preferred_element_type=F32)]
    dot_general x7 -> x2, matrix products: 30.6 us -> 2.67 us  [t_dot(): lax.dot_general(a, b, (((0,), (0,)), ((), ())), preferred_element_type=F32)]
  transfers between devices with their start and end apart: 9 -> 0, of which waited for: 9 -> 0; matrix products, arithmetic and copies ran while one was open for 9% -> 0% of each run, Pallas kernels for 0% -> 0%
where the time goes in v2:
time: 564 us; the launch traced here: 553 us
  Pallas kernels  439 us (78%)
  other arithmetic  45 us (8%)
  matrix products  34.7 us (6%)
  local copies, waits for them, and re-layouts  33.4 us (6%)
    pallas_call x6, Pallas kernels, call(): pl.pallas_call(kernel, out_shape=[jax.ShapeDtypeStruct(s, d) for s, d in...  439 us
    unnamed x34, local copies, waits for them, and re-layouts  21.3 us
    dot_general x2, matrix products, dot_t(): lax.dot_general(a, b, (((1,), (1,)), ((), ())), preferred_element_type=F32)  19.8 us
    dot_general x3, matrix products, dot(): return jnp.dot(a, b, preferred_element_type=F32)  12.2 us

profile of v2, /device:TPU:0, one launch (start us, length us, event | category | flops | bytes accessed | tf_op | source)
XLA Modules:
  0.0 553.4 jit_solution(12835125691065658399)
XLA Ops:
  0.7 1.3 fusion.54
  2.0 0.7 scatter.6
  2.6 0.7 scatter.9.gains
  3.3 1.3 log_negate_fusion
  4.6 0.7 subtract_convert_fusion
  5.3 0.7 fusion.44
  5.9 0.0 copy-start.1
  5.9 1.4 copy.39
  7.3 1.2 copy.40
  8.6 1.2 copy.41
  9.8 0.0 copy-start.2
  9.8 1.3 fusion.23.w
  11.2 0.6 copy-done.2
  11.7 0.4 pad_bitcast_fusion
  12.1 1.0 copy-done
  13.1 1.3 fusion.52
  14.4 2.4 pad_maximum_fusion.w
  16.8 42.9 %gather_acts.1 = (bf16[16,128,2048]{2,1,0:T(8,128)(2,1)}, bf16[16,16,128]{2,1,0:T(8,128)(2,1)}) custom-call(bf16[128,2048]{1,0:T(8,128)(2,1)} %bitcast.83, bf16[16,128]{1,0:T(8,128)(2,1)} %copy-done.7), custom_call_target="tpu_custom_call" | custom-call | tf_op jit(solution)/shard_map/gather_acts/pallas_call | solution.py:406
  59.7 1.4 fusion.49
  61.1 5.1 multiply_reduce_fusion
  66.2 0.1 rsqrt.13
  66.3 7.0 %fusion.1 = f32[16,2,64,384]{3,2,1,0:T(8,128)S(1)} fusion(f32[2048]{0:T(1024)S(1)} %bitcast.98, f32[16,2,64]{2,1,0:T(2,128)S(1)} %rsqrt.13, bf16[2048,128]{0,1:T(8,128)(2,1)S(1)} %copy.41, bf16[2048,128]{0,1:T(8,128)(2,1)S(1)} %copy.40, bf16[2048,128]{0,1:T(8,128)(2,1)S(1)} %copy.39, bf16[16,2,64,2048]{3,2,1,0:T(8,128)(2,1)} %bitcast.76), kind=kOutput, calls=%fused_computation.8 | convolution fusion | flops 3242721280 | bytes 13123584 | tf_op jit(solution)/shard_map/dot_general | solution.py:20
  73.3 8.6 %multiply_convert_fusion.normed = bf16[16,128,2048]{2,1,0:T(8,128)(2,1)} fusion(bf16[16,128,2048]{2,1,0:T(8,128)(2,1)} %get-tuple-element.52, f32[2048]{0:T(1024)S(1)} %bitcast.99, f32[16,128]{1,0:T(8,128)S(1)} %add_rsqrt_fusion), kind=kLoop, calls=%fused_computation | loop fusion | flops 16777216 | bytes 16793600 | tf_op jit(solution)/shard_map/convert_element_type | solution.py:841
  82.0 0.3 slice_bitcast_fusion
  82.2 0.1 reverse_bitcast_fusion
  82.3 0.3 pad_maximum_fusion.1
  82.7 2.6 fusion.50
  85.3 2.3 copy.60
  87.6 2.3 copy.61
  90.0 2.3 copy.59
  92.3 2.3 copy.62
  94.6 4.0 fusion.33
  98.6 10.4 %select_convert_fusion.1 = (bf16[2048,2048]{1,0:T(8,128)(2,1)S(1)}, f32[2048,2048]{1,0:T(8,128)}) fusion(s32[2048]{0:T(1024)S(1)} %fusion.44, f32[2048]{0:T(1024)S(1)} %log_negate_fusion, bf16[2048,64]{0,1:T(8,128)(2,1)S(1)} %get-tuple-element.119, bf16[2048,64]{0,1:T(8,128)(2,1)S(1)} %get-tuple-element.120, bf16[2048,64]{0,1:T(8,128)(2,1)S(1)} %get-tuple-element.109, ...), kind=kOutput, calls=%fused_computation.2 | convolution fusion | flops 1113587712 | bytes 26230784 | tf_op jit(solution)/shard_map/dot_general | solution.py:24
  109.1 2.4 convolution_convert_fusion.1
  111.4 0.9 copy-done.8
  112.3 0.8 pad_maximum_fusion.7
  113.2 74.4 %attention_branch.1 = (f32[128,2048]{1,0:T(8,128)}, bf16[16,128,2048]{2,1,0:T(8,128)(2,1)}) custom-call(bf16[2048,128]{1,0:T(8,128)(2,1)} %bitcast.81, bf16[128,2048]{1,0:T(8,128)(2,1)} %w_out.3, bf16[128,2048]{1,0:T(8,128)(2,1)} %bitcast.93), custom_call_target="tpu_custom_call" | custom-call | tf_op jit(solution)/shard_map/attention_branch/pallas_call | solution.py:406
  187.6 92.0 %mlp.1 = (f32[128,2048]{1,0:T(8,128)}, f32[128,2048]{1,0:T(8,128)}, f32[1,2048]{1,0:T(1,128)}, bf16[2048,384]{1,0:T(8,128)(2,1)}, bf16[1056,2048]{1,0:T(8,128)(2,1)}) custom-call(bf16[128,2048]{1,0:T(8,128)(2,1)} %bitcast.84, f32[128,2048]{1,0:T(8,128)} %get-tuple-element.54.branch, f32[1,2048]{1,0:T(1,128)} %get-tuple-element.117.gain, ...), custom_call_target="tpu_custom_call" | custom-call | tf_op jit(solution)/shard_map/mlp/pallas_call | solution.py:406
  279.6 81.0 %d_branch.1 = (bf16[2048,128]{1,0:T(8,128)(2,1)}, bf16[128,2048]{1,0:T(8,128)(2,1)}, bf16[1056,512]{1,0:T(8,128)(2,1)}) custom-call(f32[128,2048]{1,0:T(8,128)} %get-tuple-element.58.d_res, bf16[2048,128]{1,0:T(8,128)(2,1)} %bitcast.82, bf16[128,2048]{1,0:T(8,128)(2,1)} %w_out.3, bf16[1056,2048]{1,0:T(8,128)(2,1)} %get-tuple-element.59.ff), custom_call_target="tpu_custom_call" | custom-call | tf_op jit(solution)/shard_map/d_branch/pallas_call | solution.py:406
  360.5 67.7 %mlp_out.1 = (bf16[128,2048]{1,0:T(8,128)(2,1)}, bf16[1056,2048]{1,0:T(8,128)(2,1)}) custom-call(bf16[2048,384]{1,0:T(8,128)(2,1)} %get-tuple-element.56.hidden, bf16[384,2048]{1,0:T(8,128)(2,1)} %get-tuple-element.106.w, f32[128,2048]{1,0:T(8,128)} %get-tuple-element.57.residual, bf16[1056,512]{1,0:T(8,128)(2,1)} %get-tuple-element.60.chunk), custom_call_target="tpu_custom_call" | custom-call | tf_op jit(solution)/shard_map/mlp_out/pallas_call | solution.py:406
  428.3 1.1 slice_bitcast_fusion.1
  429.4 9.4 %select_convert_fusion = bf16[2048,2048]{1,0:T(8,128)(2,1)S(1)} fusion(f32[2048,2048]{1,0:T(8,128)} %get-tuple-element.126, bf16[2048,128]{1,0:T(8,128)(2,1)S(1)} %bitcast.95, s32[2048]{0:T(1024)S(1)} %fusion.44, f32[2048,384]{1,0:T(8,128)S(1)} %bitcast.79), kind=kOutput, calls=%fused_computation.1 | convolution fusion | flops 1107296256 | bytes 26230784 | tf_op jit(solution)/shard_map/dot_general | solution.py:24
  438.8 1.3 convolution_multiply_fusion
  440.2 2.9 convolution_multiply_fusion.1
  443.1 2.3 fusion.43
  445.3 2.3 fusion.42
  447.6 2.3 fusion.41
  449.9 2.3 fusion.40
  452.2 1.3 fusion.4
  453.5 0.1 fusion.51
  453.7 0.4 copy.50
  454.0 0.4 copy.51
  454.4 0.1 reverse_bitcast_fusion.1
  454.5 0.2 pad_maximum_fusion.3
  454.7 1.3 copy.52
  456.0 80.9 %d_normed.1 = (f32[128,2048]{1,0:T(8,128)}, bf16[512,2048]{1,0:T(8,128)(2,1)}, f32[8,128]{1,0:T(8,128)}) custom-call(bf16[2048,384]{1,0:T(8,128)(2,1)} %bitcast.80, bf16[384,2048]{1,0:T(8,128)(2,1)} %fusion.23.w, bf16[16,128,2048]{2,1,0:T(8,128)(2,1)} %multiply_convert_fusion.normed, bf16[128,2048]{1,0:T(8,128)(2,1)} %bitcast.85, ...), custom_call_target="tpu_custom_call" | custom-call | tf_op jit(solution)/shard_map/d_normed/pallas_call | solution.py:406
  536.9 1.3 slice_bitcast_fusion.2
  538.1 3.0 slice_convert_fusion.2
  541.1 1.3 copy.55
  542.4 1.3 copy.54
  543.7 1.3 copy.53
  545.1 6.1 %slice_convert_fusion = (f32[344,2048]{1,0:T(8,128)}, f32[2048,344]{0,1:T(8,128)}, f32[2048,344]{0,1:T(8,128)}) fusion(bf16[1056,2048]{1,0:T(8,128)(2,1)} %get-tuple-element.67), kind=kLoop, calls=%fused_computation.27 | loop fusion | flops 2113536 | bytes 12681216 | tf_op jit(solution)/shard_map/convert_element_type | solution.py:897
  551.1 0.8 copy.71
  551.9 1.0 copy.72
  (24 shorter events, 0.2 us)
Async XLA Ops:
  3.3 7.8 %copy-start.7 = (bf16[16,128]{1,0:T(8,128)(2,1)}, bf16[16,128]{1,0:T(8,128)(2,1)S(1)}, u32[]{:S(2)}) copy-start(bf16[16,128]{1,0:T(8,128)(2,1)S(1)} %scatter.9.gains) | copy-start | bytes 12292
  5.9 5.2 copy-start.1
  9.8 1.9 copy-start.2
  11.7 1.4 copy-start
  98.6 10.4 %copy-start.5 = (bf16[2048,64]{0,1:T(8,128)(2,1)}, bf16[2048,64]{0,1:T(8,128)(2,1)S(1)}, u32[]{:S(2)}) copy-start(bf16[2048,64]{0,1:T(8,128)(2,1)S(1)} %get-tuple-element.120) | copy-start | bytes 786436
  109.0 3.2 copy-start.8
  438.8 1.4 copy-start.6
  438.8 13.3 %slice-start = ((s8[8388608]{0:T(1024)(128)(4,1)}), s8[4194304]{0:T(1024)(128)(4,1)S(1)}, s32[]{:S(2)}) async-start(s8[8388608]{0:T(1024)(128)(4,1)} %bitcast.102), calls=%async_computation | async-start | bytes 8388608
  440.2 12.0 %slice-start.1 = ((s8[8388608]{0:T(1024)(128)(4,1)}), s8[4194304]{0:T(1024)(128)(4,1)S(1)}, s32[]{:S(2)}) async-start(s8[8388608]{0:T(1024)(128)(4,1)} %bitcast.102), calls=%async_computation.1 | async-start | bytes 8388608
  545.1 6.1 %copy-start.4 = (bf16[128,2048]{1,0:T(8,128)(2,1)S(1)}, bf16[128,2048]{1,0:T(8,128)(2,1)}, u32[]{:S(2)}) copy-start(bf16[128,2048]{1,0:T(8,128)(2,1)} %get-tuple-element.61) | copy-start | bytes 1572868
  545.1 6.9 %copy-start.3 = (f32[128,2048]{1,0:T(8,128)S(1)}, f32[128,2048]{1,0:T(8,128)}, u32[]{:S(2)}) copy-start(f32[128,2048]{1,0:T(8,128)} %get-tuple-element.65) | copy-start | bytes 3145732

commit v3 on v2

v3 whole, which is shorter than its diff:
```python
import math

import jax
import jax.numpy as jnp
from jax import lax
from jax.experimental import pallas as pl
from jax.experimental.pallas import tpu as pltpu
from jax.sharding import PartitionSpec as P

EPSILON = 1e-05
BF = jnp.bfloat16
F32 = jnp.float32
MESH = pl.DeviceIdType.MESH
VM = pl.BlockSpec(memory_space=pltpu.VMEM)
FF_ROWS = 352
FF_PAD = 384


def dot(a, b):
    return jnp.dot(a, b, preferred_element_type=F32)


def dot_t(a, b):
    return lax.dot_general(a, b, (((1,), (1,)), ((), ())), preferred_element_type=F32)


def t_dot(a, b):
    return lax.dot_general(a, b, (((0,), (0,)), ((), ())), preferred_element_type=F32)


def place():
    c, g = lax.axis_index("ctx"), lax.axis_index("grp")
    return c // 8, (c // 2) % 4, c % 2, g // 4, g % 4


def slot_at(pos, dz, dy, dk=0):
    z, y, k = pos[:3]
    return ((z + dz) % 2) * 8 + ((y + dy) % 4) * 2 + (k + dk) % 2


HOPS = {"p": (0, 1, 0), "m": (0, 3, 0), "z": (1, 0, 0), "c": (0, 0, 1)}
GROUP_HOPS = {"e": (0, 1), "w": (0, 3), "h": (1, 0)}


def neighbour(pos, link):
    if link in HOPS:
        return (lax.axis_index("grp"), slot_at(pos, *HOPS[link]))
    dh, dx = GROUP_HOPS[link]
    return (((pos[3] + dh) % 2) * 4 + (pos[4] + dx) % 4, lax.axis_index("ctx"))


def ctx_peer(d):
    return (lax.axis_index("grp"), (lax.axis_index("ctx") + d) % 16)


def grp_peer(d):
    return ((lax.axis_index("grp") + d) % 8, lax.axis_index("ctx"))


def greet(targets):
    barrier = pltpu.get_barrier_semaphore()
    for t in targets:
        pl.semaphore_signal(barrier, inc=1, device_id=t, device_id_type=MESH)
    pl.semaphore_wait(barrier, len(targets))


class Copies:
    def __init__(self, pos, send, recv):
        self.pos, self.send, self.recv, self.all = pos, send, recv, {}
        self.unsent, self.count = {}, 0

    def start(self, name, target, src, dst):
        n, self.count = self.count, self.count + 1
        if isinstance(target, str):
            target = neighbour(self.pos, target)
        copy = pltpu.make_async_remote_copy(
            src_ref=src,
            dst_ref=dst,
            send_sem=self.send.at[n],
            recv_sem=self.recv.at[n],
            device_id=target,
            device_id_type=MESH,
        )
        copy.start()
        self.all[name] = self.unsent[name] = copy

    def got(self, *names):
        for name in names:
            self.all[name].wait_recv()

    def sent(self, name):
        self.unsent.pop(name).wait_send()

    def finish(self):
        for name in list(self.unsent):
            self.sent(name)


def columns(width, body, step=512):
    def tile(j, _):
        body(pl.ds(pl.multiple_of(j * step, step), step))
        return 0

    lax.fori_loop(0, width // step, tile, 0)


def add_to(dst, *srcs):
    def tile(cols):
        total = dst[:, cols].astype(F32)
        for s in srcs:
            total = total + s[:, cols].astype(F32)
        dst[:, cols] = total.astype(dst.dtype)

    columns(dst.shape[1], tile)


N_GATHER = 37


def gather_steps(net, pos, buf, tag):
    def send(name, link, dz, dy, lo, n):
        ref = buf.at[slot_at(pos, dz, dy), pl.ds(lo, n)]
        net.start(tag + name, link, ref, ref)

    def got(*names):
        net.got(*[tag + name for name in names])

    send("p1a", "p", 0, 0, 0, 64)
    send("m1a", "m", 0, 0, 64, 64)
    send("z0", "z", 0, 0, 32, 64)
    send("c0", "c", 0, 0, 0, 128)
    send("p1b", "p", 0, 0, 64, 64)
    send("m1b", "m", 0, 0, 0, 64)
    send("zb00", "z", 0, 0, 0, 32)
    send("zb01", "z", 0, 0, 96, 32)
    got("c0")
    yield 0, 0
    got("p1a")
    send("p2", "p", 0, 3, 0, 64)
    send("zb30", "z", 0, 3, 0, 32)
    got("m1a")
    send("m2", "m", 0, 1, 64, 64)
    send("zb11", "z", 0, 1, 96, 32)
    got("z0")
    send("p3", "p", 1, 0, 32, 64)
    send("m3", "m", 1, 0, 32, 64)
    send("c3", "c", 1, 0, 32, 64)
    yield None
    got("p1b")
    send("zb31", "z", 0, 3, 96, 32)
    send("c1", "c", 0, 3, 0, 128)
    got("m1b")
    send("zb10", "z", 0, 1, 0, 32)
    send("c2", "c", 0, 1, 0, 128)
    got("c1")
    yield 0, 3
    got("zb00", "zb01")
    send("c4", "c", 1, 0, 0, 32)
    send("c5", "c", 1, 0, 96, 32)
    got("c2")
    yield 0, 1
    got("p2")
    send("zb20", "z", 0, 2, 0, 32)
    send("c6", "c", 0, 2, 0, 64)
    got("m2")
    send("zb21", "z", 0, 2, 96, 32)
    send("c7", "c", 0, 2, 64, 64)
    got("c3", "c4", "c5")
    yield 1, 0
    got("p3")
    send("p4", "p", 1, 3, 32, 32)
    send("c8", "c", 1, 3, 32, 64)
    got("m3")
    send("m4", "m", 1, 1, 64, 32)
    send("c9", "c", 1, 1, 32, 64)
    got("c6", "c7")
    yield 0, 2
    got("zb30", "zb31")
    send("c10", "c", 1, 3, 0, 32)
    send("c11", "c", 1, 3, 96, 32)
    got("zb10", "zb11")
    send("c12", "c", 1, 1, 0, 32)
    send("c13", "c", 1, 1, 96, 32)
    got("c8", "c10", "c11")
    yield 1, 3
    got("p4")
    send("c14", "c", 1, 2, 32, 32)
    got("m4")
    send("c15", "c", 1, 2, 64, 32)
    got("c9", "c12", "c13")
    yield 1, 1
    got("zb20")
    send("c16", "c", 1, 2, 0, 32)
    got("zb21")
    send("c17", "c", 1, 2, 96, 32)
    got("c14", "c15", "c16", "c17")
    yield 1, 2


def gather_round_steps(net, pos, buf, tag):
    def send(name, link, dz, dy, lo=0, n=128):
        ref = buf.at[slot_at(pos, dz, dy), pl.ds(lo, n)]
        net.start(tag + name, link, ref, ref)

    def got(*names):
        net.got(*[tag + name for name in names])

    send("z0", "z", 0, 0)
    send("p1a", "p", 0, 0, 0, 64)
    send("m1a", "m", 0, 0, 64, 64)
    send("c0", "c", 0, 0)
    send("p1b", "p", 0, 0, 64, 64)
    send("m1b", "m", 0, 0, 0, 64)
    got("c0")
    yield 0, 0
    got("p1a")
    send("p2", "p", 0, 3, 0, 64)
    got("m1a")
    send("m2", "m", 0, 1, 64, 64)
    got("z0")
    send("p3a", "p", 1, 0, 0, 64)
    send("m3a", "m", 1, 0, 64, 64)
    send("p3b", "p", 1, 0, 64, 64)
    send("m3b", "m", 1, 0, 0, 64)
    send("c3", "c", 1, 0)
    got("p1b")
    send("c1", "c", 0, 3)
    got("m1b")
    send("c2", "c", 0, 1)
    got("c1")
    yield 0, 3
    got("c2")
    yield 0, 1
    got("p2")
    send("c4", "c", 0, 2, 0, 64)
    got("m2")
    send("c5", "c", 0, 2, 64, 64)
    got("c3")
    yield 1, 0
    got("p3a")
    send("p4", "p", 1, 3, 0, 64)
    got("m3a")
    send("m4", "m", 1, 1, 64, 64)
    got("c4", "c5")
    yield 0, 2
    got("p3b")
    send("c6", "c", 1, 3)
    got("m3b")
    send("c7", "c", 1, 1)
    got("c6")
    yield 1, 3
    got("c7")
    yield 1, 1
    got("p4")
    send("c8", "c", 1, 2, 0, 64)
    got("m4")
    send("c9", "c", 1, 2, 64, 64)
    got("c8", "c9")
    yield 1, 2


N_SCATTER = 29
INBOX_ROWS = 896


def scatter_scratch(w):
    return [
        pltpu.VMEM((16, 128, w), BF),
        pltpu.VMEM((8, 128, w), BF),
        pltpu.VMEM((INBOX_ROWS, w), BF),
    ]


class Scatter:
    def __init__(self, net, pos, part, sib, inbox, tag, z_last=False):
        self.net, self.pos, self.part, self.sib, self.tag = net, pos, part, sib, tag
        self.box, at = {}, 0
        if z_last:
            rows = [(side + step, n) for step, n in zip("4321", (64, 128, 64, 128)) for side in "pm"]
            rows.append(("z0", 128))
        else:
            rows = [("zb%d%d" % (dy, h), 32) for dy in range(4) for h in range(2)]
            rows += [(side + step, n) for step, n in zip("4321", (32, 64, 64, 128)) for side in "pm"]
            rows.append(("z0", 64))
        for key, n in rows:
            self.box[key] = inbox.at[pl.ds(at, n)]
            at += n
        for side in "pm":
            whole = self.box[side + "1"]
            self.box[side + "1a"] = whole.at[pl.ds(32, 64)]
            self.box[side + "1b"] = whole.at[pl.ds(0, 32)]
            self.box[side + "1c"] = whole.at[pl.ds(96, 32)]

    def mine(self, dz, dy, lo=0, n=128):
        return self.part.at[slot_at(self.pos, dz, dy), pl.ds(lo, n)]

    def swap(self, dz, dy):
        src = self.part.at[slot_at(self.pos, dz, dy, 1)]
        self.net.start(self.tag + "c%d%d" % (dz, dy), "c", src, self.sib.at[dz * 4 + dy])

    def joined(self, dz, dy):
        self.got("c%d%d" % (dz, dy))
        add_to(self.mine(dz, dy), self.sib.at[dz * 4 + dy])

    def got(self, *names):
        self.net.got(*[self.tag + name for name in names])

    def put(self, name, link, src):
        self.net.start(self.tag + name, link, src, self.box[name])

    def put_zb(self, dy):
        for h, lo in ((0, 0), (1, 96)):
            self.put("zb%d%d" % (dy, h), "z", self.mine(1, dy, lo, 32))

    def take(self, name, dz, dy, lo, n):
        self.got(name)
        add_to(self.mine(dz, dy, lo, n), self.box[name])

    def take_zb(self, dy):
        self.take("zb%d0" % dy, 0, dy, 0, 32)
        self.take("zb%d1" % dy, 0, dy, 96, 32)

    def steps(self):
        self.joined(1, 2)
        self.put_zb(2)
        self.put("p4", "p", self.mine(1, 2, 64, 32))
        self.put("m4", "m", self.mine(1, 2, 32, 32))
        self.joined(1, 1)
        self.put_zb(1)
        self.joined(1, 3)
        self.put_zb(3)
        yield
        self.take("p4", 1, 1, 64, 32)
        self.put("p3", "p", self.mine(1, 1, 32, 64))
        self.take("m4", 1, 3, 32, 32)
        self.put("m3", "m", self.mine(1, 3, 32, 64))
        self.joined(0, 2)
        yield
        self.take_zb(2)
        self.put("p2", "p", self.mine(0, 2, 64, 64))
        self.put("m2", "m", self.mine(0, 2, 0, 64))
        self.joined(1, 0)
        self.joined(0, 1)
        self.joined(0, 3)
        yield
        self.take("p3", 1, 0, 32, 64)
        self.take("m3", 1, 0, 32, 64)
        self.put("z0", "z", self.mine(1, 0, 32, 64))
        yield
        self.take("p2", 0, 1, 64, 64)
        self.put("p1a", "p", self.mine(0, 1, 32, 64))
        self.take("m2", 0, 3, 0, 64)
        self.put("m1a", "m", self.mine(0, 3, 32, 64))
        self.joined(0, 0)
        yield
        self.take_zb(1)
        self.put("p1b", "p", self.mine(0, 1, 0, 32))
        self.put("p1c", "p", self.mine(0, 1, 96, 32))
        self.put_zb(0)
        self.take_zb(3)
        self.put("m1b", "m", self.mine(0, 3, 0, 32))
        self.put("m1c", "m", self.mine(0, 3, 96, 32))
        yield
        self.take("z0", 0, 0, 32, 64)
        self.take_zb(0)
        yield
        self.got("p1a", "m1a", "p1b", "p1c", "m1b", "m1c")

    def z_last_steps(self):
        self.joined(1, 2)
        self.put("p4", "p", self.mine(1, 2, 64, 64))
        self.put("m4", "m", self.mine(1, 2, 0, 64))
        self.joined(0, 2)
        self.put("p2", "p", self.mine(0, 2, 64, 64))
        self.put("m2", "m", self.mine(0, 2, 0, 64))
        self.joined(1, 1)
        self.joined(1, 3)
        yield
        self.take("p4", 1, 1, 64, 64)
        self.put("p3", "p", self.mine(1, 1))
        self.take("m4", 1, 3, 0, 64)
        self.put("m3", "m", self.mine(1, 3))
        self.joined(0, 1)
        self.joined(0, 3)
        yield
        self.take("p2", 0, 1, 64, 64)
        self.put("p1", "p", self.mine(0, 1))
        self.take("m2", 0, 3, 0, 64)
        self.put("m1", "m", self.mine(0, 3))
        self.joined(1, 0)
        self.joined(0, 0)
        yield
        self.take("p3", 1, 0, 0, 128)
        self.take("m3", 1, 0, 0, 128)
        self.put("z0", "z", self.mine(1, 0))
        yield
        self.take("z0", 0, 0, 0, 128)
        self.got("p1", "m1")

    def total(self, cols):
        sums = self.mine(0, 0)[:, cols].astype(F32)
        return sums + self.box["p1"][:, cols].astype(F32) + self.box["m1"][:, cols].astype(F32)


SCATTER_ORDER = [(1, 2), (1, 1), (1, 3), (1, 0), (0, 2), (0, 1), (0, 3), (0, 0)]


def pair_rows(pos, dz, dy):
    first = slot_at(pos, dz, dy) // 2
    return first * 2, pl.ds(pl.multiple_of(first * 256, 256), 256)


def product(pos, part, dz, dy, *factors):
    slot, rows = pair_rows(pos, dz, dy)

    def tile(cols):
        total = None
        for a, b in factors:
            term = dot(a[rows, :], b[:, cols])
            total = term if total is None else total + term
        part[slot, :, cols] = total[:128].astype(BF)
        part[slot + 1, :, cols] = total[128:].astype(BF)

    columns(part.shape[2], tile)


def span(pos, d, part, half=None):
    start = ((pos[4] + d) % 4) * 512 + part * 256
    if half is None:
        return pl.ds(pl.multiple_of(start, 256), 256)
    return pl.ds(pl.multiple_of(start + half * 128, 128), 128)


def ring_sum_scratch(rows):
    return [
        pltpu.VMEM((2, 2, rows, 128), BF),
        pltpu.VMEM((2, 2, rows, 256), BF),
    ]


def by_rows(rows, body):
    def step(i, _):
        body(pl.ds(pl.multiple_of(i * 32, 32), 32))
        return 0

    lax.fori_loop(0, rows // 32, step, 0)


class Ring:
    def __init__(self, net, pos, tag):
        self.net, self.pos, self.tag = net, pos, tag

    def put(self, name, link, src, dst):
        self.net.start(self.tag + name, link, src, dst)

    def got(self, *names):
        self.net.got(*[self.tag + name for name in names])

    def far(self, p, terms, far):
        self.put("e2%d" % p, "e", terms.at[:, span(self.pos, 2, p, 0)], far.at[p, 0])
        self.put("w2%d" % p, "w", terms.at[:, span(self.pos, 2, p, 1)], far.at[p, 1])

    def near(self, p, terms, far, near):
        for name, d, half in (("e", 1, 0), ("w", 3, 1)):
            self.got("%s2%d" % (name, p))
            cols = span(self.pos, d, p, half)

            def fold(r, half=half, cols=cols):
                total = terms[r, cols].astype(F32) + far[p, half, r, :].astype(F32)
                terms[r, cols] = total.astype(BF)

            by_rows(terms.shape[0], fold)
            src = terms.at[:, span(self.pos, d, p)]
            self.put("%s1%d" % (name, p), name, src, near.at[p, half])

    def join(self, p, terms, near, chunk):
        self.got("e1%d" % p, "w1%d" % p)

        def add(r):
            total = terms[r, span(self.pos, 0, p)].astype(F32) + near[p, 0, r, :].astype(F32)
            chunk[p, r, :] = (total + near[p, 1, r, :].astype(F32)).astype(BF)

        by_rows(terms.shape[0], add)

    def across(self, p, chunk, box):
        self.put("h%d" % p, "h", chunk.at[p], box.at[p])

    def crossed(self, p, chunk, box, whole):
        self.got("h%d" % p)
        cols = span(self.pos, 0, p)

        def add(r):
            total = chunk[p, r, :].astype(F32) + box[p, r, :].astype(F32)
            whole[r, cols] = total.astype(BF)

        by_rows(whole.shape[0], add)
        for name in "ew":
            self.put("%s3%d" % (name, p), name, whole.at[:, cols], whole.at[:, cols])

    def share(self, p, whole):
        for name, d, half in (("e", 3, 0), ("w", 1, 1)):
            self.got("%s3%d" % (name, p))
            ref = whole.at[:, span(self.pos, d, p, half)]
            self.put("%s4%d" % (name, p), name, ref, ref)

    def shared(self, p):
        self.got("e4%d" % p, "w4%d" % p)


N_RING_SUM = 8
N_RING_SHARE = 10


def run(*steps):
    steps = list(steps)
    while steps:
        for s in list(steps):
            try:
                next(s)
            except StopIteration:
                steps.remove(s)


def sems(n):
    return [pltpu.SemaphoreType.DMA((n,)), pltpu.SemaphoreType.DMA((n,))]


def call(kernel, name, cid, outs, scratch, args, mib=60):
    return pl.pallas_call(
        kernel,
        out_shape=[jax.ShapeDtypeStruct(s, d) for s, d in outs],
        in_specs=[VM] * len(args),
        out_specs=[VM] * len(outs),
        scratch_shapes=scratch,
        compiler_params=pltpu.CompilerParams(
            collective_id=cid, has_side_effects=True, vmem_limit_bytes=mib * 2**20
        ),
        name=name,
    )(*args)


def norm_factor(u):
    return lax.rsqrt(jnp.mean(u * u, -1, keepdims=True) + EPSILON)


def d_normed_kernel(
    d_qkv,
    w,
    normed,
    acts,
    d_res,
    gain,
    grad_out,
    gain_two_part,
    acts_grad,
    whole,
    gains,
    part,
    sib,
    inbox,
    terms,
    chunk,
    box,
    far,
    near,
    low_t,
    gain_terms,
    gain_box,
    gain_sum,
    gain_wide,
    send,
    recv,
):
    pos = place()
    net = Copies(pos, send, recv)
    me = lax.axis_index("ctx")
    greet([ctx_peer(d) for d in range(1, 16)] + [grp_peer(d) for d in range(1, 8)])
    sums = Scatter(net, pos, part, sib, inbox, "s", True)
    low_t[...] = d_qkv[...].T
    terms[pl.ds(384, 128), :] = grad_out[...]
    gain_terms[...] = jnp.zeros_like(gain_terms)
    for j in range(16):
        cols = slice(j * 128, (j + 1) * 128)
        gain_terms[j, 0:1, :] = gain_two_part[:, cols]

    def weight_grads(d, p):
        cols = span(pos, d, p)
        g = dot(low_t[...], normed[:, :, cols].reshape(2048, 256))
        terms[pl.ds(0, 384), cols] = g.astype(BF)
        by_column = jnp.sum(g * w[:, cols].astype(F32), 0, keepdims=True) / gain[:, cols]
        first = ((pos[4] + d) % 4) * 4 + p * 2
        gain_terms[first, 1:2, :] = by_column[:, :128]
        gain_terms[first + 1, 1:2, :] = by_column[:, 128:]

    def products(pairs):
        for dz, dy in pairs:
            product(pos, part, dz, dy, (d_qkv, w))
            sums.swap(dz, dy)

    ring = Ring(net, pos, "r")
    back = sums.z_last_steps()
    weight_grads(2, 0)
    ring.far(0, terms, far)
    products(SCATTER_ORDER[:1])
    weight_grads(2, 1)
    ring.far(1, terms, far)
    products(SCATTER_ORDER[1:])
    next(back)
    weight_grads(1, 0)
    weight_grads(3, 0)
    ring.near(0, terms, far, near)
    next(back)
    weight_grads(1, 1)
    weight_grads(3, 1)
    ring.near(1, terms, far, near)
    next(back)
    weight_grads(0, 0)
    weight_grads(0, 1)
    for d in range(1, 16):
        net.start("g%d" % d, ctx_peer(d), gain_terms.at[(me + d) % 16], gain_box.at[d])
    gain_box[0] = gain_terms[me]
    ring.join(0, terms, near, chunk)
    ring.across(0, chunk, box)
    ring.join(1, terms, near, chunk)
    ring.across(1, chunk, box)
    next(back)
    ring.crossed(0, chunk, box, whole)
    net.got(*["g%d" % d for d in range(1, 16)])
    gain_sum[...] = jnp.sum(gain_box[...], 0)
    for d in range(1, 8):
        net.start("h%d" % d, grp_peer(d), gain_sum, gain_wide.at[d])
    gain_wide[0] = gain_sum[...]
    ring.crossed(1, chunk, box, whole)
    ring.share(0, whole)
    run(back)
    ring.share(1, whole)
    net.got(*["h%d" % d for d in range(1, 8)])
    gains[...] = jnp.sum(gain_wide[...], 0)

    def finish(i, _):
        r = pl.ds(pl.multiple_of(i * 32, 32), 32)
        e = (
            part[me, r, :].astype(F32)
            + sums.box["p1"][r, :].astype(F32)
            + sums.box["m1"][r, :].astype(F32)
        )
        u = acts[r, :].astype(F32)
        f = norm_factor(u)
        scaled = e * gain[...]
        grad = f * scaled - u * f * f * f * jnp.mean(scaled * u, -1, keepdims=True)
        acts_grad[r, :] = d_res[r, :] + grad
        return 0

    lax.fori_loop(0, 4, finish, 0)
    ring.shared(0)
    ring.shared(1)
    net.finish()


def d_normed(d_qkv, w, normed, acts, d_res, gain, grad_out, gain_two_part, cid):
    return call(
        d_normed_kernel,
        "d_normed",
        cid,
        [((128, 2048), F32), ((512, 2048), BF), ((8, 128), F32)],
        scatter_scratch(2048)
        + [pltpu.VMEM((512, 2048), BF), pltpu.VMEM((2, 512, 256), BF), pltpu.VMEM((2, 512, 256), BF)]
        + ring_sum_scratch(512)
        + [
            pltpu.VMEM((384, 2048), BF),
            pltpu.VMEM((16, 8, 128), F32),
            pltpu.VMEM((16, 8, 128), F32),
            pltpu.VMEM((8, 128), F32),
            pltpu.VMEM((8, 8, 128), F32),
        ]
        + sems(N_SCATTER + N_RING_SUM + N_RING_SHARE + 22),
        [d_qkv, w, normed, acts, d_res, gain, grad_out, gain_two_part],
    )


def rope(u, cosine, sine):
    return u * cosine + pltpu.roll(u, 64, 1) * sine


def block_start(c, half):
    return c * 64 if half == 0 else (31 - c) * 64


def document_start(position, lens):
    first = lens[0:1, 0:1]
    return jnp.where(position >= first, first, 0)


def bias_at(position, lens):
    own = jnp.where(position >= lens[0:1, 0:1], lens[1:2, 0:1], lens[0:1, 0:1])
    return -jnp.log(own.astype(F32))


def project_kernel(
    x,
    gains,
    lens,
    frequency,
    w_query,
    w_key,
    w_value,
    normed,
    qkv,
    cosines,
    sines,
    gain_rows,
    buf,
    gain_box,
    w,
    send,
    recv,
):
    pos = place()
    net = Copies(pos, send, recv)
    me = lax.axis_index("ctx")
    buf[me] = x[...]
    gain_box[me] = gains[...]
    greet([ctx_peer(d) for d in range(1, 16)])
    for d in range(1, 16):
        ref = gain_box.at[me]
        net.start("g%d" % d, ctx_peer(d), ref, ref)
    arrivals = gather_steps(net, pos, buf, "x")
    dz, dy = next(arrivals)

    def table(i, _):
        r = pl.ds(pl.multiple_of(i * 256, 256), 256)
        position = lax.broadcasted_iota(jnp.int32, (256, 128), 0) + i * 256
        offset = position - document_start(position, lens)
        angle = offset.astype(F32) * frequency[0:1, :]
        lane = lax.broadcasted_iota(jnp.int32, (256, 128), 1)
        cosines[r, :] = jnp.cos(angle)
        sines[r, :] = jnp.where(lane < 64, -1.0, 1.0) * jnp.sin(angle)
        return 0

    lax.fori_loop(0, 8, table, 0)
    for i, ref in enumerate((w_query, w_key, w_value)):
        w[:, i * 128 : (i + 1) * 128] = ref[...]
    net.got(*["g%d" % d for d in range(1, 16)])
    gain_rows[...] = jnp.zeros_like(gain_rows)
    for j in range(16):
        gain_rows[0:2, j * 128 : (j + 1) * 128] = gain_box[j].astype(F32)[0:2]

    while True:
        slot, _ = pair_rows(pos, dz, dy)

        def normalise(i, _, slot=slot):
            r = pl.ds(pl.multiple_of((i % 2) * 64, 64), 64)
            u = buf[slot + i // 2, r, :].astype(F32)
            normed[slot + i // 2, r, :] = (u * norm_factor(u) * gain_rows[0:1, :]).astype(BF)
            return 0

        lax.fori_loop(0, 4, normalise, 0)
        out = dot(normed[pl.ds(slot, 2)].reshape(256, 2048), w[...])
        for b in range(2):
            for half in range(2):
                at = pl.ds(pl.multiple_of(block_start(slot + b, half), 64), 64)
                rows = slice(b * 128 + half * 64, b * 128 + half * 64 + 64)
                c, s = cosines[at, :], sines[at, :]
                qkv[0, at, :] = rope(out[rows, :128], c, s).astype(BF)
                qkv[1, at, :] = rope(out[rows, 128:256], c, s).astype(BF)
                qkv[2, at, :] = out[rows, 256:].astype(BF)
        arrived = next(arrivals, ())
        if arrived is None:
            arrived = next(arrivals)
        if not arrived:
            break
        dz, dy = arrived
    net.finish()


def project(x, gains, lens, frequency, w_query, w_key, w_value, cid):
    return call(
        project_kernel,
        "project",
        cid,
        [
            ((16, 128, 2048), BF),
            ((3, 2048, 128), BF),
            ((2048, 128), F32),
            ((2048, 128), F32),
            ((8, 2048), F32),
        ],
        [
            pltpu.VMEM((16, 128, 2048), BF),
            pltpu.VMEM((16, 16, 128), BF),
            pltpu.VMEM((2048, 384), BF),
        ]
        + sems(N_GATHER + 15),
        [x, gains, lens, frequency, w_query, w_key, w_value],
    )


SCALE = 1.0 / math.sqrt(128)


def attend_block(qkv, lens, i):
    q = qkv[0, 256 * i : 256 * (i + 1), :]
    row = lax.broadcasted_iota(jnp.int32, (256, 1), 0) + 256 * i
    start = document_start(row, lens)
    bias = bias_at(row, lens)
    total = jnp.zeros((256, 128), F32)
    for lo in range(0, 256 * (i + 1), 512):
        n = min(512, 256 * (i + 1) - lo)
        score = dot_t(q, qkv[1, lo : lo + n, :]) * SCALE + bias
        col = lax.broadcasted_iota(jnp.int32, (1, n), 1) + lo
        visible = col >= start
        if lo + n > 256 * i:
            visible = visible & (col <= row)
        prob = jnp.where(visible, jax.nn.sigmoid(score), 0.0).astype(BF)
        total = total + dot(prob, qkv[2, lo : lo + n, :])
    return total


def packed_start(block):
    return block * 128 if block < 16 else (31 - block) * 128 + 64


def middle_kernel(
    qkv,
    lens,
    w_out,
    cot,
    acts,
    gain,
    w,
    attended,
    residual,
    d_res,
    gain_part,
    hidden,
    grads,
    cot_all,
    buf,
    low_t,
    part,
    sib,
    inbox,
    send,
    recv,
):
    pos = place()
    net = Copies(pos, send, recv)
    me = lax.axis_index("ctx")
    cot_all[me] = cot[...]
    greet([neighbour(pos, l) for l in "pmzc"])
    cots = gather_steps(net, pos, cot_all, "c")
    next(cots)
    for i in range(8):
        out = attend_block(qkv, lens, i).astype(BF)
        for b in range(4):
            at = packed_start(4 * i + b)
            attended[at : at + 64, :] = out[64 * b : 64 * (b + 1)]
        if i == 6:
            next(cots)
    sums = Scatter(net, pos, part, sib, inbox, "a")
    for dz, dy in SCATTER_ORDER:
        product(pos, part, dz, dy, (attended, w_out))
        sums.swap(dz, dy)
    run(sums.steps(), cots)

    def normalise(i, _):
        r = pl.ds(pl.multiple_of(i * 32, 32), 32)
        u = (
            acts[r, :].astype(F32)
            + part[me, r, :].astype(F32)
            + sums.box["p1"][r, :].astype(F32)
            + sums.box["m1"][r, :].astype(F32)
        )
        residual[r, :] = u
        buf[me, r, :] = (u * norm_factor(u) * gain[...]).astype(BF)
        return 0

    lax.fori_loop(0, 4, normalise, 0)
    net.finish()
    sums = Scatter(net, pos, part, sib, inbox, "s")
    for arrived in gather_steps(net, pos, buf, "x"):
        if arrived is None:
            continue
        dz, dy = arrived
        slot, rows = pair_rows(pos, dz, dy)
        n2 = buf[pl.ds(slot, 2)].reshape(256, 2048)
        ct = cot_all[pl.ds(slot, 2)].reshape(256, 2048)
        gate = dot_t(n2, w[0])
        up = dot_t(n2, w[1])
        d_hidden = dot_t(ct, w[2])
        sig = jax.nn.sigmoid(gate)
        silu = gate * sig
        h = (silu * up).astype(BF)
        dg = (d_hidden * up * sig * (1.0 + gate * (1.0 - sig))).astype(BF)
        du = (d_hidden * silu).astype(BF)
        hidden[rows, :] = h
        low_t[0, :, rows] = dg.T
        low_t[1, :, rows] = du.T
        low_t[2, :, rows] = h.T

        def tile(cols):
            t = dot(dg, w[0, :, cols]) + dot(du, w[1, :, cols])
            part[slot, :, cols] = t[:128].astype(BF)
            part[slot + 1, :, cols] = t[128:].astype(BF)

        columns(2048, tile)
        sums.swap(dz, dy)

    def weight_grads():
        for i, other in ((0, buf), (1, buf), (2, cot_all)):

            def tile(cols, i=i, other=other):
                rhs = other[:, :, cols].reshape(2048, 256)
                g = dot(low_t[i], rhs)
                grads[i * FF_ROWS : (i + 1) * FF_ROWS, cols] = g[:FF_ROWS].astype(BF)

            for half in range(2):

                def part_tile(j, _, half=half, tile=tile):
                    tile(pl.ds(pl.multiple_of(half * 1024 + j * 256, 256), 256))
                    return 0

                lax.fori_loop(0, 4, part_tile, 0)
                yield

    run(sums.steps(), weight_grads())

    gain_part[...] = jnp.zeros_like(gain_part)

    def back(i, _):
        r = pl.ds(pl.multiple_of(i * 32, 32), 32)
        slot = me
        e = (
            part[slot, r, :].astype(F32)
            + sums.box["p1"][r, :].astype(F32)
            + sums.box["m1"][r, :].astype(F32)
        )
        u = residual[r, :]
        f = norm_factor(u)
        scaled = e * gain[...]
        grad = f * scaled - u * f * f * f * jnp.mean(scaled * u, -1, keepdims=True)
        d_res[r, :] = cot[r, :].astype(F32) + grad
        gain_part[...] += jnp.sum(e * u * f, 0, keepdims=True)
        return 0

    lax.fori_loop(0, 4, back, 0)
    net.finish()


def middle(*args):
    return call(
        middle_kernel,
        "middle",
        1,
        [
            ((2048, 128), BF),
            ((128, 2048), F32),
            ((128, 2048), F32),
            ((1, 2048), F32),
            ((2048, FF_PAD), BF),
            ((3 * FF_ROWS, 2048), BF),
        ],
        [pltpu.VMEM((16, 128, 2048), BF), pltpu.VMEM((16, 128, 2048), BF)]
        + [pltpu.VMEM((3, FF_PAD, 2048), BF)]
        + scatter_scratch(2048)
        + sems(2 * N_SCATTER + 2 * N_GATHER),
        args,
        62,
    )


def attention_back_kernel(
    d_res,
    attended,
    w_out,
    ff,
    qkv,
    lens,
    cosines,
    sines,
    hidden,
    w_down,
    residual,
    d_qkv,
    grad_out,
    mixed,
    whole,
    buf,
    part,
    sib,
    inbox,
    far,
    near,
    chunk,
    box,
    total,
    do,
    dq,
    send,
    recv,
):
    pos = place()
    net = Copies(pos, send, recv)
    buf[lax.axis_index("ctx")] = d_res[...].astype(BF)
    greet([neighbour(pos, l) for l in "pmzcewh"])
    sums = Scatter(net, pos, part, sib, inbox, "s", True)
    back = sums.z_last_steps()
    ring = Ring(net, pos, "r")
    arrivals = gather_steps(net, pos, buf, "x")

    def arrive():
        pair = next(arrivals)
        if pair is None:
            pair = next(arrivals)
        slot, rows = pair_rows(pos, *pair)
        d = buf[pl.ds(slot, 2)].reshape(256, 2048)
        g = dot_t(d, w_out[...]).astype(BF)
        for b in range(2):
            for half in range(2):
                at = pl.ds(pl.multiple_of(block_start(slot + b, half), 64), 64)
                do[at, :] = g[b * 128 + half * 64 : b * 128 + half * 64 + 64]
        total[...] += t_dot(attended[rows, :], d)

    def products(pairs):
        for dz, dy in pairs:
            product(pos, part, dz, dy, (hidden, w_down))
            sums.swap(dz, dy)

    def put(block, value, i):
        for b in range(4):
            at = packed_start(4 * block + b)
            d_qkv[at : at + 64, 128 * i : 128 * (i + 1)] = value[64 * b : 64 * (b + 1)]

    def unrotate(u, block):
        r = slice(256 * block, 256 * (block + 1))
        return rope(u * SCALE, cosines[r, :], -sines[r, :]).astype(BF)

    def keys(j):
        mine = slice(256 * j, 256 * (j + 1))
        k, v = qkv[1, mine, :], qkv[2, mine, :]
        row = lax.broadcasted_iota(jnp.int32, (256, 1), 0) + 256 * j
        dk = jnp.zeros((256, 128), F32)
        dv = jnp.zeros((256, 128), F32)
        for lo in range(256 * j, 2048, 512):
            n = min(512, 2048 - lo)
            rows = slice(lo, lo + n)
            col = lax.broadcasted_iota(jnp.int32, (1, n), 1) + lo
            q, d = qkv[0, rows, :], do[rows, :]
            sig = jax.nn.sigmoid(dot_t(k, q) * SCALE + bias_at(col, lens))
            visible = row >= document_start(col, lens)
            if lo == 256 * j:
                visible = visible & (row <= col)
            sig = jnp.where(visible, sig, 0.0)
            dv = dv + dot(sig.astype(BF), d)
            ds = (dot_t(v, d) * sig * (1.0 - sig)).astype(BF)
            dk = dk + dot(ds, q)
            dq[rows, :] += t_dot(ds, k)
        put(j, unrotate(dk, j), 1)
        put(j, dv.astype(BF), 2)

    ring.far(0, ff, far)
    ring.far(1, ff, far)
    total[...] = jnp.zeros_like(total)
    dq[...] = jnp.zeros_like(dq)
    arrive()
    products(SCATTER_ORDER)
    ring.near(0, ff, far, near)
    arrive()
    ring.near(1, ff, far, near)
    arrive()
    arrive()
    arrive()
    arrive()
    next(back)
    arrive()
    ring.join(0, ff, near, chunk)
    ring.across(0, chunk, box)
    arrive()
    grad_out[...] = total[...].astype(BF)
    keys(0)
    next(back)
    ring.join(1, ff, near, chunk)
    ring.across(1, chunk, box)
    keys(1)
    keys(2)
    next(back)
    ring.crossed(0, chunk, box, whole)
    keys(3)
    keys(4)
    next(back)
    keys(5)
    keys(6)
    ring.crossed(1, chunk, box, whole)
    ring.share(0, whole)
    keys(7)
    for i in range(8):
        put(i, unrotate(dq[256 * i : 256 * (i + 1), :], i), 0)
    run(back)

    def last(cols):
        mixed[:, cols] = (residual[:, cols] + sums.total(cols)).astype(BF)

    columns(2048, last)
    ring.share(1, whole)
    ring.shared(0)
    ring.shared(1)
    net.finish()


def attention_back(*args):
    return call(
        attention_back_kernel,
        "attention_back",
        3,
        [
            ((2048, 384), BF),
            ((128, 2048), BF),
            ((128, 2048), BF),
            ((3 * FF_ROWS, 2048), BF),
        ],
        [pltpu.VMEM((16, 128, 2048), BF)]
        + scatter_scratch(2048)
        + ring_sum_scratch(3 * FF_ROWS)
        + [pltpu.VMEM((2, 3 * FF_ROWS, 256), BF), pltpu.VMEM((2, 3 * FF_ROWS, 256), BF)]
        + [
            pltpu.VMEM((128, 2048), F32),
            pltpu.VMEM((2048, 128), BF),
            pltpu.VMEM((2048, 128), F32),
        ]
        + sems(N_GATHER + N_SCATTER + N_RING_SUM + N_RING_SHARE),
        args,
    )


def local(
    acts,
    doc_lengths,
    w_query,
    w_key,
    w_value,
    w_out,
    w_gate,
    w_up,
    w_down,
    gain_attn,
    gain_mlp,
    cotangent,
):
    tok = acts.shape[2]
    width = acts.shape[3]
    head = w_query.shape[1]
    ff = w_gate.shape[1]

    acts_rows = acts.reshape(tok, width)
    cot_low = cotangent.reshape(tok, width)
    gains = jnp.zeros((16, head), BF).at[0].set(gain_attn).at[1].set(gain_mlp)
    lens = jnp.broadcast_to(
        jnp.concatenate([doc_lengths.reshape(2), jnp.zeros((6,), jnp.int32)])[:, None], (8, head)
    )
    lane = jnp.arange(head) % (head // 2)
    frequency = 10000.0 ** (-(lane.astype(F32) * 2.0 / head))
    frequency = jnp.broadcast_to(frequency, (8, head))
    normed, qkv, cosines, sines, gain_rows = project(
        acts_rows, gains, lens, frequency, w_query, w_key, w_value, 0
    )
    def padded(w):
        return jnp.pad(w, ((0, FF_PAD - ff), (0, 0)))

    ff_w = jnp.stack([padded(w_gate.T), padded(w_up.T), padded(w_down)])
    attended, residual, d_res, gain_two_part, hidden, ff_grads = middle(
        qkv, lens, w_out, cot_low, acts_rows, gain_rows[1:2], ff_w
    )
    d_qkv, grad_out, mixed, ff_sums = attention_back(
        d_res, attended, w_out, ff_grads, qkv, lens, cosines, sines, hidden, ff_w[2], residual
    )
    acts_grad, attn_sums, gain_grads = d_normed(
        d_qkv,
        jnp.concatenate([w_query.T, w_key.T, w_value.T]),
        normed,
        acts_rows,
        d_res,
        gain_rows[0:1],
        grad_out,
        gain_two_part,
        5,
    )

    def ff_grad(i):
        return ff_sums[i * FF_ROWS : i * FF_ROWS + ff].astype(F32)

    def attn_grad(i):
        return attn_sums[i * head : (i + 1) * head].astype(F32)

    return (
        mixed.reshape(1, 1, tok, width),
        acts_grad.reshape(1, 1, tok, width),
        attn_grad(0).T,
        attn_grad(1).T,
        attn_grad(2).T,
        attn_grad(3),
        ff_grad(0).T,
        ff_grad(1).T,
        ff_grad(2),
        gain_grads[1],
        gain_grads[0],
    )


def solution(mesh):
    row = P("grp", "ctx", None, None)
    col = P(None, "ctx")
    dep = P("ctx", None)
    vec = P("ctx")
    in_specs = (row, P("grp", None), col, col, col, dep, col, col, dep, vec, vec, row)
    out_specs = (row, row, col, col, col, dep, col, col, dep, vec, vec)
    return jax.shard_map(local, mesh=mesh, in_specs=in_specs, out_specs=out_specs, check_vma=False)
```

time: 564 us -> 405 us (0.72)
  Pallas kernels: 439 us -> 367 us
  matrix products: 34.7 us -> 0 us
  other arithmetic: 45 us -> 12.9 us
  local copies, waits for them, and re-layouts: 33.4 us -> 15.7 us
    pallas_call x6 -> x4, Pallas kernels: 439 us -> 367 us  [call(): pl.pallas_call(kernel, out_shape=[jax.ShapeDtypeStruct(s, d) for s, d in...]
    dot_general x7 -> x0, matrix products: 34.7 us -> none  [the longest x2 19.8 us: dot_t(): lax.dot_general(a, b, (((1,), (1,)), ((), ())), preferred_element_type=F32)]
    unnamed x34 -> x26, local copies, waits for them, and re-layouts: 21.3 us -> 7.87 us
    convert_element_type x4 -> x0, other arithmetic: 11.4 us -> none  [the longest x1 8.64 us: local(): normed = (tokens_all * norm_factor(tokens_all) * gain_first).astype(BF)]
    unnamed x5 -> x0, other arithmetic: 9.04 us -> none
where the time goes in v3:
time: 405 us; the launch traced here: 397 us
  Pallas kernels  367 us (91%)
  local copies, waits for them, and re-layouts  15.7 us (4%)
  other arithmetic  12.9 us (3%)
    pallas_call x4, Pallas kernels, call(): pl.pallas_call(kernel, out_shape=[jax.ShapeDtypeStruct(s, d) for s, d in...  367 us

profile of v3, /device:TPU:0, one launch (start us, length us, event | category | flops | bytes accessed | tf_op | source)
XLA Modules:
  0.0 396.8 jit_solution(12682607394701769415)
XLA Ops:
  0.6 0.0 copy-start.3
  0.7 0.8 concatenate.10
  1.4 0.7 broadcast_in_dim.4.lens
  2.1 0.7 scatter.6
  2.7 0.7 scatter.9.gains
  3.4 0.0 copy-start.8
  3.4 0.6 broadcast_in_dim.5.frequency
  4.0 0.0 copy-done.8
  4.0 45.3 %project.1 = (bf16[16,128,2048]{2,1,0:T(8,128)(2,1)}, bf16[3,2048,128]{2,1,0:T(8,128)(2,1)}, f32[2048,128]{1,0:T(8,128)}, f32[2048,128]{1,0:T(8,128)}, f32[8,2048]{1,0:T(8,128)}) custom-call(bf16[128,2048]{1,0:T(8,128)(2,1)} %bitcast.32, bf16[16,128]{1,0:T(8,128)(2,1)} %copy-done.8, s32[8,128]{1,0:T(8,128)} %broadcast_in_dim.4.lens, ...), custom_call_target="tpu_custom_call" | custom-call | tf_op jit(solution)/shard_map/project/pallas_call | solution.py:529
  49.4 1.5 fusion.5
  50.9 0.0 copy-done.3
  50.9 0.0 copy-start.4
  50.9 0.0 copy-start.5
  50.9 1.4 fusion.4
  52.3 0.3 copy-done.4
  52.6 0.6 copy-done.5
  53.3 0.3 pad_bitcast_fusion
  53.6 2.6 pad_maximum_fusion.w
  56.2 150.8 %middle.1 = (bf16[2048,128]{1,0:T(8,128)(2,1)}, f32[128,2048]{1,0:T(8,128)}, f32[128,2048]{1,0:T(8,128)}, f32[1,2048]{1,0:T(1,128)}, bf16[2048,384]{1,0:T(8,128)(2,1)}, /*index=5*/bf16[1056,2048]{1,0:T(8,128)(2,1)}) custom-call(bf16[3,2048,128]{2,1,0:T(8,128)(2,1)} %get-tuple-element.53.qkv, s32[8,128]{1,0:T(8,128)} %broadcast_in_dim.4.lens, ...), custom_call_target="tpu_custom_call" | custom-call | tf_op jit(solution)/shard_map/middle/pallas_call | solution.py:529
  207.0 0.0 copy-start
  207.0 0.0 copy-start.1
  207.0 97.5 %attention_back.1 = (bf16[2048,384]{1,0:T(8,128)(2,1)}, bf16[128,2048]{1,0:T(8,128)(2,1)}, bf16[128,2048]{1,0:T(8,128)(2,1)}, bf16[1056,2048]{1,0:T(8,128)(2,1)}) custom-call(f32[128,2048]{1,0:T(8,128)} %get-tuple-element.55.d_res, bf16[2048,128]{1,0:T(8,128)(2,1)} %get-tuple-element.56.attended, bf16[128,2048]{1,0:T(8,128)(2,1)} %w_out.3, ...), custom_call_target="tpu_custom_call" | custom-call | tf_op jit(solution)/shard_map/attention_back/pallas_call | solution.py:529
  304.5 0.0 copy-start.2
  304.5 0.0 copy-done
  304.5 0.2 copy.23
  304.7 0.0 copy-done.1
  304.7 0.2 copy.24
  304.9 0.6 copy-done.2
  305.5 0.2 copy.25
  305.7 1.2 pad_maximum_fusion.1.w
  307.0 73.6 %d_normed.1 = (f32[128,2048]{1,0:T(8,128)}, bf16[512,2048]{1,0:T(8,128)(2,1)}, f32[8,128]{1,0:T(8,128)}) custom-call(bf16[2048,384]{1,0:T(8,128)(2,1)} %get-tuple-element.63.d_qkv, bf16[384,2048]{1,0:T(8,128)(2,1)} %pad_maximum_fusion.1.w, bf16[16,128,2048]{2,1,0:T(8,128)(2,1)} %get-tuple-element.64.normed, bf16[128,2048]{1,0:T(8,128)(2,1)} %bitcast.34, ...), custom_call_target="tpu_custom_call" | custom-call | tf_op jit(solution)/shard_map/d_normed/pallas_call | solution.py:529
  380.6 3.0 slice_convert_fusion.1
  383.6 1.3 copy.26
  384.9 1.3 copy.27
  386.2 1.3 copy.28
  387.5 0.0 copy-start.7
  387.5 6.0 %slice_convert_fusion = (f32[344,2048]{1,0:T(8,128)}, f32[2048,344]{0,1:T(8,128)}, f32[2048,344]{0,1:T(8,128)}) fusion(bf16[1056,2048]{1,0:T(8,128)(2,1)} %get-tuple-element.69), kind=kLoop, calls=%fused_computation.6 | loop fusion | flops 2113536 | bytes 12681216 | tf_op jit(solution)/shard_map/convert_element_type | solution.py:1189
  393.5 0.0 copy-start.6
  393.6 1.3 slice_bitcast_fusion
  394.8 0.0 copy-done.7
  394.8 0.8 copy.32
  395.6 0.0 copy-done.6
  395.6 1.0 copy.33
  (1 shorter events, 0.0 us)
Async XLA Ops:
  0.6 50.3 %copy-start.3 = (bf16[344,2048]{1,0:T(8,128)(2,1)S(1)}, bf16[344,2048]{1,0:T(8,128)(2,1)}, u32[]{:S(2)}) copy-start(bf16[344,2048]{1,0:T(8,128)(2,1)} %param.24) | copy-start | bytes 4227076
  3.4 0.6 copy-start.8
  50.9 1.7 copy-start.4
  50.9 2.3 copy-start.5
  207.0 97.5 %copy-start = (bf16[2048,128]{1,0:T(8,128)(2,1)S(1)}, bf16[2048,128]{1,0:T(8,128)(2,1)}, u32[]{:S(2)}) copy-start(bf16[2048,128]{1,0:T(8,128)(2,1)} %w_query.1) | copy-start | bytes 1572868
  207.0 97.7 %copy-start.1 = (bf16[2048,128]{1,0:T(8,128)(2,1)S(1)}, bf16[2048,128]{1,0:T(8,128)(2,1)}, u32[]{:S(2)}) copy-start(bf16[2048,128]{1,0:T(8,128)(2,1)} %w_key.1) | copy-start | bytes 1572868
  304.5 1.0 copy-start.2
  387.5 7.3 %copy-start.7 = (bf16[128,2048]{1,0:T(8,128)(2,1)S(1)}, bf16[128,2048]{1,0:T(8,128)(2,1)}, u32[]{:S(2)}) copy-start(bf16[128,2048]{1,0:T(8,128)(2,1)} %get-tuple-element.62) | copy-start | bytes 1572868
  393.5 2.1 copy-start.6

commit v4 on v3

--- a/solution.py
+++ b/solution.py
@@ -2,6 +2,7 @@
 
 import jax
 import jax.numpy as jnp
+import numpy as np
 from jax import lax
 from jax.experimental import pallas as pl
 from jax.experimental.pallas import tpu as pltpu
@@ -152,11 +153,11 @@
     got("m1b")
     send("zb10", "z", 0, 1, 0, 32)
     send("c2", "c", 0, 1, 0, 128)
-    got("c1")
-    yield 0, 3
     got("zb00", "zb01")
     send("c4", "c", 1, 0, 0, 32)
     send("c5", "c", 1, 0, 96, 32)
+    got("c1")
+    yield 0, 3
     got("c2")
     yield 0, 1
     got("p2")
@@ -165,6 +166,7 @@
     got("m2")
     send("zb21", "z", 0, 2, 96, 32)
     send("c7", "c", 0, 2, 64, 64)
+    yield None
     got("c3", "c4", "c5")
     yield 1, 0
     got("p3")
@@ -173,6 +175,7 @@
     got("m3")
     send("m4", "m", 1, 1, 64, 32)
     send("c9", "c", 1, 1, 32, 64)
+    yield None
     got("c6", "c7")
     yield 0, 2
     got("zb30", "zb31")
@@ -181,20 +184,21 @@
     got("zb10", "zb11")
     send("c12", "c", 1, 1, 0, 32)
     send("c13", "c", 1, 1, 96, 32)
-    got("c8", "c10", "c11")
-    yield 1, 3
     got("p4")
     send("c14", "c", 1, 2, 32, 32)
     got("m4")
     send("c15", "c", 1, 2, 64, 32)
-    got("c9", "c12", "c13")
-    yield 1, 1
+    yield None
     got("zb20")
     send("c16", "c", 1, 2, 0, 32)
     got("zb21")
     send("c17", "c", 1, 2, 96, 32)
     got("c14", "c15", "c16", "c17")
     yield 1, 2
+    got("c9", "c12", "c13")
+    yield 1, 1
+    got("c8", "c10", "c11")
+    yield 1, 3
 
 
 def gather_round_steps(net, pos, buf, tag):
@@ -325,6 +329,7 @@
         self.put_zb(2)
         self.put("p4", "p", self.mine(1, 2, 64, 32))
         self.put("m4", "m", self.mine(1, 2, 32, 32))
+        yield
         self.joined(1, 1)
         self.put_zb(1)
         self.joined(1, 3)
@@ -334,29 +339,30 @@
         self.put("p3", "p", self.mine(1, 1, 32, 64))
         self.take("m4", 1, 3, 32, 32)
         self.put("m3", "m", self.mine(1, 3, 32, 64))
+        yield
         self.joined(0, 2)
-        yield
         self.take_zb(2)
         self.put("p2", "p", self.mine(0, 2, 64, 64))
         self.put("m2", "m", self.mine(0, 2, 0, 64))
+        yield
         self.joined(1, 0)
         self.joined(0, 1)
         self.joined(0, 3)
+        self.joined(0, 0)
         yield
         self.take("p3", 1, 0, 32, 64)
         self.take("m3", 1, 0, 32, 64)
         self.put("z0", "z", self.mine(1, 0, 32, 64))
+        self.put_zb(0)
         yield
         self.take("p2", 0, 1, 64, 64)
         self.put("p1a", "p", self.mine(0, 1, 32, 64))
         self.take("m2", 0, 3, 0, 64)
         self.put("m1a", "m", self.mine(0, 3, 32, 64))
-        self.joined(0, 0)
         yield
         self.take_zb(1)
         self.put("p1b", "p", self.mine(0, 1, 0, 32))
         self.put("p1c", "p", self.mine(0, 1, 96, 32))
-        self.put_zb(0)
         self.take_zb(3)
         self.put("m1b", "m", self.mine(0, 3, 0, 32))
         self.put("m1c", "m", self.mine(0, 3, 96, 32))
@@ -424,18 +430,15 @@
     columns(part.shape[2], tile)
 
 
-def span(pos, d, part, half=None):
-    start = ((pos[4] + d) % 4) * 512 + part * 256
+def quarter(pos, d, half=None):
+    start = ((pos[4] + d) % 4) * 256
     if half is None:
         return pl.ds(pl.multiple_of(start, 256), 256)
     return pl.ds(pl.multiple_of(start + half * 128, 128), 128)
 
 
-def ring_sum_scratch(rows):
-    return [
-        pltpu.VMEM((2, 2, rows, 128), BF),
-        pltpu.VMEM((2, 2, rows, 256), BF),
-    ]
+def part_columns(pos, d, p):
+    return pl.ds(pl.multiple_of(((pos[4] + d) % 4) * 512 + p * 256, 256), 256)
 
 
 def by_rows(rows, body):
@@ -446,6 +449,14 @@
     lax.fori_loop(0, rows // 32, step, 0)
 
 
+def ring_sum_scratch(rows):
+    return [pltpu.VMEM((2, rows, 128), BF), pltpu.VMEM((2, rows, 256), BF)]
+
+
+N_RING_SUM = 4
+N_RING_SHARE = 5
+
+
 class Ring:
     def __init__(self, net, pos, tag):
         self.net, self.pos, self.tag = net, pos, tag
@@ -456,59 +467,53 @@
     def got(self, *names):
         self.net.got(*[self.tag + name for name in names])
 
-    def far(self, p, terms, far):
-        self.put("e2%d" % p, "e", terms.at[:, span(self.pos, 2, p, 0)], far.at[p, 0])
-        self.put("w2%d" % p, "w", terms.at[:, span(self.pos, 2, p, 1)], far.at[p, 1])
-
-    def near(self, p, terms, far, near):
+    def far(self, terms, far):
+        self.put("e2", "e", terms.at[:, quarter(self.pos, 2, 0)], far.at[0])
+        self.put("w2", "w", terms.at[:, quarter(self.pos, 2, 1)], far.at[1])
+
+    def near(self, terms, far, near):
         for name, d, half in (("e", 1, 0), ("w", 3, 1)):
-            self.got("%s2%d" % (name, p))
-            cols = span(self.pos, d, p, half)
+            self.got(name + "2")
+            cols = quarter(self.pos, d, half)
 
             def fold(r, half=half, cols=cols):
-                total = terms[r, cols].astype(F32) + far[p, half, r, :].astype(F32)
+                total = terms[r, cols].astype(F32) + far[half, r, :].astype(F32)
                 terms[r, cols] = total.astype(BF)
 
             by_rows(terms.shape[0], fold)
-            src = terms.at[:, span(self.pos, d, p)]
-            self.put("%s1%d" % (name, p), name, src, near.at[p, half])
-
-    def join(self, p, terms, near, chunk):
-        self.got("e1%d" % p, "w1%d" % p)
+            self.put(name + "1", name, terms.at[:, quarter(self.pos, d)], near.at[half])
+
+    def join(self, terms, near, chunk):
+        self.got("e1", "w1")
 
         def add(r):
-            total = terms[r, span(self.pos, 0, p)].astype(F32) + near[p, 0, r, :].astype(F32)
-            chunk[p, r, :] = (total + near[p, 1, r, :].astype(F32)).astype(BF)
+            total = terms[r, quarter(self.pos, 0)].astype(F32) + near[0, r, :].astype(F32)
+            chunk[r, :] = (total + near[1, r, :].astype(F32)).astype(BF)
 
         by_rows(terms.shape[0], add)
 
-    def across(self, p, chunk, box):
-        self.put("h%d" % p, "h", chunk.at[p], box.at[p])
-
-    def crossed(self, p, chunk, box, whole):
-        self.got("h%d" % p)
-        cols = span(self.pos, 0, p)
+    def across(self, chunk, box):
+        self.put("h", "h", chunk, box)
+
+    def crossed(self, chunk, box, whole):
+        self.got("h")
+        cols = quarter(self.pos, 0)
 
         def add(r):
-            total = chunk[p, r, :].astype(F32) + box[p, r, :].astype(F32)
-            whole[r, cols] = total.astype(BF)
+            whole[r, cols] = (chunk[r, :].astype(F32) + box[r, :].astype(F32)).astype(BF)
 
         by_rows(whole.shape[0], add)
         for name in "ew":
-            self.put("%s3%d" % (name, p), name, whole.at[:, cols], whole.at[:, cols])
-
-    def share(self, p, whole):
+            self.put(name + "3", name, whole.at[:, cols], whole.at[:, cols])
+
+    def share(self, whole):
         for name, d, half in (("e", 3, 0), ("w", 1, 1)):
-            self.got("%s3%d" % (name, p))
-            ref = whole.at[:, span(self.pos, d, p, half)]
-            self.put("%s4%d" % (name, p), name, ref, ref)
-
-    def shared(self, p):
-        self.got("e4%d" % p, "w4%d" % p)
-
-
-N_RING_SUM = 8
-N_RING_SHARE = 10
+            self.got(name + "3")
+            ref = whole.at[:, quarter(self.pos, d, half)]
+            self.put(name + "4", name, ref, ref)
+
+    def shared(self):
+        self.got("e4", "w4")
 
 
 def run(*steps):
@@ -525,12 +530,15 @@
     return [pltpu.SemaphoreType.DMA((n,)), pltpu.SemaphoreType.DMA((n,))]
 
 
-def call(kernel, name, cid, outs, scratch, args, mib=60):
+HBM = pl.BlockSpec(memory_space=pl.ANY)
+
+
+def call(kernel, name, cid, outs, scratch, args, mib=60, in_hbm=(), out_hbm=()):
     return pl.pallas_call(
         kernel,
         out_shape=[jax.ShapeDtypeStruct(s, d) for s, d in outs],
-        in_specs=[VM] * len(args),
-        out_specs=[VM] * len(outs),
+        in_specs=[HBM if i in in_hbm else VM for i in range(len(args))],
+        out_specs=[HBM if i in out_hbm else VM for i in range(len(outs))],
         scratch_shapes=scratch,
         compiler_params=pltpu.CompilerParams(
             collective_id=cid, has_side_effects=True, vmem_limit_bytes=mib * 2**20
@@ -546,7 +554,7 @@
 def d_normed_kernel(
     d_qkv,
     w,
-    normed,
+    far_normed,
     acts,
     d_res,
     gain,
@@ -555,14 +563,17 @@
     acts_grad,
     whole,
     gains,
+    normed,
     part,
     sib,
     inbox,
     terms,
     chunk,
     box,
-    far,
-    near,
+    far0,
+    near0,
+    far1,
+    near1,
     low_t,
     gain_terms,
     gain_box,
@@ -570,23 +581,29 @@
     gain_wide,
     send,
     recv,
+    in_sem,
 ):
     pos = place()
     net = Copies(pos, send, recv)
     me = lax.axis_index("ctx")
+    fetch = pltpu.make_async_copy(far_normed, normed, in_sem)
+    fetch.start()
     greet([ctx_peer(d) for d in range(1, 16)] + [grp_peer(d) for d in range(1, 8)])
     sums = Scatter(net, pos, part, sib, inbox, "s", True)
     low_t[...] = d_qkv[...].T
-    terms[pl.ds(384, 128), :] = grad_out[...]
+    for q in range(4):
+        for p in range(2):
+            cols = slice(q * 512 + p * 256, q * 512 + p * 256 + 256)
+            terms[p, pl.ds(384, 128), q * 256 : (q + 1) * 256] = grad_out[:, cols]
     gain_terms[...] = jnp.zeros_like(gain_terms)
     for j in range(16):
         cols = slice(j * 128, (j + 1) * 128)
         gain_terms[j, 0:1, :] = gain_two_part[:, cols]
 
     def weight_grads(d, p):
-        cols = span(pos, d, p)
+        cols = part_columns(pos, d, p)
         g = dot(low_t[...], normed[:, :, cols].reshape(2048, 256))
-        terms[pl.ds(0, 384), cols] = g.astype(BF)
+        terms[p, pl.ds(0, 384), quarter(pos, d)] = g.astype(BF)
         by_column = jnp.sum(g * w[:, cols].astype(F32), 0, keepdims=True) / gain[:, cols]
         first = ((pos[4] + d) % 4) * 4 + p * 2
         gain_terms[first, 1:2, :] = by_column[:, :128]
@@ -597,43 +614,45 @@
             product(pos, part, dz, dy, (d_qkv, w))
             sums.swap(dz, dy)
 
-    ring = Ring(net, pos, "r")
     back = sums.z_last_steps()
+    rings = Ring(net, pos, "r"), Ring(net, pos, "q")
+    boxes = (far0, near0), (far1, near1)
+    products(SCATTER_ORDER[:2])
+    fetch.wait()
     weight_grads(2, 0)
-    ring.far(0, terms, far)
-    products(SCATTER_ORDER[:1])
+    rings[0].far(terms.at[0], far0)
+    products(SCATTER_ORDER[2:4])
     weight_grads(2, 1)
-    ring.far(1, terms, far)
-    products(SCATTER_ORDER[1:])
+    rings[1].far(terms.at[1], far1)
+    products(SCATTER_ORDER[4:])
     next(back)
     weight_grads(1, 0)
     weight_grads(3, 0)
-    ring.near(0, terms, far, near)
+    rings[0].near(terms.at[0], far0, near0)
     next(back)
     weight_grads(1, 1)
     weight_grads(3, 1)
-    ring.near(1, terms, far, near)
+    rings[1].near(terms.at[1], far1, near1)
     next(back)
     weight_grads(0, 0)
     weight_grads(0, 1)
     for d in range(1, 16):
         net.start("g%d" % d, ctx_peer(d), gain_terms.at[(me + d) % 16], gain_box.at[d])
     gain_box[0] = gain_terms[me]
-    ring.join(0, terms, near, chunk)
-    ring.across(0, chunk, box)
-    ring.join(1, terms, near, chunk)
-    ring.across(1, chunk, box)
-    next(back)
-    ring.crossed(0, chunk, box, whole)
+    for p in range(2):
+        rings[p].join(terms.at[p], boxes[p][1], chunk.at[p])
+        rings[p].across(chunk.at[p], box.at[p])
+    next(back)
+    rings[0].crossed(chunk.at[0], box.at[0], whole.at[0])
     net.got(*["g%d" % d for d in range(1, 16)])
     gain_sum[...] = jnp.sum(gain_box[...], 0)
     for d in range(1, 8):
         net.start("h%d" % d, grp_peer(d), gain_sum, gain_wide.at[d])
     gain_wide[0] = gain_sum[...]
-    ring.crossed(1, chunk, box, whole)
-    ring.share(0, whole)
+    rings[1].crossed(chunk.at[1], box.at[1], whole.at[1])
+    rings[0].share(whole.at[0])
     run(back)
-    ring.share(1, whole)
+    rings[1].share(whole.at[1])
     net.got(*["h%d" % d for d in range(1, 8)])
     gains[...] = jnp.sum(gain_wide[...], 0)
 
@@ -652,19 +671,22 @@
         return 0
 
     lax.fori_loop(0, 4, finish, 0)
-    ring.shared(0)
-    ring.shared(1)
+    rings[0].shared()
+    rings[1].shared()
     net.finish()
 
 
-def d_normed(d_qkv, w, normed, acts, d_res, gain, grad_out, gain_two_part, cid):
+def d_normed(*args):
     return call(
         d_normed_kernel,
         "d_normed",
-        cid,
-        [((128, 2048), F32), ((512, 2048), BF), ((8, 128), F32)],
-        scatter_scratch(2048)
-        + [pltpu.VMEM((512, 2048), BF), pltpu.VMEM((2, 512, 256), BF), pltpu.VMEM((2, 512, 256), BF)]
+        3,
+        [((128, 2048), F32), ((2, 512, 1024), BF), ((8, 128), F32)],
+        [pltpu.VMEM((16, 128, 2048), BF)]
+        + scatter_scratch(2048)
+        + [pltpu.VMEM((2, 512, 1024), BF)]
+        + [pltpu.VMEM((2, 512, 256), BF), pltpu.VMEM((2, 512, 256), BF)]
+        + ring_sum_scratch(512)
         + ring_sum_scratch(512)
         + [
             pltpu.VMEM((384, 2048), BF),
@@ -673,9 +695,40 @@
             pltpu.VMEM((8, 128), F32),
             pltpu.VMEM((8, 8, 128), F32),
         ]
-        + sems(N_SCATTER + N_RING_SUM + N_RING_SHARE + 22),
-        [d_qkv, w, normed, acts, d_res, gain, grad_out, gain_two_part],
+        + sems(N_SCATTER + 2 * N_RING_SUM + 2 * N_RING_SHARE + 22)
+        + [pltpu.SemaphoreType.DMA],
+        args,
+        in_hbm=(2,),
     )
+
+
+def widen_kernel(ff, attn, gate, up, down, query, key, value, out):
+    for i, ref in enumerate((gate, up, down)):
+        ref[...] = ff[0, i * FF_ROWS : i * FF_ROWS + ref.shape[0], :].astype(F32)
+    for i, ref in enumerate((query, key, value)):
+        ref[...] = attn[0, i * 128 : (i + 1) * 128, :].astype(F32).T
+    out[...] = attn[0, 384:512, :].astype(F32)
+
+
+def widen(ff_sums, attn_sums, ff):
+    by_part = lambda j: (j % 2, 0, j // 2)
+    column, row = lambda j: (0, j), lambda j: (j, 0)
+    return pl.pallas_call(
+        widen_kernel,
+        grid=(8,),
+        out_shape=[jax.ShapeDtypeStruct((ff, 2048), F32)] * 3
+        + [jax.ShapeDtypeStruct((2048, 128), F32)] * 3
+        + [jax.ShapeDtypeStruct((128, 2048), F32)],
+        in_specs=[
+            pl.BlockSpec((1, 3 * FF_ROWS, 256), by_part),
+            pl.BlockSpec((1, 512, 256), by_part),
+        ],
+        out_specs=[pl.BlockSpec((ff, 256), column)] * 3
+        + [pl.BlockSpec((256, 128), row)] * 3
+        + [pl.BlockSpec((128, 256), column)],
+        compiler_params=pltpu.CompilerParams(vmem_limit_bytes=40 * 2**20),
+        name="widen",
+    )(ff_sums, attn_sums)
 
 
 def rope(u, cosine, sine):
@@ -692,34 +745,45 @@
 
 
 def bias_at(position, lens):
-    own = jnp.where(position >= lens[0:1, 0:1], lens[1:2, 0:1], lens[0:1, 0:1])
+    own = jnp.where(position >= lens[0:1, 0:1], lens[0:1, 1:2], lens[0:1, 0:1])
     return -jnp.log(own.astype(F32))
 
 
 def project_kernel(
     x,
-    gains,
+    gain_attn,
+    gain_mlp,
     lens,
     frequency,
     w_query,
     w_key,
     w_value,
+    w_gate_t,
+    w_up_t,
+    w_down,
     normed,
     qkv,
     cosines,
     sines,
     gain_rows,
+    w_t,
+    ff_in,
+    ff_out,
     buf,
+    normal,
     gain_box,
     w,
     send,
     recv,
+    out_sem,
 ):
     pos = place()
     net = Copies(pos, send, recv)
     me = lax.axis_index("ctx")
     buf[me] = x[...]
-    gain_box[me] = gains[...]
+    gain_box[me] = jnp.zeros((8, 128), F32)
+    gain_box[me, 0:1, :] = gain_attn[...].astype(F32)
+    gain_box[me, 1:2, :] = gain_mlp[...].astype(F32)
     greet([ctx_peer(d) for d in range(1, 16)])
     for d in range(1, 16):
         ref = gain_box.at[me]
@@ -743,19 +807,26 @@
     net.got(*["g%d" % d for d in range(1, 16)])
     gain_rows[...] = jnp.zeros_like(gain_rows)
     for j in range(16):
-        gain_rows[0:2, j * 128 : (j + 1) * 128] = gain_box[j].astype(F32)[0:2]
-
+        gain_rows[:, j * 128 : (j + 1) * 128] = gain_box[j]
+
+    leaving = []
+    done = 0
     while True:
         slot, _ = pair_rows(pos, dz, dy)
 
         def normalise(i, _, slot=slot):
             r = pl.ds(pl.multiple_of((i % 2) * 64, 64), 64)
             u = buf[slot + i // 2, r, :].astype(F32)
-            normed[slot + i // 2, r, :] = (u * norm_factor(u) * gain_rows[0:1, :]).astype(BF)
+            normal[slot + i // 2, r, :] = (u * norm_factor(u) * gain_rows[0:1, :]).astype(BF)
             return 0
 
         lax.fori_loop(0, 4, normalise, 0)
-        out = dot(normed[pl.ds(slot, 2)].reshape(256, 2048), w[...])
+        copy = pltpu.make_async_copy(
+            normal.at[pl.ds(slot, 2)], normed.at[pl.ds(slot, 2)], out_sem.at[done]
+        )
+        copy.start()
+        leaving.append(copy)
+        out = dot(normal[pl.ds(slot, 2)].reshape(256, 2048), w[...])
         for b in range(2):
             for half in range(2):
                 at = pl.ds(pl.multiple_of(block_start(slot + b, half), 64), 64)
@@ -764,34 +835,56 @@
                 qkv[0, at, :] = rope(out[rows, :128], c, s).astype(BF)
                 qkv[1, at, :] = rope(out[rows, 128:256], c, s).astype(BF)
                 qkv[2, at, :] = out[rows, 256:].astype(BF)
-        arrived = next(arrivals, ())
-        if arrived is None:
+        done += 1
+        if done == 1:
+            w_t[...] = w[...].T
+            for i, ref in enumerate((w_gate_t, w_up_t)):
+                pad_rows(ff_in.at[i], ref)
+            pad_rows(ff_out, w_down)
+        if done == 8:
+            break
+        arrived = next(arrivals)
+        while arrived is None:
             arrived = next(arrivals)
-        if not arrived:
-            break
         dz, dy = arrived
+    for _ in arrivals:
+        pass
+    for copy in leaving:
+        copy.wait()
     net.finish()
 
 
-def project(x, gains, lens, frequency, w_query, w_key, w_value, cid):
+def pad_rows(dst, src):
+    rows = src.shape[0]
+    dst[pl.ds(0, rows), :] = src[...]
+    dst[pl.ds(rows, FF_PAD - rows), :] = jnp.zeros((FF_PAD - rows, dst.shape[1]), BF)
+
+
+def project(*args):
     return call(
         project_kernel,
         "project",
-        cid,
+        0,
         [
             ((16, 128, 2048), BF),
             ((3, 2048, 128), BF),
             ((2048, 128), F32),
             ((2048, 128), F32),
             ((8, 2048), F32),
+            ((384, 2048), BF),
+            ((2, FF_PAD, 2048), BF),
+            ((FF_PAD, 2048), BF),
         ],
         [
             pltpu.VMEM((16, 128, 2048), BF),
-            pltpu.VMEM((16, 16, 128), BF),
+            pltpu.VMEM((16, 128, 2048), BF),
+            pltpu.VMEM((16, 8, 128), F32),
             pltpu.VMEM((2048, 384), BF),
         ]
-        + sems(N_GATHER + 15),
-        [x, gains, lens, frequency, w_query, w_key, w_value],
+        + sems(N_GATHER + 15)
+        + [pltpu.SemaphoreType.DMA((8,))],
+        args,
+        out_hbm=(0,),
     )
 
 
@@ -827,19 +920,24 @@
     cot,
     acts,
     gain,
-    w,
+    ff_in,
+    ff_out,
     attended,
     residual,
     d_res,
     gain_part,
     hidden,
-    grads,
+    chunk,
+    later,
     cot_all,
     buf,
     low_t,
     part,
     sib,
     inbox,
+    terms,
+    far,
+    near,
     send,
     recv,
 ):
@@ -847,7 +945,7 @@
     net = Copies(pos, send, recv)
     me = lax.axis_index("ctx")
     cot_all[me] = cot[...]
-    greet([neighbour(pos, l) for l in "pmzc"])
+    greet([neighbour(pos, l) for l in "pmzcew"])
     cots = gather_steps(net, pos, cot_all, "c")
     next(cots)
     for i in range(8):
@@ -855,7 +953,7 @@
         for b in range(4):
             at = packed_start(4 * i + b)
             attended[at : at + 64, :] = out[64 * b : 64 * (b + 1)]
-        if i == 6:
+        if i in (6, 7):
             next(cots)
     sums = Scatter(net, pos, part, sib, inbox, "a")
     for dz, dy in SCATTER_ORDER:
@@ -878,6 +976,7 @@
     lax.fori_loop(0, 4, normalise, 0)
     net.finish()
     sums = Scatter(net, pos, part, sib, inbox, "s")
+    back = sums.steps()
     for arrived in gather_steps(net, pos, buf, "x"):
         if arrived is None:
             continue
@@ -885,9 +984,9 @@
         slot, rows = pair_rows(pos, dz, dy)
         n2 = buf[pl.ds(slot, 2)].reshape(256, 2048)
         ct = cot_all[pl.ds(slot, 2)].reshape(256, 2048)
-        gate = dot_t(n2, w[0])
-        up = dot_t(n2, w[1])
-        d_hidden = dot_t(ct, w[2])
+        gate = dot_t(n2, ff_in[0])
+        up = dot_t(n2, ff_in[1])
+        d_hidden = dot_t(ct, ff_out[...])
         sig = jax.nn.sigmoid(gate)
         silu = gate * sig
         h = (silu * up).astype(BF)
@@ -899,31 +998,42 @@
         low_t[2, :, rows] = h.T
 
         def tile(cols):
-            t = dot(dg, w[0, :, cols]) + dot(du, w[1, :, cols])
+            t = dot(dg, ff_in[0, :, cols]) + dot(du, ff_in[1, :, cols])
             part[slot, :, cols] = t[:128].astype(BF)
             part[slot + 1, :, cols] = t[128:].astype(BF)
 
         columns(2048, tile)
         sums.swap(dz, dy)
 
-    def weight_grads():
+        if (dz, dy) == (1, 1):
+            next(back)
+
+    def weight_grads(d, p, dst):
+        cols, to = part_columns(pos, d, p), quarter(pos, d)
         for i, other in ((0, buf), (1, buf), (2, cot_all)):
-
-            def tile(cols, i=i, other=other):
-                rhs = other[:, :, cols].reshape(2048, 256)
-                g = dot(low_t[i], rhs)
-                grads[i * FF_ROWS : (i + 1) * FF_ROWS, cols] = g[:FF_ROWS].astype(BF)
-
-            for half in range(2):
-
-                def part_tile(j, _, half=half, tile=tile):
-                    tile(pl.ds(pl.multiple_of(half * 1024 + j * 256, 256), 256))
-                    return 0
-
-                lax.fori_loop(0, 4, part_tile, 0)
-                yield
-
-    run(sums.steps(), weight_grads())
+            g = dot(low_t[i], other[:, :, cols].reshape(2048, 256))
+            dst[pl.ds(i * FF_ROWS, FF_ROWS), to] = g[:FF_ROWS].astype(BF)
+
+    ring = Ring(net, pos, "r")
+    next(back)
+    next(back)
+    weight_grads(2, 0, terms)
+    ring.far(terms, far)
+    next(back)
+    weight_grads(1, 0, terms)
+    weight_grads(3, 0, terms)
+    next(back)
+    ring.near(terms, far, near)
+    next(back)
+    weight_grads(0, 0, terms)
+    weight_grads(0, 1, later)
+    next(back)
+    weight_grads(1, 1, later)
+    weight_grads(2, 1, later)
+    next(back)
+    weight_grads(3, 1, later)
+    run(back)
+    ring.join(terms, near, chunk)
 
     gain_part[...] = jnp.zeros_like(gain_part)
 
@@ -958,12 +1068,15 @@
             ((128, 2048), F32),
             ((1, 2048), F32),
             ((2048, FF_PAD), BF),
-            ((3 * FF_ROWS, 2048), BF),
+            ((3 * FF_ROWS, 256), BF),
+            ((3 * FF_ROWS, 1024), BF),
         ],
         [pltpu.VMEM((16, 128, 2048), BF), pltpu.VMEM((16, 128, 2048), BF)]
         + [pltpu.VMEM((3, FF_PAD, 2048), BF)]
         + scatter_scratch(2048)
-        + sems(2 * N_SCATTER + 2 * N_GATHER),
+        + [pltpu.VMEM((3 * FF_ROWS, 1024), BF)]
+        + ring_sum_scratch(3 * FF_ROWS)
+        + sems(2 * N_SCATTER + 2 * N_GATHER + N_RING_SUM),
         args,
         62,
     )
@@ -973,7 +1086,8 @@
     d_res,
     attended,
     w_out,
-    ff,
+    chunk0,
+    terms,
     qkv,
     lens,
     cosines,
@@ -991,7 +1105,7 @@
     inbox,
     far,
     near,
-    chunk,
+    chunk1,
     box,
     total,
     do,
@@ -1005,14 +1119,11 @@
     greet([neighbour(pos, l) for l in "pmzcewh"])
     sums = Scatter(net, pos, part, sib, inbox, "s", True)
     back = sums.z_last_steps()
-    ring = Ring(net, pos, "r")
-    arrivals = gather_steps(net, pos, buf, "x")
+    rings = Ring(net, pos, "r"), Ring(net, pos, "q")
+    arrivals = gather_round_steps(net, pos, buf, "x")
 
     def arrive():
-        pair = next(arrivals)
-        if pair is None:
-            pair = next(arrivals)
-        slot, rows = pair_rows(pos, *pair)
+        slot, rows = pair_rows(pos, *next(arrivals))
         d = buf[pl.ds(slot, 2)].reshape(256, 2048)
         g = dot_t(d, w_out[...]).astype(BF)
         for b in range(2):
@@ -1058,41 +1169,39 @@
         put(j, unrotate(dk, j), 1)
         put(j, dv.astype(BF), 2)
 
-    ring.far(0, ff, far)
-    ring.far(1, ff, far)
+    rings[1].far(terms, far)
     total[...] = jnp.zeros_like(total)
     dq[...] = jnp.zeros_like(dq)
     arrive()
+    rings[0].across(chunk0, box.at[0])
     products(SCATTER_ORDER)
-    ring.near(0, ff, far, near)
-    arrive()
-    ring.near(1, ff, far, near)
+    rings[1].near(terms, far, near)
     arrive()
     arrive()
     arrive()
     arrive()
     next(back)
+    rings[0].crossed(chunk0, box.at[0], whole.at[0])
     arrive()
-    ring.join(0, ff, near, chunk)
-    ring.across(0, chunk, box)
+    rings[1].join(terms, near, chunk1)
+    rings[1].across(chunk1, box.at[1])
+    arrive()
     arrive()
     grad_out[...] = total[...].astype(BF)
     keys(0)
     next(back)
-    ring.join(1, ff, near, chunk)
-    ring.across(1, chunk, box)
+    rings[0].share(whole.at[0])
     keys(1)
     keys(2)
     next(back)
-    ring.crossed(0, chunk, box, whole)
+    rings[1].crossed(chunk1, box.at[1], whole.at[1])
     keys(3)
     keys(4)
-    next(back)
     keys(5)
+    next(back)
     keys(6)
-    ring.crossed(1, chunk, box, whole)
-    ring.share(0, whole)
     keys(7)
+    rings[1].share(whole.at[1])
     for i in range(8):
         put(i, unrotate(dq[256 * i : 256 * (i + 1), :], i), 0)
     run(back)
@@ -1101,9 +1210,8 @@
         mixed[:, cols] = (residual[:, cols] + sums.total(cols)).astype(BF)
 
     columns(2048, last)
-    ring.share(1, whole)
-    ring.shared(0)
-    ring.shared(1)
+    rings[0].shared()
+    rings[1].shared()
     net.finish()
 
 
@@ -1111,23 +1219,23 @@
     return call(
         attention_back_kernel,
         "attention_back",
-        3,
+        2,
         [
             ((2048, 384), BF),
             ((128, 2048), BF),
             ((128, 2048), BF),
-            ((3 * FF_ROWS, 2048), BF),
+            ((2, 3 * FF_ROWS, 1024), BF),
         ],
         [pltpu.VMEM((16, 128, 2048), BF)]
         + scatter_scratch(2048)
         + ring_sum_scratch(3 * FF_ROWS)
-        + [pltpu.VMEM((2, 3 * FF_ROWS, 256), BF), pltpu.VMEM((2, 3 * FF_ROWS, 256), BF)]
+        + [pltpu.VMEM((3 * FF_ROWS, 256), BF), pltpu.VMEM((2, 3 * FF_ROWS, 256), BF)]
         + [
             pltpu.VMEM((128, 2048), F32),
             pltpu.VMEM((2048, 128), BF),
             pltpu.VMEM((2048, 128), F32),
         ]
-        + sems(N_GATHER + N_SCATTER + N_RING_SUM + N_RING_SHARE),
+        + sems(N_GATHER + N_SCATTER + N_RING_SUM + 2 * N_RING_SHARE),
         args,
     )
 
@@ -1153,54 +1261,53 @@
 
     acts_rows = acts.reshape(tok, width)
     cot_low = cotangent.reshape(tok, width)
-    gains = jnp.zeros((16, head), BF).at[0].set(gain_attn).at[1].set(gain_mlp)
-    lens = jnp.broadcast_to(
-        jnp.concatenate([doc_lengths.reshape(2), jnp.zeros((6,), jnp.int32)])[:, None], (8, head)
+    lane = np.arange(head) % (head // 2)
+    frequency = 10000.0 ** (-(lane.astype(np.float64) * 2.0 / head))
+    frequency = jnp.asarray(np.broadcast_to(frequency.astype(np.float32), (8, head)))
+    normed, qkv, cosines, sines, gain_rows, w_t, ff_in, ff_out = project(
+        acts_rows,
+        gain_attn.reshape(1, head),
+        gain_mlp.reshape(1, head),
+        doc_lengths,
+        frequency,
+        w_query,
+        w_key,
+        w_value,
+        w_gate.T,
+        w_up.T,
+        w_down,
     )
-    lane = jnp.arange(head) % (head // 2)
-    frequency = 10000.0 ** (-(lane.astype(F32) * 2.0 / head))
-    frequency = jnp.broadcast_to(frequency, (8, head))
-    normed, qkv, cosines, sines, gain_rows = project(
-        acts_rows, gains, lens, frequency, w_query, w_key, w_value, 0
-    )
-    def padded(w):
-        return jnp.pad(w, ((0, FF_PAD - ff), (0, 0)))
-
-    ff_w = jnp.stack([padded(w_gate.T), padded(w_up.T), padded(w_down)])
-    attended, residual, d_res, gain_two_part, hidden, ff_grads = middle(
-        qkv, lens, w_out, cot_low, acts_rows, gain_rows[1:2], ff_w
+    attended, residual, d_res, gain_two_part, hidden, chunk, later = middle(
+        qkv, doc_lengths, w_out, cot_low, acts_rows, gain_rows[1:2], ff_in, ff_out
     )
     d_qkv, grad_out, mixed, ff_sums = attention_back(
-        d_res, attended, w_out, ff_grads, qkv, lens, cosines, sines, hidden, ff_w[2], residual
+        d_res,
+        attended,
+        w_out,
+        chunk,
+        later,
+        qkv,
+        doc_lengths,
+        cosines,
+        sines,
+        hidden,
+        ff_out,
+        residual,
     )
     acts_grad, attn_sums, gain_grads = d_normed(
-        d_qkv,
-        jnp.concatenate([w_query.T, w_key.T, w_value.T]),
-        normed,
-        acts_rows,
-        d_res,
-        gain_rows[0:1],
-        grad_out,
-        gain_two_part,
-        5,
+        d_qkv, w_t, normed, acts_rows, d_res, gain_rows[0:1], grad_out, gain_two_part
     )
-
-    def ff_grad(i):
-        return ff_sums[i * FF_ROWS : i * FF_ROWS + ff].astype(F32)
-
-    def attn_grad(i):
-        return attn_sums[i * head : (i + 1) * head].astype(F32)
-
+    gate, up, down, query, key, value, out = widen(ff_sums, attn_sums, ff)
     return (
         mixed.reshape(1, 1, tok, width),
         acts_grad.reshape(1, 1, tok, width),
-        attn_grad(0).T,
-        attn_grad(1).T,
-        attn_grad(2).T,
-        attn_grad(3),
-        ff_grad(0).T,
-        ff_grad(1).T,
-        ff_grad(2),
+        query,
+        key,
+        value,
+        out,
+        gate.T,
+        up.T,
+        down,
         gain_grads[1],
         gain_grads[0],
     )

time: 405 us -> 377 us (0.931)
  other arithmetic: 12.9 us -> 0 us
  Pallas kernels: 367 us -> 359 us
  local copies, waits for them, and re-layouts: 15.7 us -> 9.63 us
    pallas_call x4, Pallas kernels: 367 us -> 353 us  [call(): pl.pallas_call(kernel, out_shape=[jax.ShapeDtypeStruct(s, d) for s, d in...]
    convert_element_type x2 -> x0, other arithmetic: 9.02 us -> none  [the longest x1 6.01 us: ff_grad(): return ff_sums[i * FF_ROWS:i * FF_ROWS + ff].astype(F32)]
    pallas_call x0 -> x1, Pallas kernels: none -> 5.86 us  [widen(): pl.pallas_call(widen_kernel, grid=(8,), out_shape=[jax.ShapeDtypeStruct((...]
where the time goes in v4:
time: 377 us; the launch traced here: 370 us
  Pallas kernels  359 us (95%)
  local copies, waits for them, and re-layouts  9.63 us (3%)
    pallas_call x4, Pallas kernels, call(): pl.pallas_call(kernel, out_shape=[jax.ShapeDtypeStruct(s, d) for s, d in...  353 us

profile of v4, /device:TPU:0, one launch (start us, length us, event | category | flops | bytes accessed | tf_op | source)
XLA Modules:
  0.0 369.9 jit_solution(3170998898939783385)
XLA Ops:
  0.6 1.3 jit_solution_.3.frequency
  1.9 48.6 %project.1 = (bf16[16,128,2048]{2,1,0:T(8,128)(2,1)}, bf16[3,2048,128]{2,1,0:T(8,128)(2,1)}, f32[2048,128]{1,0:T(8,128)}, f32[2048,128]{1,0:T(8,128)}, f32[8,204...) custom-call(bf16[128,2048]{1,0:T(8,128)(2,1)} %bitcast.14, ...), custom_call_target="tpu_custom_call" | custom-call | tf_op jit(solution)/shard_map/project/pallas_call | solution.py:537
  50.5 1.5 fusion
  52.0 146.3 %middle.1 = (bf16[2048,128]{1,0:T(8,128)(2,1)}, f32[128,2048]{1,0:T(8,128)}, f32[128,2048]{1,0:T(8,128)}, f32[1,2048]{1,0:T(1,128)}, bf16[2048,384]{1,0:T(8,128)...) custom-call(bf16[3,2048,128]{2,1,0:T(8,128)(2,1)} %get-tuple-element.40.qkv, s32[1,2]{1,0:T(1,128)} %lens.5, ...), custom_call_target="tpu_custom_call" | custom-call | tf_op jit(solution)/shard_map/middle/pallas_call | solution.py:537
  198.3 87.0 %attention_back.1 = (bf16[2048,384]{1,0:T(8,128)(2,1)}, bf16[128,2048]{1,0:T(8,128)(2,1)}, bf16[128,2048]{1,0:T(8,128)(2,1)}, bf16[2,1056,1024]{2,1,0:T(8,128)(2,1)}) custom-call(f32[128,2048]{1,0:T(8,128)} %get-tuple-element.44.d_res, bf16[2048,128]{1,0:T(8,128)(2,1)} %get-tuple-element.45.attended, bf16[128,2048]{1,0:T(8,128)(2,1)} %w_out.3, ...), custom_call_target="tpu_custom_call" | custom-call | tf_op jit(solution)/shard_map/attention_back/pallas_call | solution.py:537
  285.4 71.4 %d_normed.1 = (f32[128,2048]{1,0:T(8,128)}, bf16[2,512,1024]{2,1,0:T(8,128)(2,1)}, f32[8,128]{1,0:T(8,128)}) custom-call(bf16[2048,384]{1,0:T(8,128)(2,1)} %get-tuple-element.53.d_qkv, bf16[384,2048]{1,0:T(8,128)(2,1)} %get-tuple-element.54.w, bf16[16,128,2048]{2,1,0:T(8,128)(2,1)} %get-tuple-element.55.far_normed, bf16[128,2048]{1,0:T(8,128)(2,1)} %bitcast.16, ...), custom_call_target="tpu_custom_call" | custom-call | tf_op jit(solution)/shard_map/d_normed/pallas_call | solution.py:537
  356.8 1.3 slice_bitcast_fusion
  358.0 0.0 copy-start
  358.0 2.2 copy-done
  360.3 0.0 copy-start.1
  360.3 1.6 copy-done.1
  361.9 0.0 copy-start.3
  361.9 0.0 copy-start.2
  361.9 5.9 %widen.1 = (f32[344,2048]{1,0:T(8,128)}, f32[344,2048]{1,0:T(8,128)}, f32[344,2048]{1,0:T(8,128)}, f32[2048,128]{1,0:T(8,128)}, f32[2048,128]{1,0:T(8,128)}, /*index=5*/f32[2048,128]{1,0:T(8,128)}, f32[128,2048]{1,0:T(8,128)}) custom-call(bf16[2,1056,1024]{2,1,0:T(8,128)(2,1)S(1)} %copy-done, bf16[2,512,1024]{2,1,0:T(8,128)(2,1)S(1)} %copy-done.1), custom_call_target="tpu_custom_call" | custom-call | tf_op jit(solution)/shard_map/widen/pallas_call | solution.py:716
  367.7 0.0 copy-done.3
  367.7 0.8 copy.26
  368.5 0.0 copy-done.2
  368.5 1.0 copy.27
Async XLA Ops:
  358.0 2.2 copy-start
  360.3 1.6 copy-start.1
  361.9 5.9 %copy-start.3 = (bf16[128,2048]{1,0:T(8,128)(2,1)S(1)}, bf16[128,2048]{1,0:T(8,128)(2,1)}, u32[]{:S(2)}) copy-start(bf16[128,2048]{1,0:T(8,128)(2,1)} %get-tuple-element.52) | copy-start | bytes 1572868
  361.9 6.7 %copy-start.2 = (f32[128,2048]{1,0:T(8,128)S(1)}, f32[128,2048]{1,0:T(8,128)}, u32[]{:S(2)}) copy-start(f32[128,2048]{1,0:T(8,128)} %get-tuple-element.58) | copy-start | bytes 3145732
